TPU v7x, 32 devices: a whole 2x2x4 slice. The times are simulated.
32 devices in a mesh: sec: 4 (over y, core), op: 8 (over z, x).
Axes of the slice: x: 2, y: 2, z: 4, core: 2. Of those that a mesh axis runs over, the one named last changes fastest.
Arguments:
- wavefunction: bfloat16 [4, 2, 384, 384], P('sec', None, 'op'), may hold values from -6 to 6
- diagonal: float32 [4, 384, 384], P('sec', 'op'), may hold values from 0.5 to 2
- left_ops: bfloat16 [128, 384, 384], P(('sec', 'op')), may hold values from -0.0390625 to 0.0390625
- right_ops: bfloat16 [128, 384, 384], P(('sec', 'op')), may hold values from -0.3125 to 0.3125
- offsets: int32 [128, 2], P(('sec', 'op')), may hold values from 0 to 1
Outputs:
- preconditioned: bfloat16 [4, 2, 384, 384], P('sec', None, 'op')
All inputs are finite; a program needn't handle non-finite values.
Results may differ from a plain program's by a relative error of at most 0.025.
Values may be sent and summed in bfloat16 or wider, within the bound.
No kernel may reach another device: no remote copies, remote signals or barrier semaphores. Data moves between devices by JAX's collectives and lax.ppermute only.
A program may use at most 64 MiB of HBM per device.

v0:
```python
import jax
import jax.numpy as jnp
from jax import lax
from jax.sharding import PartitionSpec as P

ITERS = 2


def from_behind(block, axis, distance):
    devices = range(lax.axis_size(axis))
    route = [(i - distance, i) for i in devices if i - distance in devices]
    return lax.ppermute(block, axis, route)


def on_device(wavefunction, diagonal, left_ops, right_ops, offsets):
    nothing = jnp.zeros((), jnp.bfloat16)
    raise_mask = (offsets[:, 0] == 1)[:, None, None]
    lower_mask = (offsets[:, 1] == 1)[:, None, None]
    left_raise = jnp.where(raise_mask, left_ops, nothing)
    left_stay = jnp.where(raise_mask, nothing, left_ops)
    left_lower = jnp.where(lower_mask, left_ops, nothing)
    left_back = jnp.where(lower_mask, nothing, left_ops)
    members = lax.axis_size("op")
    trial_vec = wavefunction
    for turn in range(ITERS):
        rows_block = lax.all_gather(trial_vec, "op", axis=2, tiled=True)[0]
        turned = jnp.einsum(
            "xab,pcb->pxac", rows_block, right_ops, preferred_element_type=jnp.float32
        ).astype(jnp.bfloat16)
        plain_rows = jnp.einsum(
            "xab,pbc->pxac", rows_block, right_ops, preferred_element_type=jnp.float32
        ).astype(jnp.bfloat16)
        halves = jnp.stack([turned, plain_rows])
        apply_turned = halves[0]
        apply_plain_rows = halves[1]
        raised = jnp.einsum(
            "pab,pxbc->xac", left_raise, apply_turned, preferred_element_type=jnp.float32
        ).astype(jnp.bfloat16)
        staying = jnp.einsum(
            "pab,pxbc->xac", left_stay, apply_turned, preferred_element_type=jnp.float32
        )
        staying = (
            staying
            + jnp.einsum(
                "pba,pxbc->xac", left_back, apply_plain_rows, preferred_element_type=jnp.float32
            )
        ).astype(jnp.bfloat16)
        lowered = jnp.einsum(
            "pba,pxbc->xac", left_lower, apply_plain_rows, preferred_element_type=jnp.float32
        ).astype(jnp.bfloat16)
        stacked = jnp.stack([staying, raised, lowered])
        width = stacked.shape[3]
        shaped = stacked.reshape(3, stacked.shape[1], members, width // members, width)
        received = lax.all_to_all(shaped, "op", split_axis=2, concat_axis=2, tiled=True)
        summed = jnp.sum(received.astype(jnp.float32), axis=2)
        owned = summed[0]
        below_sum = from_behind(summed[1].astype(jnp.bfloat16), "sec", 1).astype(jnp.float32)
        above_sum = from_behind(summed[2].astype(jnp.bfloat16), "sec", -1).astype(jnp.float32)
        sigma_rows = owned + below_sum + above_sum
        trial_vec = (sigma_rows / diagonal[0][None]).astype(jnp.bfloat16)[None]
    return trial_vec


def solution(mesh):
    in_specs = (
        P("sec", None, "op", None),
        P("sec", "op", None),
        P(("sec", "op"), None, None),
        P(("sec", "op"), None, None),
        P(("sec", "op"), None),
    )
    out_specs = P("sec", None, "op", None)
    return jax.shard_map(
        on_device, mesh=mesh, in_specs=in_specs, out_specs=out_specs, check_vma=False
    )
```

profile of v0, /device:TPU:0, one launch (start us, length us, event | category | flops | bytes accessed | tf_op | source)
XLA Modules:
  0.0 176.4 jit_solution(10685222998068650754)
XLA Ops:
  0.0 33.5 %all_gather.6 = bf16[1,2,384,384]{3,2,1,0:T(8,128)(2,1)S(1)} all-gather(bf16[1,2,48,384]{3,2,1,0:T(8,128)(2,1)} %param.5), channel_id=1, replica_groups=mesh['sec'=4,'op'=8] {'op'}, dimensions={2}, use_global_device_ids=true | all-gather | bytes 663552 | tf_op jit(solution)/shard_map/all_gather | solution.py:26
  33.5 1.4 convolution_convert_fusion.3
  35.0 0.0 copy-start.2
  35.0 0.0 copy-start.3
  35.0 1.4 convolution_convert_fusion.2
  36.5 1.1 fusion.16
  37.6 1.1 fusion.55
  38.8 1.2 fusion.52
  40.0 1.3 fusion.58
  41.3 0.2 pad_maximum_fusion
  41.5 0.2 copy.53
  41.7 40.8 %all_to_all.10 = bf16[3,2,8,48,384]{4,3,1,0,2:T(8,128)(2,1)S(1)} all-to-all(bf16[3,2,8,48,384]{4,3,1,0,2:T(8,128)(2,1)S(1)} %copy.53), channel_id=1, replica_groups=mesh['sec'=4,'op'=8] {'op'}, dimensions={2} | all-to-all | bytes 3538944 | tf_op jit(solution)/shard_map/all_to_all | solution.py:54
  82.5 0.2 convert_reduce_fusion.1
  82.8 1.3 collective-permute-start
  84.1 1.3 collective-permute-start.1
  85.4 0.0 collective-permute-done
  85.4 3.6 %collective-permute-done.1 = bf16[2,48,384]{2,1,0:T(8,128)(2,1)S(1)} collective-permute-done((bf16[2,48,384]{2,1,0:T(8,128)(2,1)S(1)}, bf16[2,48,384]{2,1,0:T(8,128)(2,1)S(1)}, u32[]{:S(2)}, u32[]{:S(2)}) %collective-permute-start.1) | collective-permute-done | bytes 73760 | tf_op jit(solution)/shard_map/ppermute | solution.py:12
  89.1 31.9 %all-gather = bf16[2,384,384]{2,1,0:T(8,128)(2,1)S(1)} all-gather(bf16[2,48,384]{2,1,0:T(8,128)(2,1)S(1)} %fusion.86), channel_id=2, replica_groups=mesh['sec'=4,'op'=8] {'op'}, dimensions={1}, use_global_device_ids=true | all-gather | bytes 663552 | tf_op jit(solution)/shard_map/all_gather | solution.py:26
  121.0 1.4 convolution_convert_fusion.1
  122.4 1.4 convolution_convert_fusion
  123.8 1.1 fusion.31
  124.9 1.1 fusion.49
  126.1 1.2 fusion.46
  127.3 1.2 fusion.61
  128.6 0.2 pad_maximum_fusion.1
  128.8 0.2 copy.56
  129.0 42.0 %all_to_all.11 = bf16[3,2,8,48,384]{4,3,1,0,2:T(8,128)(2,1)S(1)} all-to-all(bf16[3,2,8,48,384]{4,3,1,0,2:T(8,128)(2,1)S(1)} %copy.56), channel_id=1, replica_groups=mesh['sec'=4,'op'=8] {'op'}, dimensions={2} | all-to-all | bytes 3538944 | tf_op jit(solution)/shard_map/all_to_all | solution.py:54
  171.0 0.2 convert_reduce_fusion
  171.3 1.3 collective-permute-start.2
  172.6 1.3 collective-permute-start.3
  173.9 1.8 %collective-permute-done.3 = bf16[2,48,384]{2,1,0:T(8,128)(2,1)S(1)} collective-permute-done((bf16[2,48,384]{2,1,0:T(8,128)(2,1)S(1)}, bf16[2,48,384]{2,1,0:T(8,128)(2,1)S(1)}, u32[]{:S(2)}, u32[]{:S(2)}) %collective-permute-start.3) | collective-permute-done | bytes 73760 | tf_op jit(solution)/shard_map/ppermute | solution.py:12
  175.8 0.7 fusion.88
  (13 shorter events, 0.2 us)
Async XLA Ops:
  0.0 33.5 %copy-start = (bf16[4,384,384]{2,1,0:T(8,128)(2,1)S(1)}, bf16[4,384,384]{2,1,0:T(8,128)(2,1)}, u32[]{:S(2)}) copy-start(bf16[4,384,384]{2,1,0:T(8,128)(2,1)} %param.8) | copy-start | bytes 3538948
  35.0 1.5 copy-start.2
  35.0 1.5 copy-start.3
  82.5 6.5 %copy-start.1 = (f32[1,48,384]{2,1,0:T(8,128)S(1)}, f32[1,48,384]{2,1,0:T(8,128)}, u32[]{:S(2)}) copy-start(f32[1,48,384]{2,1,0:T(8,128)} %param.6) | copy-start | bytes 221188
  82.8 2.6 %collective-permute-start = (bf16[2,48,384]{2,1,0:T(8,128)(2,1)S(1)}, bf16[2,48,384]{2,1,0:T(8,128)(2,1)S(1)}, u32[]{:S(2)}, u32[]{:S(2)}) collective-permute-start(bf16[2,48,384]{2,1,0:T(8,128)(2,1)S(1)} %get-tuple-element.7), channel_id=1, source_target_pairs={{0,8},{8,16},{16,24},{1,9},{9,17},{17,25},{2,10},{10,18},{18,26},{... | collective-permute-start | bytes 221192 | tf_op jit(solution)/shard_map/ppermute | solution.py:12
  84.1 4.9 %collective-permute-start.1 = (bf16[2,48,384]{2,1,0:T(8,128)(2,1)S(1)}, bf16[2,48,384]{2,1,0:T(8,128)(2,1)S(1)}, u32[]{:S(2)}, u32[]{:S(2)}) collective-permute-start(bf16[2,48,384]{2,1,0:T(8,128)(2,1)S(1)} %get-tuple-element.8), channel_id=1, source_target_pairs={{8,0},{16,8},{24,16},{9,1},{17,9},{25,17},{10,2},{18,10},{26,18},{... | collective-permute-start | bytes 221192 | tf_op jit(solution)/shard_map/ppermute | solution.py:12
  171.3 2.6 %collective-permute-start.2 = (bf16[2,48,384]{2,1,0:T(8,128)(2,1)S(1)}, bf16[2,48,384]{2,1,0:T(8,128)(2,1)S(1)}, u32[]{:S(2)}, u32[]{:S(2)}) collective-permute-start(bf16[2,48,384]{2,1,0:T(8,128)(2,1)S(1)} %get-tuple-element.5), channel_id=1, source_target_pairs={{0,8},{8,16},{16,24},{1,9},{9,17},{17,25},{2,10},{10,18},{18,26},{... | collective-permute-start | bytes 221192 | tf_op jit(solution)/shard_map/ppermute | solution.py:12
  172.6 3.2 %collective-permute-start.3 = (bf16[2,48,384]{2,1,0:T(8,128)(2,1)S(1)}, bf16[2,48,384]{2,1,0:T(8,128)(2,1)S(1)}, u32[]{:S(2)}, u32[]{:S(2)}) collective-permute-start(bf16[2,48,384]{2,1,0:T(8,128)(2,1)S(1)} %get-tuple-element.6), channel_id=1, source_target_pairs={{8,0},{16,8},{24,16},{9,1},{17,9},{25,17},{10,2},{18,10},{26,18},{... | collective-permute-start | bytes 221192 | tf_op jit(solution)/shard_map/ppermute | solution.py:12
where the time goes:
time: 177 us; the launch traced here: 176 us
  blocking collectives  148 us (84%)
  matrix products  15.2 us (9%)
  waiting for transfers between devices  5.45 us (3%)
  starting transfers between devices  5.17 us (3%)
    all_to_all x2, blocking collectives, on_device(): lax.all_to_all(shaped, 'op', split_axis=2, concat_axis=2, tiled=True)  82.8 us
    all_gather x2, blocking collectives, on_device(): rows_block = lax.all_gather(trial_vec, 'op', axis=2, tiled=True)[0]  65.4 us
    ppermute x4, waiting for transfers between devices, from_behind(): return lax.ppermute(block, axis, route)  5.45 us
    ppermute x4, starting transfers between devices, from_behind(): return lax.ppermute(block, axis, route)  5.17 us
  transfers between devices with their start and end apart: 4, of which 2 were waited for; matrix products, arithmetic and copies ran while one was open for 0% of the time, Pallas kernels for 0%

commit v1 on v0

v1 whole, which is shorter than its diff:
```python
import jax
import jax.numpy as jnp
from jax import lax
from jax.sharding import PartitionSpec as P

ITERS = 2


def swap(block, axis, distance):
    route = [(i, i ^ distance) for i in range(lax.axis_size(axis))]
    return lax.ppermute(block, axis, route)


def side(axis, distance):
    return lax.rem(lax.axis_index(axis) // distance, 2)


def split(block, distance, rows):
    roots, height, width = block.shape
    return block.reshape(roots, height // (2 * rows), 2, rows, width)


def widen(block, distance, which):
    other = swap(block, "op", distance)
    low = jnp.where(which == 0, block, other)
    high = jnp.where(which == 0, other, block)
    return low, high


def on_device(wavefunction, diagonal, left_ops, right_ops, offsets):
    nothing = jnp.zeros((), jnp.bfloat16)
    raise_mask = (offsets[:, 0] == 1)[:, None, None]
    lower_mask = (offsets[:, 1] == 1)[:, None, None]
    left_raise = jnp.where(raise_mask, left_ops, nothing)
    left_stay = jnp.where(raise_mask, nothing, left_ops)
    left_lower = jnp.where(lower_mask, left_ops, nothing)
    left_back = jnp.where(lower_mask, nothing, left_ops)
    members = lax.axis_size("op")
    sectors = lax.axis_size("sec")
    odd = side("sec", 1) == 1
    steps = [1 << k for k in range(members.bit_length() - 1)]
    roots, shard, width = wavefunction.shape[1:]
    own = diagonal[0]
    last = steps[-1]
    last_side = side("op", last)
    other = swap(own, "op", last)
    both = jnp.stack([jnp.where(last_side == 0, own, other), jnp.where(last_side == 0, other, own)])

    def grow(block, distance):
        which = side("op", distance)
        arrived = swap(block, "op", distance)
        low = jnp.where(which == 0, block, arrived)
        high = jnp.where(which == 0, arrived, block)
        return jnp.stack([low, high], axis=2).reshape(roots, -1, shard, width)

    def gather(block, distances):
        for distance in distances:
            block = grow(block, distance)
        return block

    vector = gather(wavefunction[0][:, None], steps[::-1])
    for turn in range(ITERS):
        rows_block = vector.reshape(roots, members * shard, width)
        turned = jnp.einsum(
            "xab,pcb->pxac", rows_block, right_ops, preferred_element_type=jnp.float32
        ).astype(jnp.bfloat16)
        plain = jnp.einsum(
            "xab,pbc->pxac", rows_block, right_ops, preferred_element_type=jnp.float32
        ).astype(jnp.bfloat16)
        raised = jnp.einsum(
            "pab,pxbc->xac", left_raise, turned, preferred_element_type=jnp.float32
        ).astype(jnp.bfloat16)
        lowered = jnp.einsum(
            "pba,pxbc->xac", left_lower, plain, preferred_element_type=jnp.float32
        ).astype(jnp.bfloat16)
        staying = jnp.einsum(
            "pab,pxbc->xac", left_stay, turned, preferred_element_type=jnp.float32
        )
        staying = staying + jnp.einsum(
            "pba,pxbc->xac", left_back, plain, preferred_element_type=jnp.float32
        )
        staying = staying.astype(jnp.bfloat16)
        near = jnp.where(odd, lowered, raised)
        cross = jnp.where(odd, raised, lowered)
        from_cross = lax.ppermute(
            cross,
            "sec",
            [(i, i + 1) for i in range(1, sectors - 1, 2)] + [(i, i - 1) for i in range(2, sectors, 2)],
        )
        from_near = swap(near, "sec", 1)
        block = (
            staying.astype(jnp.float32) + from_near.astype(jnp.float32) + from_cross.astype(jnp.float32)
        ).astype(jnp.bfloat16)
        block = block.reshape(roots, members, shard, width)
        final = turn == ITERS - 1
        for distance in steps:
            which = side("op", distance)
            if distance == last and not final:
                arrived = swap(block, "op", distance)
                total = block.astype(jnp.float32) + arrived.astype(jnp.float32)
                block = (total / both[None]).astype(jnp.bfloat16)
                break
            halves = block.reshape(roots, -1, 2, shard, width)
            keep = jnp.where(which == 0, halves[:, :, 0], halves[:, :, 1])
            send = jnp.where(which == 0, halves[:, :, 1], halves[:, :, 0])
            arrived = swap(send, "op", distance)
            total = keep.astype(jnp.float32) + arrived.astype(jnp.float32)
            if distance == last:
                return (total[:, 0] / own[None]).astype(jnp.bfloat16)[None]
            block = total.astype(jnp.bfloat16)
        vector = gather(block, steps[-2::-1])


def solution(mesh):
    in_specs = (
        P("sec", None, "op", None),
        P("sec", "op", None),
        P(("sec", "op"), None, None),
        P(("sec", "op"), None, None),
        P(("sec", "op"), None),
    )
    out_specs = P("sec", None, "op", None)
    return jax.shard_map(
        on_device, mesh=mesh, in_specs=in_specs, out_specs=out_specs, check_vma=False
    )
```

time: 177 us -> 110 us (0.62)
  the two profiles are of different devices: /device:TPU:0 before, /device:TPU:28 now
where the time goes in v1:
time: 110 us
  waiting for transfers between devices  78.6 us (71%)
  matrix products  15.5 us (14%)
  starting transfers between devices  12.3 us (11%)
  other arithmetic  2.61 us (2%)
    ppermute x14, waiting for transfers between devices, swap(): return lax.ppermute(block, axis, route)  63.2 us
    ppermute x2, waiting for transfers between devices, on_device(): lax.ppermute(cross, 'sec', [(i, i + 1) for i in range(1, sectors - 1, 2)]...  15.5 us
    ppermute x14, starting transfers between devices, swap(): return lax.ppermute(block, axis, route)  7.73 us
    ppermute x2, starting transfers between devices, on_device(): lax.ppermute(cross, 'sec', [(i, i + 1) for i in range(1, sectors - 1, 2)]...  4.61 us
    dot_general x2, matrix products, on_device(): jnp.einsum('xab,pcb->pxac', rows_block, right_ops, preferred_element_type...  2.84 us
    dot_general x2, matrix products, on_device(): jnp.einsum('pba,pxbc->xac', left_back, plain, preferred_element_type=jnp....  2.82 us
    dot_general x2, matrix products, on_device(): jnp.einsum('xab,pbc->pxac', rows_block, right_ops, preferred_element_type...  2.77 us
    dot_general x2, matrix products, on_device(): jnp.einsum('pba,pxbc->xac', left_lower, plain, preferred_element_type=jnp...  2.48 us
  transfers between devices with their start and end apart: 16, of which 13 were waited for; matrix products, arithmetic and copies ran while one was open for 2% of the time, Pallas kernels for 0%

profile of v1, /device:TPU:28, one launch (start us, length us, event | category | flops | bytes accessed | tf_op | source)
XLA Modules:
  0.0 109.7 jit_solution(649117523852639057)
XLA Ops:
  0.3 6.2 %collective-permute-done = bf16[2,1,48,384]{3,2,0,1:T(8,128)(2,1)S(1)} collective-permute-done((bf16[2,1,48,384]{3,2,0,1:T(8,128)(2,1)}, bf16[2,1,48,384]{3,2,0,1:T(8,128)(2,1)S(1)}, u32[]{:S(2)}, u32[]{:S(2)}) %collective-permute-start) | collective-permute-done | bytes 73760 | tf_op jit(solution)/shard_map/ppermute | solution.py:11
  6.6 0.9 select_bitcast_fusion.19
  7.6 5.5 %collective-permute-done.1 = bf16[2,2,48,384]{3,2,1,0:T(8,128)(2,1)S(1)} collective-permute-done((bf16[2,2,48,384]{3,2,1,0:T(8,128)(2,1)S(1)}, bf16[2,2,48,384]{3,2,1,0:T(8,128)(2,1)S(1)}, u32[]{:S(2)}, u32[]{:S(2)}) %collective-permute-start.1) | collective-permute-done | bytes 147488 | tf_op jit(solution)/shard_map/ppermute | solution.py:11
  13.2 1.6 %collective-permute-start.2 = (bf16[2,4,48,384]{3,2,1,0:T(8,128)(2,1)S(1)}, bf16[2,4,48,384]{3,2,1,0:T(8,128)(2,1)S(1)}, u32[]{:S(2)}, u32[]{:S(2)}) collective-permute-start(bf16[2,4,48,384]{3,2,1,0:T(8,128)(2,1)S(1)} %bitcast.343), channel_id=1, source_target_pairs={{0,1},{1,0},{2,3},{3,2},{4,5},{5,4},{6,7},{7,6},{8,9},{9,8},{10,11... | collective-permute-start | bytes 884744 | tf_op jit(solution)/shard_map/ppermute | solution.py:11
  14.8 6.3 %collective-permute-done.2 = bf16[2,4,48,384]{3,2,1,0:T(8,128)(2,1)S(1)} collective-permute-done((bf16[2,4,48,384]{3,2,1,0:T(8,128)(2,1)S(1)}, bf16[2,4,48,384]{3,2,1,0:T(8,128)(2,1)S(1)}, u32[]{:S(2)}, u32[]{:S(2)}) %collective-permute-start.2) | collective-permute-done | bytes 294944 | tf_op jit(solution)/shard_map/ppermute | solution.py:11
  21.3 1.4 %convolution_convert_fusion.2 = bf16[2,384,4,384]{3,1,2,0:T(8,128)(2,1)S(1)} fusion(bf16[2,384,384,1]{2,1,3,0:T(8,128)(2,1)S(1)} %bitcast.347, bf16[4,384,384]{2,1,0:T(8,128)(2,1)S(1)} %copy-done), kind=kOutput, calls=%fused_computation.18 | convolution fusion | flops 907149312 | bytes 4128768 | tf_op jit(solution)/shard_map/xab,pbc->pxac/dot_general | solution.py:67
  22.7 1.4 %convolution_convert_fusion.3 = bf16[2,384,4,384]{3,1,2,0:T(8,128)(2,1)S(1)} fusion(bf16[2,384,384,1]{2,1,3,0:T(8,128)(2,1)S(1)} %bitcast.348, bf16[4,384,384]{2,1,0:T(8,128)(2,1)S(1)} %copy-done), kind=kOutput, calls=%fused_computation.19 | convolution fusion | flops 907149312 | bytes 4128768 | tf_op jit(solution)/shard_map/xab,pcb->pxac/dot_general | solution.py:64
  24.1 1.2 %fusion.52 = bf16[2,384,384]{1,2,0:T(8,128)(2,1)S(1)} fusion(bf16[2,384,4,384]{3,1,2,0:T(8,128)(2,1)S(1)} %convolution_convert_fusion.2, bf16[4,384,384]{2,1,0:T(8,128)(2,1)S(1)} %copy-done.3, pred[4]{0:T(512)(128)(4,1)S(1)} %get-tuple-element.21), kind=kOutput, calls=%fused_computation.32 | convolution fusion | flops 906854400 | bytes 4128772 | tf_op jit(solution)/shard_map/pba,pxbc->xac/dot_general | solution.py:73
  25.4 1.2 %select_bitcast_fusion.3 = (bf16[2,384,384]{2,1,0:T(8,128)(2,1)S(1)}, bf16[2,384,384]{2,1,0:T(8,128)(2,1)S(1)}) fusion(bf16[2,384,384]{1,2,0:T(8,128)(2,1)S(1)} %fusion.52, pred[]{:T(512)S(6)} %eq.58, bf16[2,384,4,384]{3,1,2,0:T(8,128)(2,1)S(1)} %convolution_convert_fusion.3, bf16[4,384,384]{2,1,0:T(8,128)(2,1)S(1)} %copy-done.3, ...), kind=kOutput, calls=%fused_computation.67 | convolution fusion | flops 907444224 | bytes 5308421 | tf_op jit(solution)/shard_map/pab,pxbc->xac/dot_general | solution.py:70
  26.6 2.7 %collective-permute-start.4 = (bf16[2,384,384]{2,1,0:T(8,128)(2,1)S(1)}, bf16[2,384,384]{2,1,0:T(8,128)(2,1)S(1)}, u32[]{:S(2)}, u32[]{:S(2)}) collective-permute-start(bf16[2,384,384]{2,1,0:T(8,128)(2,1)S(1)} %get-tuple-element.8), channel_id=1, source_target_pairs={{8,16},{16,8},{9,17},{17,9},{10,18},{18,10},{11,19},{19,11},{12,20... | collective-permute-start | bytes 1769480 | tf_op jit(solution)/shard_map/ppermute | solution.py:85
  29.3 1.1 %fusion.19 = f32[2,384,384]{1,2,0:T(8,128)S(1)} fusion(bf16[2,384,4,384]{3,1,2,0:T(8,128)(2,1)S(1)} %convolution_convert_fusion.3, bf16[4,384,384]{2,1,0:T(8,128)(2,1)S(1)} %copy-done.3, pred[4]{0:T(512)(128)(4,1)S(1)} %get-tuple-element.22), kind=kOutput, calls=%fused_computation.21 | convolution fusion | flops 906559488 | bytes 4718596 | tf_op jit(solution)/shard_map/pab,pxbc->xac/dot_general | solution.py:76
  30.5 7.3 %collective-permute-done.4 = bf16[2,384,384]{2,1,0:T(8,128)(2,1)S(1)} collective-permute-done((bf16[2,384,384]{2,1,0:T(8,128)(2,1)S(1)}, bf16[2,384,384]{2,1,0:T(8,128)(2,1)S(1)}, u32[]{:S(2)}, u32[]{:S(2)}) %collective-permute-start.4) | collective-permute-done | bytes 589856 | tf_op jit(solution)/shard_map/ppermute | solution.py:85
  37.8 1.4 %add_convert_fusion.1 = bf16[2,384,384]{2,1,0:T(8,128)(2,1)S(1)} fusion(bf16[2,384,384]{2,1,0:T(8,128)(2,1)S(1)} %collective-permute-done.4, bf16[2,384,384]{2,1,0:T(8,128)(2,1)S(1)} %collective-permute-done.3, f32[2,384,384]{1,2,0:T(8,128)S(1)} %fusion.19, bf16[4,384,384]{2,1,0:T(8,128)(2,1)S(1)} %copy-done.3, pred[4]{0:T(512)(128)(4,1)S(1)} %get-tuple-element.21, ...), kind=kOutput, calls=%fused_computation.53 | convolution fusion | flops 908918784 | bytes 6488068 | tf_op jit(solution)/shard_map/pba,pxbc->xac/dot_general | solution.py:79
  39.3 1.6 %collective-permute-start.5 = (bf16[2,4,48,384]{3,2,1,0:T(8,128)(2,1)S(1)}, bf16[2,4,48,384]{3,2,1,0:T(8,128)(2,1)S(1)}, u32[]{:S(2)}, u32[]{:S(2)}) collective-permute-start(bf16[2,4,48,384]{3,2,1,0:T(8,128)(2,1)S(1)} %select_bitcast_fusion.7), channel_id=1, source_target_pairs={{0,1},{1,0},{2,3},{3,2},{4,5},{5,4},{6,7},{7,6},{8,9},{9,8},{10,11... | collective-permute-start | bytes 884744 | tf_op jit(solution)/shard_map/ppermute | solution.py:11
  40.9 5.2 %collective-permute-done.5 = bf16[2,4,48,384]{3,2,1,0:T(8,128)(2,1)S(1)} collective-permute-done((bf16[2,4,48,384]{3,2,1,0:T(8,128)(2,1)S(1)}, bf16[2,4,48,384]{3,2,1,0:T(8,128)(2,1)S(1)}, u32[]{:S(2)}, u32[]{:S(2)}) %collective-permute-start.5) | collective-permute-done | bytes 294944 | tf_op jit(solution)/shard_map/ppermute | solution.py:11
  46.9 6.6 %collective-permute-done.6 = bf16[2,2,48,384]{3,2,1,0:T(8,128)(2,1)S(1)} collective-permute-done((bf16[2,2,48,384]{3,2,1,0:T(8,128)(2,1)S(1)}, bf16[2,2,48,384]{3,2,1,0:T(8,128)(2,1)S(1)}, u32[]{:S(2)}, u32[]{:S(2)}) %collective-permute-start.6) | collective-permute-done | bytes 147488 | tf_op jit(solution)/shard_map/ppermute | solution.py:11
  53.7 7.1 %collective-permute-done.7 = bf16[2,2,48,384]{3,2,1,0:T(8,128)(2,1)S(1)} collective-permute-done((bf16[2,2,48,384]{3,2,1,0:T(8,128)(2,1)S(1)}, bf16[2,2,48,384]{3,2,1,0:T(8,128)(2,1)S(1)}, u32[]{:S(2)}, u32[]{:S(2)}) %collective-permute-start.7) | collective-permute-done | bytes 147488 | tf_op jit(solution)/shard_map/ppermute | solution.py:11
  60.9 5.1 %collective-permute-done.9 = bf16[2,2,48,384]{3,2,1,0:T(8,128)(2,1)S(1)} collective-permute-done((bf16[2,2,48,384]{3,2,1,0:T(8,128)(2,1)S(1)}, bf16[2,2,48,384]{3,2,1,0:T(8,128)(2,1)S(1)}, u32[]{:S(2)}, u32[]{:S(2)}) %collective-permute-start.9) | collective-permute-done | bytes 147488 | tf_op jit(solution)/shard_map/ppermute | solution.py:11
  66.2 1.6 %collective-permute-start.10 = (bf16[2,4,48,384]{3,2,1,0:T(8,128)(2,1)S(1)}, bf16[2,4,48,384]{3,2,1,0:T(8,128)(2,1)S(1)}, u32[]{:S(2)}, u32[]{:S(2)}) collective-permute-start(bf16[2,4,48,384]{3,2,1,0:T(8,128)(2,1)S(1)} %bitcast.345), channel_id=1, source_target_pairs={{0,1},{1,0},{2,3},{3,2},{4,5},{5,4},{6,7},{7,6},{8,9},{9,8},{10,11... | collective-permute-start | bytes 884744 | tf_op jit(solution)/shard_map/ppermute | solution.py:11
  67.8 5.2 %collective-permute-done.10 = bf16[2,4,48,384]{3,2,1,0:T(8,128)(2,1)S(1)} collective-permute-done((bf16[2,4,48,384]{3,2,1,0:T(8,128)(2,1)S(1)}, bf16[2,4,48,384]{3,2,1,0:T(8,128)(2,1)S(1)}, u32[]{:S(2)}, u32[]{:S(2)}) %collective-permute-start.10) | collective-permute-done | bytes 294944 | tf_op jit(solution)/shard_map/ppermute | solution.py:11
  73.2 1.4 %convolution_convert_fusion = bf16[2,384,4,384]{3,1,2,0:T(8,128)(2,1)S(1)} fusion(bf16[2,384,384,1]{2,1,3,0:T(8,128)(2,1)S(1)} %bitcast.349, bf16[4,384,384]{2,1,0:T(8,128)(2,1)S(1)} %copy-done), kind=kOutput, calls=%fused_computation.16 | convolution fusion | flops 907149312 | bytes 4128768 | tf_op jit(solution)/shard_map/xab,pbc->pxac/dot_general | solution.py:67
  74.6 1.4 %convolution_convert_fusion.1 = bf16[2,384,4,384]{3,1,2,0:T(8,128)(2,1)S(1)} fusion(bf16[2,384,384,1]{2,1,3,0:T(8,128)(2,1)S(1)} %bitcast.350, bf16[4,384,384]{2,1,0:T(8,128)(2,1)S(1)} %copy-done), kind=kOutput, calls=%fused_computation.17 | convolution fusion | flops 907149312 | bytes 4128768 | tf_op jit(solution)/shard_map/xab,pcb->pxac/dot_general | solution.py:64
  76.0 1.2 %fusion.46 = bf16[2,384,384]{1,2,0:T(8,128)(2,1)S(1)} fusion(bf16[2,384,4,384]{3,1,2,0:T(8,128)(2,1)S(1)} %convolution_convert_fusion, bf16[4,384,384]{2,1,0:T(8,128)(2,1)S(1)} %copy-done.3, pred[4]{0:T(512)(128)(4,1)S(1)} %get-tuple-element.21), kind=kOutput, calls=%fused_computation.30 | convolution fusion | flops 906854400 | bytes 4128772 | tf_op jit(solution)/shard_map/pba,pxbc->xac/dot_general | solution.py:73
  77.3 1.2 %select_bitcast_fusion.1 = (bf16[2,384,384]{2,1,0:T(8,128)(2,1)S(1)}, bf16[2,384,384]{2,1,0:T(8,128)(2,1)S(1)}) fusion(bf16[2,384,384]{1,2,0:T(8,128)(2,1)S(1)} %fusion.46, pred[]{:T(512)S(6)} %eq.58, bf16[2,384,4,384]{3,1,2,0:T(8,128)(2,1)S(1)} %convolution_convert_fusion.1, bf16[4,384,384]{2,1,0:T(8,128)(2,1)S(1)} %copy-done.3, ...), kind=kOutput, calls=%fused_computation.65 | convolution fusion | flops 907444224 | bytes 5308421 | tf_op jit(solution)/shard_map/pab,pxbc->xac/dot_general | solution.py:70
  78.5 1.9 %collective-permute-start.12 = (bf16[2,384,384]{2,1,0:T(8,128)(2,1)S(1)}, bf16[2,384,384]{2,1,0:T(8,128)(2,1)S(1)}, u32[]{:S(2)}, u32[]{:S(2)}) collective-permute-start(bf16[2,384,384]{2,1,0:T(8,128)(2,1)S(1)} %get-tuple-element.6), channel_id=1, source_target_pairs={{8,16},{16,8},{9,17},{17,9},{10,18},{18,10},{11,19},{19,11},{12,20... | collective-permute-start | bytes 1769480 | tf_op jit(solution)/shard_map/ppermute | solution.py:85
  80.4 1.1 %fusion.31 = f32[2,384,384]{1,2,0:T(8,128)S(1)} fusion(bf16[2,384,4,384]{3,1,2,0:T(8,128)(2,1)S(1)} %convolution_convert_fusion.1, bf16[4,384,384]{2,1,0:T(8,128)(2,1)S(1)} %copy-done.3, pred[4]{0:T(512)(128)(4,1)S(1)} %get-tuple-element.22), kind=kOutput, calls=%fused_computation.25 | convolution fusion | flops 906559488 | bytes 4718596 | tf_op jit(solution)/shard_map/pab,pxbc->xac/dot_general | solution.py:76
  81.6 8.1 %collective-permute-done.12 = bf16[2,384,384]{2,1,0:T(8,128)(2,1)S(1)} collective-permute-done((bf16[2,384,384]{2,1,0:T(8,128)(2,1)S(1)}, bf16[2,384,384]{2,1,0:T(8,128)(2,1)S(1)}, u32[]{:S(2)}, u32[]{:S(2)}) %collective-permute-start.12) | collective-permute-done | bytes 589856 | tf_op jit(solution)/shard_map/ppermute | solution.py:85
  89.7 1.4 %add_convert_fusion = bf16[2,384,384]{2,1,0:T(8,128)(2,1)S(1)} fusion(bf16[2,384,384]{2,1,0:T(8,128)(2,1)S(1)} %collective-permute-done.12, bf16[2,384,384]{2,1,0:T(8,128)(2,1)S(1)} %collective-permute-done.11, f32[2,384,384]{1,2,0:T(8,128)S(1)} %fusion.31, bf16[4,384,384]{2,1,0:T(8,128)(2,1)S(1)} %copy-done.3, pred[4]{0:T(512)(128)(4,1)S(1)} %get-tuple-element.21, ...), kind=kOutput, calls=%fused_computation.52 | convolution fusion | flops 908918784 | bytes 6488068 | tf_op jit(solution)/shard_map/pba,pxbc->xac/dot_general | solution.py:79
  91.2 1.6 %collective-permute-start.13 = (bf16[2,4,48,384]{3,2,1,0:T(8,128)(2,1)S(1)}, bf16[2,4,48,384]{3,2,1,0:T(8,128)(2,1)S(1)}, u32[]{:S(2)}, u32[]{:S(2)}) collective-permute-start(bf16[2,4,48,384]{3,2,1,0:T(8,128)(2,1)S(1)} %select_bitcast_fusion.4), channel_id=1, source_target_pairs={{0,1},{1,0},{2,3},{3,2},{4,5},{5,4},{6,7},{7,6},{8,9},{9,8},{10,11... | collective-permute-start | bytes 884744 | tf_op jit(solution)/shard_map/ppermute | solution.py:11
  92.7 5.2 %collective-permute-done.13 = bf16[2,4,48,384]{3,2,1,0:T(8,128)(2,1)S(1)} collective-permute-done((bf16[2,4,48,384]{3,2,1,0:T(8,128)(2,1)S(1)}, bf16[2,4,48,384]{3,2,1,0:T(8,128)(2,1)S(1)}, u32[]{:S(2)}, u32[]{:S(2)}) %collective-permute-start.13) | collective-permute-done | bytes 294944 | tf_op jit(solution)/shard_map/ppermute | solution.py:11
  98.2 5.1 %collective-permute-done.14 = bf16[2,2,48,384]{3,2,1,0:T(8,128)(2,1)S(1)} collective-permute-done((bf16[2,2,48,384]{3,2,1,0:T(8,128)(2,1)S(1)}, bf16[2,2,48,384]{3,2,1,0:T(8,128)(2,1)S(1)}, u32[]{:S(2)}, u32[]{:S(2)}) %collective-permute-start.14) | collective-permute-done | bytes 147488 | tf_op jit(solution)/shard_map/ppermute | solution.py:11
  103.5 5.5 %collective-permute-done.15 = bf16[2,1,48,384]{3,2,0,1:T(8,128)(2,1)S(1)} collective-permute-done((bf16[2,1,48,384]{3,2,0,1:T(8,128)(2,1)S(1)}, bf16[2,1,48,384]{3,2,0,1:T(8,128)(2,1)S(1)}, u32[]{:S(2)}, u32[]{:S(2)}) %collective-permute-start.15) | collective-permute-done | bytes 73760 | tf_op jit(solution)/shard_map/ppermute | solution.py:11
  (47 shorter events, 3.4 us)
Async XLA Ops:
  0.0 21.3 %copy-start = (bf16[4,384,384]{2,1,0:T(8,128)(2,1)S(1)}, bf16[4,384,384]{2,1,0:T(8,128)(2,1)}, u32[]{:S(2)}) copy-start(bf16[4,384,384]{2,1,0:T(8,128)(2,1)} %param.8) | copy-start | bytes 3538948
  0.0 14.8 %copy-start.2 = (s32[4,2]{0,1:T(2,128)S(1)}, s32[4,2]{0,1:T(2,128)}, u32[]{:S(2)}) copy-start(s32[4,2]{0,1:T(2,128)} %param.9) | copy-start | bytes 100
  0.0 6.6 %collective-permute-start = (bf16[2,1,48,384]{3,2,0,1:T(8,128)(2,1)}, bf16[2,1,48,384]{3,2,0,1:T(8,128)(2,1)S(1)}, u32[]{:S(2)}, u32[]{:S(2)}) collective-permute-start(bf16[2,1,48,384]{3,2,0,1:T(8,128)(2,1)} %bitcast.353), channel_id=1, source_target_pairs={{0,4},{1,5},{2,6},{3,7},{4,0},{5,1},{6,2},{7,3},{8,12},{9,13},{10,... | collective-permute-start | bytes 221192 | tf_op jit(solution)/shard_map/ppermute | solution.py:11
  7.5 5.6 %collective-permute-start.1 = (bf16[2,2,48,384]{3,2,1,0:T(8,128)(2,1)S(1)}, bf16[2,2,48,384]{3,2,1,0:T(8,128)(2,1)S(1)}, u32[]{:S(2)}, u32[]{:S(2)}) collective-permute-start(bf16[2,2,48,384]{3,2,1,0:T(8,128)(2,1)S(1)} %maximum_bitcast_fusion), channel_id=1, source_target_pairs={{0,2},{1,3},{2,0},{3,1},{4,6},{5,7},{6,4},{7,5},{8,10},{9,11},{10,... | collective-permute-start | bytes 442376 | tf_op jit(solution)/shard_map/ppermute | solution.py:11
  13.2 7.9 %collective-permute-start.2 = (bf16[2,4,48,384]{3,2,1,0:T(8,128)(2,1)S(1)}, bf16[2,4,48,384]{3,2,1,0:T(8,128)(2,1)S(1)}, u32[]{:S(2)}, u32[]{:S(2)}) collective-permute-start(bf16[2,4,48,384]{3,2,1,0:T(8,128)(2,1)S(1)} %bitcast.343), channel_id=1, source_target_pairs={{0,1},{1,0},{2,3},{3,2},{4,5},{5,4},{6,7},{7,6},{8,9},{9,8},{10,11... | collective-permute-start | bytes 884744 | tf_op jit(solution)/shard_map/ppermute | solution.py:11
  22.7 1.4 %copy-start.3 = (bf16[4,384,384]{2,1,0:T(8,128)(2,1)S(1)}, bf16[4,384,384]{2,1,0:T(8,128)(2,1)}, u32[]{:S(2)}) copy-start(bf16[4,384,384]{2,1,0:T(8,128)(2,1)} %param.7) | copy-start | bytes 3538948
  26.5 3.9 %collective-permute-start.3 = (bf16[2,384,384]{2,1,0:T(8,128)(2,1)S(1)}, bf16[2,384,384]{2,1,0:T(8,128)(2,1)S(1)}, u32[]{:S(2)}, u32[]{:S(2)}) collective-permute-start(bf16[2,384,384]{2,1,0:T(8,128)(2,1)S(1)} %get-tuple-element.7), channel_id=1, source_target_pairs={{0,8},{8,0},{16,24},{24,16},{1,9},{9,1},{17,25},{25,17},{2,10},{10... | collective-permute-start | bytes 1769480 | tf_op jit(solution)/shard_map/ppermute | solution.py:11
  26.6 11.2 %collective-permute-start.4 = (bf16[2,384,384]{2,1,0:T(8,128)(2,1)S(1)}, bf16[2,384,384]{2,1,0:T(8,128)(2,1)S(1)}, u32[]{:S(2)}, u32[]{:S(2)}) collective-permute-start(bf16[2,384,384]{2,1,0:T(8,128)(2,1)S(1)} %get-tuple-element.8), channel_id=1, source_target_pairs={{8,16},{16,8},{9,17},{17,9},{10,18},{18,10},{11,19},{19,11},{12,20... | collective-permute-start | bytes 1769480 | tf_op jit(solution)/shard_map/ppermute | solution.py:85
  39.2 7.7 %copy-start.1 = (f32[1,48,384]{2,1,0:T(8,128)S(1)}, f32[1,48,384]{2,1,0:T(8,128)}, u32[]{:S(2)}) copy-start(f32[1,48,384]{2,1,0:T(8,128)} %param.6) | copy-start | bytes 221188
  39.3 6.8 %collective-permute-start.5 = (bf16[2,4,48,384]{3,2,1,0:T(8,128)(2,1)S(1)}, bf16[2,4,48,384]{3,2,1,0:T(8,128)(2,1)S(1)}, u32[]{:S(2)}, u32[]{:S(2)}) collective-permute-start(bf16[2,4,48,384]{3,2,1,0:T(8,128)(2,1)S(1)} %select_bitcast_fusion.7), channel_id=1, source_target_pairs={{0,1},{1,0},{2,3},{3,2},{4,5},{5,4},{6,7},{7,6},{8,9},{9,8},{10,11... | collective-permute-start | bytes 884744 | tf_op jit(solution)/shard_map/ppermute | solution.py:11
  46.2 7.3 %collective-permute-start.6 = (bf16[2,2,48,384]{3,2,1,0:T(8,128)(2,1)S(1)}, bf16[2,2,48,384]{3,2,1,0:T(8,128)(2,1)S(1)}, u32[]{:S(2)}, u32[]{:S(2)}) collective-permute-start(bf16[2,2,48,384]{3,2,1,0:T(8,128)(2,1)S(1)} %select_bitcast_fusion.13), channel_id=1, source_target_pairs={{0,2},{1,3},{2,0},{3,1},{4,6},{5,7},{6,4},{7,5},{8,10},{9,11},{10,... | collective-permute-start | bytes 442376 | tf_op jit(solution)/shard_map/ppermute | solution.py:11
  46.9 6.7 %collective-permute-start.8 = (f32[48,384]{1,0:T(8,128)S(1)}, f32[48,384]{1,0:T(8,128)S(1)}, u32[]{:S(2)}, u32[]{:S(2)}) collective-permute-start(f32[48,384]{1,0:T(8,128)S(1)} %bitcast.351), channel_id=1, source_target_pairs={{0,4},{1,5},{2,6},{3,7},{4,0},{5,1},{6,2},{7,3},{8,12},{9,13},{10,... | collective-permute-start | bytes 221192 | tf_op jit(solution)/shard_map/ppermute | solution.py:11
  53.6 7.2 %collective-permute-start.7 = (bf16[2,2,48,384]{3,2,1,0:T(8,128)(2,1)S(1)}, bf16[2,2,48,384]{3,2,1,0:T(8,128)(2,1)S(1)}, u32[]{:S(2)}, u32[]{:S(2)}) collective-permute-start(bf16[2,2,48,384]{3,2,1,0:T(8,128)(2,1)S(1)} %fusion.99), channel_id=1, source_target_pairs={{0,4},{1,5},{2,6},{3,7},{4,0},{5,1},{6,2},{7,3},{8,12},{9,13},{10,... | collective-permute-start | bytes 442376 | tf_op jit(solution)/shard_map/ppermute | solution.py:11
  60.9 5.2 %collective-permute-start.9 = (bf16[2,2,48,384]{3,2,1,0:T(8,128)(2,1)S(1)}, bf16[2,2,48,384]{3,2,1,0:T(8,128)(2,1)S(1)}, u32[]{:S(2)}, u32[]{:S(2)}) collective-permute-start(bf16[2,2,48,384]{3,2,1,0:T(8,128)(2,1)S(1)} %divide_convert_fusion), channel_id=1, source_target_pairs={{0,2},{1,3},{2,0},{3,1},{4,6},{5,7},{6,4},{7,5},{8,10},{9,11},{10,... | collective-permute-start | bytes 442376 | tf_op jit(solution)/shard_map/ppermute | solution.py:11
  66.2 6.8 %collective-permute-start.10 = (bf16[2,4,48,384]{3,2,1,0:T(8,128)(2,1)S(1)}, bf16[2,4,48,384]{3,2,1,0:T(8,128)(2,1)S(1)}, u32[]{:S(2)}, u32[]{:S(2)}) collective-permute-start(bf16[2,4,48,384]{3,2,1,0:T(8,128)(2,1)S(1)} %bitcast.345), channel_id=1, source_target_pairs={{0,1},{1,0},{2,3},{3,2},{4,5},{5,4},{6,7},{7,6},{8,9},{9,8},{10,11... | collective-permute-start | bytes 884744 | tf_op jit(solution)/shard_map/ppermute | solution.py:11
  78.4 3.2 %collective-permute-start.11 = (bf16[2,384,384]{2,1,0:T(8,128)(2,1)S(1)}, bf16[2,384,384]{2,1,0:T(8,128)(2,1)S(1)}, u32[]{:S(2)}, u32[]{:S(2)}) collective-permute-start(bf16[2,384,384]{2,1,0:T(8,128)(2,1)S(1)} %get-tuple-element.5), channel_id=1, source_target_pairs={{0,8},{8,0},{16,24},{24,16},{1,9},{9,1},{17,25},{25,17},{2,10},{10... | collective-permute-start | bytes 1769480 | tf_op jit(solution)/shard_map/ppermute | solution.py:11
  78.5 11.2 %collective-permute-start.12 = (bf16[2,384,384]{2,1,0:T(8,128)(2,1)S(1)}, bf16[2,384,384]{2,1,0:T(8,128)(2,1)S(1)}, u32[]{:S(2)}, u32[]{:S(2)}) collective-permute-start(bf16[2,384,384]{2,1,0:T(8,128)(2,1)S(1)} %get-tuple-element.6), channel_id=1, source_target_pairs={{8,16},{16,8},{9,17},{17,9},{10,18},{18,10},{11,19},{19,11},{12,20... | collective-permute-start | bytes 1769480 | tf_op jit(solution)/shard_map/ppermute | solution.py:85
  91.2 6.8 %collective-permute-start.13 = (bf16[2,4,48,384]{3,2,1,0:T(8,128)(2,1)S(1)}, bf16[2,4,48,384]{3,2,1,0:T(8,128)(2,1)S(1)}, u32[]{:S(2)}, u32[]{:S(2)}) collective-permute-start(bf16[2,4,48,384]{3,2,1,0:T(8,128)(2,1)S(1)} %select_bitcast_fusion.4), channel_id=1, source_target_pairs={{0,1},{1,0},{2,3},{3,2},{4,5},{5,4},{6,7},{7,6},{8,9},{9,8},{10,11... | collective-permute-start | bytes 884744 | tf_op jit(solution)/shard_map/ppermute | solution.py:11
  98.1 5.2 %collective-permute-start.14 = (bf16[2,2,48,384]{3,2,1,0:T(8,128)(2,1)S(1)}, bf16[2,2,48,384]{3,2,1,0:T(8,128)(2,1)S(1)}, u32[]{:S(2)}, u32[]{:S(2)}) collective-permute-start(bf16[2,2,48,384]{3,2,1,0:T(8,128)(2,1)S(1)} %select_bitcast_fusion.10), channel_id=1, source_target_pairs={{0,2},{1,3},{2,0},{3,1},{4,6},{5,7},{6,4},{7,5},{8,10},{9,11},{10,... | collective-permute-start | bytes 442376 | tf_op jit(solution)/shard_map/ppermute | solution.py:11
  103.4 5.5 %collective-permute-start.15 = (bf16[2,1,48,384]{3,2,0,1:T(8,128)(2,1)S(1)}, bf16[2,1,48,384]{3,2,0,1:T(8,128)(2,1)S(1)}, u32[]{:S(2)}, u32[]{:S(2)}) collective-permute-start(bf16[2,1,48,384]{3,2,0,1:T(8,128)(2,1)S(1)} %fusion.104), channel_id=1, source_target_pairs={{0,4},{1,5},{2,6},{3,7},{4,0},{5,1},{6,2},{7,3},{8,12},{9,13},{10,... | collective-permute-start | bytes 221192 | tf_op jit(solution)/shard_map/ppermute | solution.py:11

commit v2 on v0

v2 whole, which is shorter than its diff:
```python
import functools

import jax
import jax.numpy as jnp
from jax import lax
from jax.experimental import pallas as pl
from jax.experimental.pallas import tpu as pltpu
from jax.sharding import PartitionSpec as P

ITERS = 2
LIMIT = 32 * 1024 * 1024
COST = 2000000000
VMEM = pl.BlockSpec(memory_space=pltpu.VMEM)
SMEM = pl.BlockSpec(memory_space=pltpu.SMEM)


def swap(block, axis, distance):
    route = [(i, i ^ distance) for i in range(lax.axis_size(axis))]
    return lax.ppermute(block, axis, route)


def side(axis, distance):
    return lax.rem(lax.axis_index(axis) // distance, 2)


def mirrored(index, bits):
    return sum(((index >> k) & 1) << (bits - 1 - k) for k in range(bits))


def outer_slot():
    return 1 - side("sec", 2) if lax.axis_size("sec") == 4 else 0 * lax.axis_index("sec")


def arrange_kernel(slot, own_steps, other_steps, left_own, left_other, right_own, right_other, piece, *outs):
    lefts, rights, counts, passed = outs
    pairs, size, _ = left_own.shape
    own = (side("sec", 1) == outer_slot()) == (slot == 0)
    passed[...] = piece[...]
    for term in range(2):
        moving = [jnp.where(own, own_steps[p, term], other_steps[p, term]) for p in range(pairs)]
        total = functools.reduce(lambda a, b: a + b, moving)
        counts[term] = jnp.full(counts.shape[1:], total, jnp.int32)
        ahead, behind = 0, total
        for p in range(pairs):
            place = jnp.where(moving[p] == 1, ahead, behind)
            ahead, behind = ahead + moving[p], behind + 1 - moving[p]
            columns = pl.ds(pl.multiple_of(place * size, 128), size)
            left = jnp.where(own, left_own[p], left_other[p])
            right = jnp.where(own, right_own[p], right_other[p])
            rights[term, :, columns] = right.T if term == 0 else right
            lefts[term, :, columns] = left if term == 0 else left.T


def arrange(slot, steps, lefts, rights, piece):
    pairs, size, _ = lefts[0].shape
    shape = jax.ShapeDtypeStruct((2, size, pairs * size), lefts[0].dtype)
    counts = jax.ShapeDtypeStruct((2, 8, 128), jnp.int32)
    return pl.pallas_call(
        functools.partial(arrange_kernel, slot),
        out_shape=(shape, shape, counts, jax.ShapeDtypeStruct(piece.shape, piece.dtype)),
        in_specs=[SMEM] * 2 + [VMEM] * 5,
        out_specs=(VMEM,) * 4,
        compiler_params=pltpu.CompilerParams(vmem_limit_bytes=LIMIT),
        cost_estimate=pl.CostEstimate(flops=COST, bytes_accessed=1, transcendentals=0),
        name="arrange",
    )(*steps, *lefts, *rights, piece)


def chunks(size, parts):
    rows = size // parts
    if rows % 16:
        return [(0, 0, size)]
    bits = parts.bit_length() - 1
    return [(i * rows, mirrored(i, bits) * rows, rows) for i in range(parts)]


def put(ref, value, parts):
    for natural, at, rows in chunks(value.shape[0], parts):
        ref[at : at + rows] = value[natural : natural + rows].astype(ref.dtype)


def one_term(parts, term, counts, vector, lefts, rights, middle, moved, stayed):
    size = vector.shape[0]
    pairs = middle.shape[0] // size
    movers = jnp.where(term == 0, jnp.max(counts[0]), jnp.max(counts[1]))
    step = 2 if pairs % 2 == 0 else 1
    for first in range(0, pairs, step):
        columns = slice(first * size, (first + step) * size)
        turned = jnp.dot(vector[...], rights[term, :, columns], preferred_element_type=jnp.float32)
        turned = turned.astype(middle.dtype)
        for p in range(step):
            for natural, at, rows in chunks(size, parts):
                to = (first + p) * size + natural
                middle[to : to + rows] = turned[at : at + rows, p * size : (p + 1) * size]
    for count in range(pairs + 1):

        @pl.when(movers == count)
        def _(cut=count * size):
            def total(part):
                if part.start == part.stop:
                    return None
                return jnp.dot(lefts[term, :, part], middle[part], preferred_element_type=jnp.float32)

            if moved is not None:
                moved(total(slice(0, cut)))
            stayed(total(slice(cut, pairs * size)))


def none_or(total, base):
    if total is None:
        return base
    return total if base is None else total + base


def inner_kernel(parts, with_cross, counts, vector, lefts, rights, near, stayed, *rest):
    cross, middle = rest if with_cross else (None, *rest)
    size = vector.shape[0]
    zeros = functools.partial(jnp.zeros, (size, size), jnp.float32)
    term = outer_slot()

    def set_near(total):
        near[...] = zeros() if total is None else total

    def set_stayed(total):
        stayed[...] = zeros() if total is None else total

    def set_cross(total):
        put(cross, zeros() if total is None else total, parts)

    def add_stayed(total):
        if total is not None:
            stayed[...] += total

    one_term(parts, 1 - term, counts, vector, lefts, rights, middle, set_near, set_stayed)
    one_term(
        parts, term, counts, vector, lefts, rights, middle, set_cross if with_cross else None, add_stayed
    )


def first_kernel(parts, counts, vector, lefts, rights, cross, stayed, middle):
    size = vector.shape[0]
    zeros = functools.partial(jnp.zeros, (size, size), jnp.float32)

    def set_cross(total):
        put(cross, zeros() if total is None else total, parts)

    def set_stayed(total):
        stayed[...] = zeros() if total is None else total

    one_term(parts, 1 - outer_slot(), counts, vector, lefts, rights, middle, set_cross, set_stayed)


def second_kernel(parts, counts, vector, lefts, rights, stayed, near_in, stayed_in, own, other, middle):
    def set_other(total):
        put(other, none_or(total, stayed_in[...]), parts)

    def set_own(total):
        put(own, none_or(total, stayed[...] + near_in[...]), parts)

    one_term(parts, outer_slot(), counts, vector, lefts, rights, middle, set_other, set_own)


def merge_kernel(own, arrived, other, *rest):
    more, outer, inner = rest if len(rest) == 3 else (None, *rest)
    outer[...] = (own[...] + arrived[...].astype(jnp.float32)).astype(outer.dtype)
    total = other[...]
    if more is not None:
        total = total + more[...].astype(jnp.float32)
    inner[...] = total.astype(inner.dtype)


def merge(own, arrived, other, *more):
    shape = jax.ShapeDtypeStruct(own.shape, jnp.bfloat16)
    return pl.pallas_call(
        merge_kernel,
        out_shape=(shape, shape),
        in_specs=[VMEM] * (3 + len(more)),
        out_specs=(VMEM, VMEM),
        compiler_params=pltpu.CompilerParams(vmem_limit_bytes=LIMIT),
        cost_estimate=pl.CostEstimate(flops=1, bytes_accessed=1, transcendentals=0),
        name="merge",
    )(own, arrived, other, *more)


def call(kernel, name, kinds, cost, vector, weights, *more):
    lefts, rights, counts = weights
    size, width = lefts.shape[1:]
    shapes = tuple(jax.ShapeDtypeStruct((size, size), kind) for kind in kinds)
    return pl.pallas_call(
        kernel,
        out_shape=shapes,
        in_specs=[VMEM] * (4 + len(more)),
        out_specs=(VMEM,) * len(shapes),
        scratch_shapes=[pltpu.VMEM((width, size), jnp.bfloat16)],
        compiler_params=pltpu.CompilerParams(vmem_limit_bytes=LIMIT),
        cost_estimate=pl.CostEstimate(flops=cost, bytes_accessed=1, transcendentals=0),
        name=name,
    )(counts, vector, lefts, rights, *more)


def on_device(wavefunction, diagonal, left_ops, right_ops, offsets):
    members = lax.axis_size("op")
    sectors = lax.axis_size("sec")
    bits = members.bit_length() - 1
    steps = [1 << k for k in range(bits)]
    groups, last = [steps[k : min(k + 2, bits - 1)] for k in range(0, bits - 1, 2)], steps[-1]
    sides = {d: side("op", d) for d in steps}
    shard, width = wavefunction.shape[2:]
    size = members * shard
    core = side("sec", 1)
    bf16, f32 = jnp.bfloat16, jnp.float32
    pair = sectors == 4
    mine = core == outer_slot()

    def both_slots(own, other):
        return jnp.where(mine, own, other), jnp.where(mine, other, own)

    def position(group):
        return functools.reduce(lambda a, d: 2 * a + sides[d], group, 0)

    def partners(group):
        count = 1 << len(group)
        return [(j, sum(d for k, d in enumerate(group) if j >> (len(group) - 1 - k) & 1)) for j in range(count - 1, 0, -1)]

    def scatter(block, group):
        rows = block.shape[0] >> len(group)
        place = position(group)
        sent = [lax.dynamic_slice_in_dim(block, (place ^ j) * rows, rows) for j, _ in partners(group)]
        arrived = [swap(piece, "op", distance) for piece, (_, distance) in zip(sent, partners(group))]
        total = lax.dynamic_slice_in_dim(block, place * rows, rows).astype(f32)
        for piece in arrived:
            total = total + piece.astype(f32)
        return total

    def gather(block, group, own=None):
        rows = block.shape[0]
        place = position(group)
        whole = jnp.zeros((rows << len(group), block.shape[1]), block.dtype)
        whole = lax.dynamic_update_slice_in_dim(whole, block if own is None else own, place * rows, 0)
        for j, distance in partners(group):
            whole = lax.dynamic_update_slice_in_dim(whole, swap(block, "op", distance), (place ^ j) * rows, 0)
        return whole

    def respread(block):
        if shard % 16 == 0:
            return block
        spread = block.reshape((2,) * bits + (shard, -1))
        return spread.transpose(tuple(range(bits))[::-1] + (bits, bits + 1)).reshape(block.shape)

    def gather_all(block):
        for group in groups[::-1]:
            block = gather(block, group)
        return respread(block)

    def beside(block, own=None):
        own = block if own is None else own
        arrived = swap(block, "op", last)
        low = jnp.where(sides[last] == 0, own, arrived)
        high = jnp.where(sides[last] == 0, arrived, own)
        return jnp.concatenate([low, high])

    own_roots = wavefunction[0]
    other_roots = swap(own_roots, "sec", 1)
    lefts = (left_ops, swap(left_ops, "sec", 1))
    rights = (right_ops, swap(right_ops, "sec", 1))
    moves = (offsets, swap(offsets, "sec", 1))
    own_root = jnp.where(core == 0, own_roots[0], own_roots[1])
    other_root = jnp.where(core == 0, other_roots[0], other_roots[1])
    start = jnp.concatenate(both_slots(own_root, other_root), axis=1)
    *outer_weights, passed = arrange(0, moves, lefts, rights, start)
    together = beside(start, passed)
    *inner_weights, passed = arrange(1, moves, lefts, rights, together)
    together = gather(together, groups[-1], passed)
    for group in groups[-2::-1]:
        together = gather(together, group)
    together = respread(together)
    vectors = [together[:, :width], together[:, width:]]
    own_diagonals = both_slots(diagonal[0], swap(diagonal[0], "sec", 1))
    both_diagonals = beside(jnp.concatenate(own_diagonals, axis=1))
    diagonals = [both_diagonals[:, :width], both_diagonals[:, width:]]

    for turn in range(ITERS):
        cross, stayed = call(
            functools.partial(first_kernel, members), "first", (bf16, f32), COST, vectors[0], outer_weights
        )
        kinds = (f32, f32) if pair else (f32, f32, bf16)
        inner = call(functools.partial(inner_kernel, members, not pair), "inner", kinds, COST, vectors[1], inner_weights)
        if pair:
            arrived = (swap(respread(cross), "sec", 2),)
        else:
            arrived = (
                lax.ppermute(respread(inner[2]), "sec", [(i, i + 2) for i in range(sectors - 2)]),
                lax.ppermute(respread(cross), "sec", [(i, i - 2) for i in range(2, sectors)]),
            )
        own, other = call(
            functools.partial(second_kernel, members),
            "second",
            (f32, f32),
            COST,
            vectors[0],
            outer_weights,
            stayed,
            inner[0],
            inner[1],
        )
        blocks = list(merge(respread(own), arrived[0], respread(other), *arrived[1:]))
        for k in range(2):
            block = blocks[k]
            for group in groups:
                block = scatter(block, group).astype(bf16)
            if turn < ITERS - 1:
                total = block.astype(f32) + swap(block, "op", last).astype(f32)
                vectors[k] = gather_all((total / diagonals[k]).astype(bf16))
            else:
                blocks[k] = (scatter(block, [last]) / own_diagonals[k]).astype(bf16)
    kept = jnp.where(mine, blocks[0], blocks[1])
    returned = swap(jnp.where(mine, blocks[1], blocks[0]), "sec", 1)
    out = jnp.where(core == 0, jnp.stack([kept, returned]), jnp.stack([returned, kept]))
    return out[None]


def solution(mesh):
    in_specs = (
        P("sec", None, "op", None),
        P("sec", "op", None),
        P(("sec", "op"), None, None),
        P(("sec", "op"), None, None),
        P(("sec", "op"), None),
    )
    out_specs = P("sec", None, "op", None)
    return jax.shard_map(
        on_device, mesh=mesh, in_specs=in_specs, out_specs=out_specs, check_vma=False
    )
```

time: 177 us -> 95.6 us (0.54)
  blocking collectives: 148 us -> 0 us
  starting transfers between devices: 5.17 us -> 43.3 us
  waiting for transfers between devices: 5.45 us -> 29.2 us
  Pallas kernels: 0 us -> 15.9 us
  matrix products: 15.2 us -> 0 us
  local copies, waits for them, and re-layouts: 0.42 us -> 3.77 us
    all_to_all x2 -> x0, blocking collectives: 82.8 us -> none  [on_device(): lax.all_to_all(shaped, 'op', split_axis=2, concat_axis=2, tiled=True)]
    all_gather x2 -> x0, blocking collectives: 65.4 us -> none  [on_device(): rows_block = lax.all_gather(trial_vec, 'op', axis=2, tiled=True)[0]]
    ppermute x4 -> x35, starting transfers between devices: 5.17 us -> 43.3 us  [swap(): return lax.ppermute(block, axis, route)]
    ppermute x4 -> x35, waiting for transfers between devices: 5.45 us -> 29.2 us  [swap(): return lax.ppermute(block, axis, route)]
    pallas_call x0 -> x10, Pallas kernels: none -> 15.9 us  [the longest x6 12.2 us: call(): pl.pallas_call(kernel, out_shape=shapes, in_specs=[VMEM] * (4 + len(more)...]
    dot_general x12 -> x0, matrix products: 15.2 us -> none  [the longest x2 2.84 us: on_device(): jnp.einsum('xab,pcb->pxac', rows_block, right_ops, preferred_element_type...]
    unnamed x8 -> x5, local copies, waits for them, and re-layouts: 0.02 us -> 3.3 us
    select_n x0 -> x6, other arithmetic: none -> 2.4 us  [the longest x2 1.7 us: both_slots(): return (jnp.where(mine, own, other), jnp.where(mine, other, own))]
  transfers between devices with their start and end apart: 4 -> 35, of which waited for: 2 -> 14; matrix products, arithmetic and copies ran while one was open for 0% -> 3% of each run, Pallas kernels for 0% -> 15%
where the time goes in v2:
time: 95.6 us; the launch traced here: 95.3 us
  starting transfers between devices  43.3 us (45%)
  waiting for transfers between devices  29.2 us (31%)
  Pallas kernels  15.9 us (17%)
  local copies, waits for them, and re-layouts  3.77 us (4%)
  other arithmetic  2.76 us (3%)
    ppermute x35, starting transfers between devices, swap(): return lax.ppermute(block, axis, route)  43.3 us
    ppermute x35, waiting for transfers between devices, swap(): return lax.ppermute(block, axis, route)  29.2 us
    pallas_call x6, Pallas kernels, call(): pl.pallas_call(kernel, out_shape=shapes, in_specs=[VMEM] * (4 + len(more)...  12.2 us
    pallas_call x2, Pallas kernels, arrange(): pl.pallas_call(functools.partial(arrange_kernel, slot), out_shape=(shape,...  3.5 us
    unnamed x5, local copies, waits for them, and re-layouts  3.3 us
  transfers between devices with their start and end apart: 35, of which 14 were waited for; matrix products, arithmetic and copies ran while one was open for 3% of the time, Pallas kernels for 15%

profile of v2, /device:TPU:0, one launch (start us, length us, event | category | flops | bytes accessed | tf_op | source)
XLA Modules:
  0.0 95.3 jit_solution(18065055948360439577)
XLA Ops:
  2.2 2.7 %collective-permute-done.13 = f32[48,384]{1,0:T(8,128)S(1)} collective-permute-done((f32[48,384]{1,0:T(8,128)}, f32[48,384]{1,0:T(8,128)S(1)}, u32[]{:S(2)}, u32[]{:S(2)}) %collective-permute-start.13) | collective-permute-done | bytes 73760 | tf_op jit(solution)/shard_map/ppermute | solution.py:19
  5.9 4.0 %collective-permute-start.14 = (f32[48,768]{1,0:T(8,128)S(1)}, f32[48,768]{1,0:T(8,128)S(1)}, u32[]{:S(2)}, u32[]{:S(2)}) collective-permute-start(f32[48,768]{1,0:T(8,128)S(1)} %pad_maximum_fusion.2), channel_id=1, source_target_pairs={{0,4},{1,5},{2,6},{3,7},{4,0},{5,1},{6,2},{7,3},{8,12},{9,13},{10,... | collective-permute-start | bytes 442376 | tf_op jit(solution)/shard_map/ppermute | solution.py:19
  10.8 8.5 %collective-permute-done.14 = f32[48,768]{1,0:T(8,128)S(1)} collective-permute-done((f32[48,768]{1,0:T(8,128)S(1)}, f32[48,768]{1,0:T(8,128)S(1)}, u32[]{:S(2)}, u32[]{:S(2)}) %collective-permute-start.14) | collective-permute-done | bytes 147488 | tf_op jit(solution)/shard_map/ppermute | solution.py:19
  20.6 1.3 %copy-done.1 = bf16[4,384,384]{2,1,0:T(8,128)(2,1)S(1)} copy-done((bf16[4,384,384]{2,1,0:T(8,128)(2,1)S(1)}, bf16[4,384,384]{2,1,0:T(8,128)(2,1)}, u32[]{:S(2)}) %copy-start.1) | copy-done | bytes 1179672
  21.9 1.7 %arrange.2 = (bf16[2,384,1536]{2,1,0:T(8,128)(2,1)S(1)}, bf16[2,384,1536]{2,1,0:T(8,128)(2,1)S(1)}, s32[2,8,128]{2,1,0:T(8,128)S(1)}, bf16[48,768]{1,0:T(8,128)(2,1)S(1)}) custom-call(s32[4,2]{1,0:T(4,128)S(1)} %copy.7.own_steps, s32[4,2]{1,0:T(4,128)S(1)} %collective-permute-done.other_steps, bf16[4,384,384]{2,1,0:T(8,128)(2,1)S(1)} %copy-done, ...), custom_call_target="tpu_custom_call" | custom-call | flops 2000000000 | bytes 1 | tf_op jit(solution)/shard_map/arrange/pallas_call | solution.py:58
  23.7 1.3 %collective-permute-start.5 = (bf16[96,768]{1,0:T(8,128)(2,1)S(1)}, bf16[96,768]{1,0:T(8,128)(2,1)S(1)}, u32[]{:S(2)}, u32[]{:S(2)}) collective-permute-start(bf16[96,768]{1,0:T(8,128)(2,1)S(1)} %pad_maximum_fusion.1.piece), channel_id=1, source_target_pairs={{0,3},{1,2},{2,1},{3,0},{4,7},{5,6},{6,5},{7,4},{8,11},{9,10},{10,... | collective-permute-start | bytes 442376 | tf_op jit(solution)/shard_map/ppermute | solution.py:19
  25.7 1.6 %collective-permute-start.7 = (bf16[96,768]{1,0:T(8,128)(2,1)S(1)}, bf16[96,768]{1,0:T(8,128)(2,1)S(1)}, u32[]{:S(2)}, u32[]{:S(2)}) collective-permute-start(bf16[96,768]{1,0:T(8,128)(2,1)S(1)} %pad_maximum_fusion.1.piece), channel_id=1, source_target_pairs={{0,2},{1,3},{2,0},{3,1},{4,6},{5,7},{6,4},{7,5},{8,10},{9,11},{10,... | collective-permute-start | bytes 442376 | tf_op jit(solution)/shard_map/ppermute | solution.py:19
  27.2 1.7 %arrange.3 = (bf16[2,384,1536]{2,1,0:T(8,128)(2,1)S(1)}, bf16[2,384,1536]{2,1,0:T(8,128)(2,1)S(1)}, s32[2,8,128]{2,1,0:T(8,128)S(1)}, bf16[96,768]{1,0:T(8,128)(2,1)S(1)}) custom-call(s32[4,2]{1,0:T(4,128)S(1)} %copy.7.own_steps, s32[4,2]{1,0:T(4,128)S(1)} %collective-permute-done.other_steps, bf16[4,384,384]{2,1,0:T(8,128)(2,1)S(1)} %copy-done, ...), custom_call_target="tpu_custom_call" | custom-call | flops 2000000000 | bytes 1 | tf_op jit(solution)/shard_map/arrange/pallas_call | solution.py:58
  29.1 2.1 %collective-permute-done.5 = bf16[96,768]{1,0:T(8,128)(2,1)S(1)} collective-permute-done((bf16[96,768]{1,0:T(8,128)(2,1)S(1)}, bf16[96,768]{1,0:T(8,128)(2,1)S(1)}, u32[]{:S(2)}, u32[]{:S(2)}) %collective-permute-start.5) | collective-permute-done | bytes 147488 | tf_op jit(solution)/shard_map/ppermute | solution.py:19
  31.1 1.6 %collective-permute-done.6 = bf16[96,768]{1,0:T(8,128)(2,1)S(1)} collective-permute-done((bf16[96,768]{1,0:T(8,128)(2,1)S(1)}, bf16[96,768]{1,0:T(8,128)(2,1)S(1)}, u32[]{:S(2)}, u32[]{:S(2)}) %collective-permute-start.6) | collective-permute-done | bytes 147488 | tf_op jit(solution)/shard_map/ppermute | solution.py:19
  32.8 1.6 %first.2 = (bf16[384,384]{1,0:T(8,128)(2,1)S(1)}, f32[384,384]{1,0:T(8,128)S(1)}) custom-call(s32[2,8,128]{2,1,0:T(8,128)S(1)} %get-tuple-element.29.counts, bf16[384,384]{1,0:T(8,128)(2,1)S(1)} %get-tuple-element.61.vector, bf16[2,384,1536]{2,1,0:T(8,128)(2,1)S(1)} %get-tuple-element.32.lefts, bf16[2,384,1536]{2,1,0:T(8,128)(2,1)S(1)} %get-tuple-element.33.rights), custom_call_target="tpu_custom_call" | custom-call | flops 2000000000 | bytes 1 | tf_op jit(solution)/shard_map/first/pallas_call | solution.py:189
  34.4 1.3 %collective-permute-start.8 = (bf16[384,384]{1,0:T(8,128)(2,1)S(1)}, bf16[384,384]{1,0:T(8,128)(2,1)S(1)}, u32[]{:S(2)}, u32[]{:S(2)}) collective-permute-start(bf16[384,384]{1,0:T(8,128)(2,1)S(1)} %get-tuple-element.41), channel_id=1, source_target_pairs={{0,16},{8,24},{16,0},{24,8},{1,17},{9,25},{17,1},{25,9},{2,18},{10... | collective-permute-start | bytes 884744 | tf_op jit(solution)/shard_map/ppermute | solution.py:19
  35.7 2.7 %inner.2 = (f32[384,384]{1,0:T(8,128)S(1)}, f32[384,384]{1,0:T(8,128)S(1)}) custom-call(s32[2,8,128]{2,1,0:T(8,128)S(1)} %get-tuple-element.35.counts, bf16[384,384]{1,0:T(8,128)(2,1)S(1)} %get-tuple-element.60.vector, bf16[2,384,1536]{2,1,0:T(8,128)(2,1)S(1)} %get-tuple-element.36.lefts, bf16[2,384,1536]{2,1,0:T(8,128)(2,1)S(1)} %get-tuple-element.37.rights), custom_call_target="tpu_custom_call" | custom-call | flops 2000000000 | bytes 1 | tf_op jit(solution)/shard_map/inner/pallas_call | solution.py:189
  38.5 1.8 %second.2 = (f32[384,384]{1,0:T(8,128)S(1)}, f32[384,384]{1,0:T(8,128)S(1)}) custom-call(s32[2,8,128]{2,1,0:T(8,128)S(1)} %get-tuple-element.29.counts, bf16[384,384]{1,0:T(8,128)(2,1)S(1)} %get-tuple-element.61.vector, bf16[2,384,1536]{2,1,0:T(8,128)(2,1)S(1)} %get-tuple-element.32.lefts, bf16[2,384,1536]{2,1,0:T(8,128)(2,1)S(1)} %get-tuple-element.33.rights, ...), custom_call_target="tpu_custom_call" | custom-call | flops 2000000000 | bytes 1 | tf_op jit(solution)/shard_map/second/pallas_call | solution.py:189
  40.2 3.0 %collective-permute-done.8.arrived = bf16[384,384]{1,0:T(8,128)(2,1)S(1)} collective-permute-done((bf16[384,384]{1,0:T(8,128)(2,1)S(1)}, bf16[384,384]{1,0:T(8,128)(2,1)S(1)}, u32[]{:S(2)}, u32[]{:S(2)}) %collective-permute-start.8) | collective-permute-done | bytes 294944 | tf_op jit(solution)/shard_map/ppermute | solution.py:19
  43.3 1.5 %collective-permute-start.10 = (bf16[96,384]{1,0:T(8,128)(2,1)S(1)}, bf16[96,384]{1,0:T(8,128)(2,1)S(1)}, u32[]{:S(2)}, u32[]{:S(2)}) collective-permute-start(bf16[96,384]{1,0:T(8,128)(2,1)S(1)} %get-tuple-element.73), channel_id=1, source_target_pairs={{0,1},{1,0},{2,3},{3,2},{4,5},{5,4},{6,7},{7,6},{8,9},{9,8},{10,11... | collective-permute-start | bytes 221192 | tf_op jit(solution)/shard_map/ppermute | solution.py:19
  45.6 1.3 %collective-permute-start.9 = (bf16[96,384]{1,0:T(8,128)(2,1)S(1)}, bf16[96,384]{1,0:T(8,128)(2,1)S(1)}, u32[]{:S(2)}, u32[]{:S(2)}) collective-permute-start(bf16[96,384]{1,0:T(8,128)(2,1)S(1)} %get-tuple-element.71), channel_id=1, source_target_pairs={{0,3},{1,2},{2,1},{3,0},{4,7},{5,6},{6,5},{7,4},{8,11},{9,10},{10,... | collective-permute-start | bytes 221192 | tf_op jit(solution)/shard_map/ppermute | solution.py:19
  46.9 1.7 %collective-permute-start.18 = (bf16[96,384]{1,0:T(8,128)(2,1)S(1)}, bf16[96,384]{1,0:T(8,128)(2,1)S(1)}, u32[]{:S(2)}, u32[]{:S(2)}) collective-permute-start(bf16[96,384]{1,0:T(8,128)(2,1)S(1)} %get-tuple-element.68), channel_id=1, source_target_pairs={{0,3},{1,2},{2,1},{3,0},{4,7},{5,6},{6,5},{7,4},{8,11},{9,10},{10,... | collective-permute-start | bytes 221192 | tf_op jit(solution)/shard_map/ppermute | solution.py:19
  51.6 2.8 %collective-permute-start.12 = (bf16[96,384]{1,0:T(8,128)(2,1)S(1)}, bf16[96,384]{1,0:T(8,128)(2,1)S(1)}, u32[]{:S(2)}, u32[]{:S(2)}) collective-permute-start(bf16[96,384]{1,0:T(8,128)(2,1)S(1)} %add_convert_fusion.3), channel_id=1, source_target_pairs={{0,4},{1,5},{2,6},{3,7},{4,0},{5,1},{6,2},{7,3},{8,12},{9,13},{10,... | collective-permute-start | bytes 221192 | tf_op jit(solution)/shard_map/ppermute | solution.py:19
  54.5 2.6 %collective-permute-start.21 = (bf16[96,384]{1,0:T(8,128)(2,1)S(1)}, bf16[96,384]{1,0:T(8,128)(2,1)S(1)}, u32[]{:S(2)}, u32[]{:S(2)}) collective-permute-start(bf16[96,384]{1,0:T(8,128)(2,1)S(1)} %add_convert_fusion.2), channel_id=1, source_target_pairs={{0,4},{1,5},{2,6},{3,7},{4,0},{5,1},{6,2},{7,3},{8,12},{9,13},{10,... | collective-permute-start | bytes 221192 | tf_op jit(solution)/shard_map/ppermute | solution.py:19
  57.1 1.4 %collective-permute-done.12 = bf16[96,384]{1,0:T(8,128)(2,1)S(1)} collective-permute-done((bf16[96,384]{1,0:T(8,128)(2,1)S(1)}, bf16[96,384]{1,0:T(8,128)(2,1)S(1)}, u32[]{:S(2)}, u32[]{:S(2)}) %collective-permute-start.12) | collective-permute-done | bytes 73760 | tf_op jit(solution)/shard_map/ppermute | solution.py:19
  62.7 1.5 %collective-permute-start.24 = (bf16[96,384]{1,0:T(8,128)(2,1)S(1)}, bf16[96,384]{1,0:T(8,128)(2,1)S(1)}, u32[]{:S(2)}, u32[]{:S(2)}) collective-permute-start(bf16[96,384]{1,0:T(8,128)(2,1)S(1)} %get-tuple-element.57), channel_id=1, source_target_pairs={{0,2},{1,3},{2,0},{3,1},{4,6},{5,7},{6,4},{7,5},{8,10},{9,11},{10,... | collective-permute-start | bytes 221192 | tf_op jit(solution)/shard_map/ppermute | solution.py:19
  65.9 2.7 %collective-permute-done.16 = bf16[96,384]{1,0:T(8,128)(2,1)S(1)} collective-permute-done((bf16[96,384]{1,0:T(8,128)(2,1)S(1)}, bf16[96,384]{1,0:T(8,128)(2,1)S(1)}, u32[]{:S(2)}, u32[]{:S(2)}) %collective-permute-start.16) | collective-permute-done | bytes 73760 | tf_op jit(solution)/shard_map/ppermute | solution.py:19
  69.6 1.6 %first.3 = (bf16[384,384]{1,0:T(8,128)(2,1)S(1)}, f32[384,384]{1,0:T(8,128)S(1)}) custom-call(s32[2,8,128]{2,1,0:T(8,128)S(1)} %get-tuple-element.29.counts, bf16[384,384]{1,0:T(8,128)(2,1)S(1)} %constant_dynamic-update-slice_fusion.4.vector, bf16[2,384,1536]{2,1,0:T(8,128)(2,1)S(1)} %get-tuple-element.32.lefts, ...), custom_call_target="tpu_custom_call" | custom-call | flops 2000000000 | bytes 1 | tf_op jit(solution)/shard_map/first/pallas_call | solution.py:189
  71.2 1.4 %collective-permute-start.25 = (bf16[384,384]{1,0:T(8,128)(2,1)S(1)}, bf16[384,384]{1,0:T(8,128)(2,1)S(1)}, u32[]{:S(2)}, u32[]{:S(2)}) collective-permute-start(bf16[384,384]{1,0:T(8,128)(2,1)S(1)} %get-tuple-element.49), channel_id=1, source_target_pairs={{0,16},{8,24},{16,0},{24,8},{1,17},{9,25},{17,1},{25,9},{2,18},{10... | collective-permute-start | bytes 884744 | tf_op jit(solution)/shard_map/ppermute | solution.py:19
  72.7 3.0 %inner.3 = (f32[384,384]{1,0:T(8,128)S(1)}, f32[384,384]{1,0:T(8,128)S(1)}) custom-call(s32[2,8,128]{2,1,0:T(8,128)S(1)} %get-tuple-element.35.counts, bf16[384,384]{1,0:T(8,128)(2,1)S(1)} %constant_dynamic-update-slice_fusion.vector, bf16[2,384,1536]{2,1,0:T(8,128)(2,1)S(1)} %get-tuple-element.36.lefts, bf16[2,384,1536]{2,1,0:T(8,128)(2,1)S(1)} %get-tuple-element.37.rights), custom_call_target="tpu_custom_call" | custom-call | flops 2000000000 | bytes 1 | tf_op jit(solution)/shard_map/inner/pallas_call | solution.py:189
  75.7 1.6 %second.3 = (f32[384,384]{1,0:T(8,128)S(1)}, f32[384,384]{1,0:T(8,128)S(1)}) custom-call(s32[2,8,128]{2,1,0:T(8,128)S(1)} %get-tuple-element.29.counts, bf16[384,384]{1,0:T(8,128)(2,1)S(1)} %constant_dynamic-update-slice_fusion.4.vector, bf16[2,384,1536]{2,1,0:T(8,128)(2,1)S(1)} %get-tuple-element.32.lefts, ...), custom_call_target="tpu_custom_call" | custom-call | flops 2000000000 | bytes 1 | tf_op jit(solution)/shard_map/second/pallas_call | solution.py:189
  80.3 1.4 %collective-permute-start.32 = (bf16[96,384]{1,0:T(8,128)(2,1)S(1)}, bf16[96,384]{1,0:T(8,128)(2,1)S(1)}, u32[]{:S(2)}, u32[]{:S(2)}) collective-permute-start(bf16[96,384]{1,0:T(8,128)(2,1)S(1)} %get-tuple-element.63), channel_id=1, source_target_pairs={{0,2},{1,3},{2,0},{3,1},{4,6},{5,7},{6,4},{7,5},{8,10},{9,11},{10,... | collective-permute-start | bytes 221192 | tf_op jit(solution)/shard_map/ppermute | solution.py:19
  83.9 1.4 %collective-permute-start.28 = (bf16[96,384]{1,0:T(8,128)(2,1)S(1)}, bf16[96,384]{1,0:T(8,128)(2,1)S(1)}, u32[]{:S(2)}, u32[]{:S(2)}) collective-permute-start(bf16[96,384]{1,0:T(8,128)(2,1)S(1)} %get-tuple-element.66), channel_id=1, source_target_pairs={{0,2},{1,3},{2,0},{3,1},{4,6},{5,7},{6,4},{7,5},{8,10},{9,11},{10,... | collective-permute-start | bytes 221192 | tf_op jit(solution)/shard_map/ppermute | solution.py:19
  85.4 2.6 %collective-permute-start.33 = (bf16[48,384]{1,0:T(8,128)(2,1)S(1)}, bf16[48,384]{1,0:T(8,128)(2,1)S(1)}, u32[]{:S(2)}, u32[]{:S(2)}) collective-permute-start(bf16[48,384]{1,0:T(8,128)(2,1)S(1)} %constant_dynamic-slice_fusion), channel_id=1, source_target_pairs={{0,4},{1,5},{2,6},{3,7},{4,0},{5,1},{6,2},{7,3},{8,12},{9,13},{10,... | collective-permute-start | bytes 110600 | tf_op jit(solution)/shard_map/ppermute | solution.py:19
  88.3 3.1 %collective-permute-start.29 = (bf16[48,384]{1,0:T(8,128)(2,1)S(1)}, bf16[48,384]{1,0:T(8,128)(2,1)S(1)}, u32[]{:S(2)}, u32[]{:S(2)}) collective-permute-start(bf16[48,384]{1,0:T(8,128)(2,1)S(1)} %constant_dynamic-slice_fusion.4), channel_id=1, source_target_pairs={{0,4},{1,5},{2,6},{3,7},{4,0},{5,1},{6,2},{7,3},{8,12},{9,13},{10,... | collective-permute-start | bytes 110600 | tf_op jit(solution)/shard_map/ppermute | solution.py:19
  91.4 1.9 %collective-permute-done.29 = bf16[48,384]{1,0:T(8,128)(2,1)S(1)} collective-permute-done((bf16[48,384]{1,0:T(8,128)(2,1)S(1)}, bf16[48,384]{1,0:T(8,128)(2,1)S(1)}, u32[]{:S(2)}, u32[]{:S(2)}) %collective-permute-start.29) | collective-permute-done | bytes 36896 | tf_op jit(solution)/shard_map/ppermute | solution.py:19
  (89 shorter events, 24.5 us)
Async XLA Ops:
  0.0 19.3 %collective-permute-start.1 = (bf16[4,384,384]{2,1,0:T(8,128)(2,1)}, bf16[4,384,384]{2,1,0:T(8,128)(2,1)S(1)}, u32[]{:S(2)}, u32[]{:S(2)}) collective-permute-start(bf16[4,384,384]{2,1,0:T(8,128)(2,1)} %left_own.3), channel_id=1, source_target_pairs={{0,8},{8,0},{16,24},{24,16},{1,9},{9,1},{17,25},{25,17},{2,10},{10... | collective-permute-start | bytes 3538952 | tf_op jit(solution)/shard_map/ppermute | solution.py:19
  0.5 18.8 %collective-permute-start.2 = (bf16[4,384,384]{2,1,0:T(8,128)(2,1)}, bf16[4,384,384]{2,1,0:T(8,128)(2,1)S(1)}, u32[]{:S(2)}, u32[]{:S(2)}) collective-permute-start(bf16[4,384,384]{2,1,0:T(8,128)(2,1)} %right_own.3), channel_id=1, source_target_pairs={{0,8},{8,0},{16,24},{24,16},{1,9},{9,1},{17,25},{25,17},{2,10},{10... | collective-permute-start | bytes 3538952 | tf_op jit(solution)/shard_map/ppermute | solution.py:19
  0.5 4.4 %collective-permute-start.13 = (f32[48,384]{1,0:T(8,128)}, f32[48,384]{1,0:T(8,128)S(1)}, u32[]{:S(2)}, u32[]{:S(2)}) collective-permute-start(f32[48,384]{1,0:T(8,128)} %bitcast.17), channel_id=1, source_target_pairs={{0,8},{8,0},{16,24},{24,16},{1,9},{9,1},{17,25},{25,17},{2,10},{10... | collective-permute-start | bytes 221192 | tf_op jit(solution)/shard_map/ppermute | solution.py:19
  1.0 8.9 %collective-permute-start.3 = (bf16[2,48,384]{2,1,0:T(8,128)(2,1)}, bf16[2,48,384]{2,1,0:T(8,128)(2,1)S(1)}, u32[]{:S(2)}, u32[]{:S(2)}) collective-permute-start(bf16[2,48,384]{2,1,0:T(8,128)(2,1)} %bitcast.16), channel_id=1, source_target_pairs={{0,8},{8,0},{16,24},{24,16},{1,9},{9,1},{17,25},{25,17},{2,10},{10... | collective-permute-start | bytes 221192 | tf_op jit(solution)/shard_map/ppermute | solution.py:19
  1.8 17.5 %collective-permute-start = (s32[4,2]{1,0:T(4,128)S(1)}, s32[4,2]{1,0:T(4,128)S(1)}, u32[]{:S(2)}, u32[]{:S(2)}) collective-permute-start(s32[4,2]{1,0:T(4,128)S(1)} %copy.7.own_steps), channel_id=1, source_target_pairs={{0,8},{8,0},{16,24},{24,16},{1,9},{9,1},{17,25},{25,17},{2,10},{10... | collective-permute-start | bytes 104 | tf_op jit(solution)/shard_map/ppermute | solution.py:19
  5.9 13.4 %collective-permute-start.14 = (f32[48,768]{1,0:T(8,128)S(1)}, f32[48,768]{1,0:T(8,128)S(1)}, u32[]{:S(2)}, u32[]{:S(2)}) collective-permute-start(f32[48,768]{1,0:T(8,128)S(1)} %pad_maximum_fusion.2), channel_id=1, source_target_pairs={{0,4},{1,5},{2,6},{3,7},{4,0},{5,1},{6,2},{7,3},{8,12},{9,13},{10,... | collective-permute-start | bytes 442376 | tf_op jit(solution)/shard_map/ppermute | solution.py:19
  10.7 12.9 %collective-permute-start.4 = (bf16[48,768]{1,0:T(8,128)(2,1)S(1)}, bf16[48,768]{1,0:T(8,128)(2,1)S(1)}, u32[]{:S(2)}, u32[]{:S(2)}) collective-permute-start(bf16[48,768]{1,0:T(8,128)(2,1)S(1)} %pad_maximum_fusion.3.piece), channel_id=1, source_target_pairs={{0,4},{1,5},{2,6},{3,7},{4,0},{5,1},{6,2},{7,3},{8,12},{9,13},{10,... | collective-permute-start | bytes 221192 | tf_op jit(solution)/shard_map/ppermute | solution.py:19
  23.7 7.5 %collective-permute-start.5 = (bf16[96,768]{1,0:T(8,128)(2,1)S(1)}, bf16[96,768]{1,0:T(8,128)(2,1)S(1)}, u32[]{:S(2)}, u32[]{:S(2)}) collective-permute-start(bf16[96,768]{1,0:T(8,128)(2,1)S(1)} %pad_maximum_fusion.1.piece), channel_id=1, source_target_pairs={{0,3},{1,2},{2,1},{3,0},{4,7},{5,6},{6,5},{7,4},{8,11},{9,10},{10,... | collective-permute-start | bytes 442376 | tf_op jit(solution)/shard_map/ppermute | solution.py:19
  25.0 7.7 %collective-permute-start.6 = (bf16[96,768]{1,0:T(8,128)(2,1)S(1)}, bf16[96,768]{1,0:T(8,128)(2,1)S(1)}, u32[]{:S(2)}, u32[]{:S(2)}) collective-permute-start(bf16[96,768]{1,0:T(8,128)(2,1)S(1)} %pad_maximum_fusion.1.piece), channel_id=1, source_target_pairs={{0,1},{1,0},{2,3},{3,2},{4,5},{5,4},{6,7},{7,6},{8,9},{9,8},{10,11... | collective-permute-start | bytes 442376 | tf_op jit(solution)/shard_map/ppermute | solution.py:19
  25.7 7.0 %collective-permute-start.7 = (bf16[96,768]{1,0:T(8,128)(2,1)S(1)}, bf16[96,768]{1,0:T(8,128)(2,1)S(1)}, u32[]{:S(2)}, u32[]{:S(2)}) collective-permute-start(bf16[96,768]{1,0:T(8,128)(2,1)S(1)} %pad_maximum_fusion.1.piece), channel_id=1, source_target_pairs={{0,2},{1,3},{2,0},{3,1},{4,6},{5,7},{6,4},{7,5},{8,10},{9,11},{10,... | collective-permute-start | bytes 442376 | tf_op jit(solution)/shard_map/ppermute | solution.py:19
  34.4 8.8 %collective-permute-start.8 = (bf16[384,384]{1,0:T(8,128)(2,1)S(1)}, bf16[384,384]{1,0:T(8,128)(2,1)S(1)}, u32[]{:S(2)}, u32[]{:S(2)}) collective-permute-start(bf16[384,384]{1,0:T(8,128)(2,1)S(1)} %get-tuple-element.41), channel_id=1, source_target_pairs={{0,16},{8,24},{16,0},{24,8},{1,17},{9,25},{17,1},{25,9},{2,18},{10... | collective-permute-start | bytes 884744 | tf_op jit(solution)/shard_map/ppermute | solution.py:19
  43.3 5.9 %collective-permute-start.10 = (bf16[96,384]{1,0:T(8,128)(2,1)S(1)}, bf16[96,384]{1,0:T(8,128)(2,1)S(1)}, u32[]{:S(2)}, u32[]{:S(2)}) collective-permute-start(bf16[96,384]{1,0:T(8,128)(2,1)S(1)} %get-tuple-element.73), channel_id=1, source_target_pairs={{0,1},{1,0},{2,3},{3,2},{4,5},{5,4},{6,7},{7,6},{8,9},{9,8},{10,11... | collective-permute-start | bytes 221192 | tf_op jit(solution)/shard_map/ppermute | solution.py:19
  44.8 5.7 %collective-permute-start.11 = (bf16[96,384]{1,0:T(8,128)(2,1)S(1)}, bf16[96,384]{1,0:T(8,128)(2,1)S(1)}, u32[]{:S(2)}, u32[]{:S(2)}) collective-permute-start(bf16[96,384]{1,0:T(8,128)(2,1)S(1)} %get-tuple-element.72), channel_id=1, source_target_pairs={{0,2},{1,3},{2,0},{3,1},{4,6},{5,7},{6,4},{7,5},{8,10},{9,11},{10,... | collective-permute-start | bytes 221192 | tf_op jit(solution)/shard_map/ppermute | solution.py:19
  45.6 6.0 %collective-permute-start.9 = (bf16[96,384]{1,0:T(8,128)(2,1)S(1)}, bf16[96,384]{1,0:T(8,128)(2,1)S(1)}, u32[]{:S(2)}, u32[]{:S(2)}) collective-permute-start(bf16[96,384]{1,0:T(8,128)(2,1)S(1)} %get-tuple-element.71), channel_id=1, source_target_pairs={{0,3},{1,2},{2,1},{3,0},{4,7},{5,6},{6,5},{7,4},{8,11},{9,10},{10,... | collective-permute-start | bytes 221192 | tf_op jit(solution)/shard_map/ppermute | solution.py:19
  46.9 7.6 %collective-permute-start.18 = (bf16[96,384]{1,0:T(8,128)(2,1)S(1)}, bf16[96,384]{1,0:T(8,128)(2,1)S(1)}, u32[]{:S(2)}, u32[]{:S(2)}) collective-permute-start(bf16[96,384]{1,0:T(8,128)(2,1)S(1)} %get-tuple-element.68), channel_id=1, source_target_pairs={{0,3},{1,2},{2,1},{3,0},{4,7},{5,6},{6,5},{7,4},{8,11},{9,10},{10,... | collective-permute-start | bytes 221192 | tf_op jit(solution)/shard_map/ppermute | solution.py:19
  48.6 5.9 %collective-permute-start.19 = (bf16[96,384]{1,0:T(8,128)(2,1)S(1)}, bf16[96,384]{1,0:T(8,128)(2,1)S(1)}, u32[]{:S(2)}, u32[]{:S(2)}) collective-permute-start(bf16[96,384]{1,0:T(8,128)(2,1)S(1)} %get-tuple-element.70), channel_id=1, source_target_pairs={{0,1},{1,0},{2,3},{3,2},{4,5},{5,4},{6,7},{7,6},{8,9},{9,8},{10,11... | collective-permute-start | bytes 221192 | tf_op jit(solution)/shard_map/ppermute | solution.py:19
  49.3 5.2 %collective-permute-start.20 = (bf16[96,384]{1,0:T(8,128)(2,1)S(1)}, bf16[96,384]{1,0:T(8,128)(2,1)S(1)}, u32[]{:S(2)}, u32[]{:S(2)}) collective-permute-start(bf16[96,384]{1,0:T(8,128)(2,1)S(1)} %get-tuple-element.69), channel_id=1, source_target_pairs={{0,2},{1,3},{2,0},{3,1},{4,6},{5,7},{6,4},{7,5},{8,10},{9,11},{10,... | collective-permute-start | bytes 221192 | tf_op jit(solution)/shard_map/ppermute | solution.py:19
  51.6 7.0 %collective-permute-start.12 = (bf16[96,384]{1,0:T(8,128)(2,1)S(1)}, bf16[96,384]{1,0:T(8,128)(2,1)S(1)}, u32[]{:S(2)}, u32[]{:S(2)}) collective-permute-start(bf16[96,384]{1,0:T(8,128)(2,1)S(1)} %add_convert_fusion.3), channel_id=1, source_target_pairs={{0,4},{1,5},{2,6},{3,7},{4,0},{5,1},{6,2},{7,3},{8,12},{9,13},{10,... | collective-permute-start | bytes 221192 | tf_op jit(solution)/shard_map/ppermute | solution.py:19
  54.5 6.1 %collective-permute-start.21 = (bf16[96,384]{1,0:T(8,128)(2,1)S(1)}, bf16[96,384]{1,0:T(8,128)(2,1)S(1)}, u32[]{:S(2)}, u32[]{:S(2)}) collective-permute-start(bf16[96,384]{1,0:T(8,128)(2,1)S(1)} %add_convert_fusion.2), channel_id=1, source_target_pairs={{0,4},{1,5},{2,6},{3,7},{4,0},{5,1},{6,2},{7,3},{8,12},{9,13},{10,... | collective-permute-start | bytes 221192 | tf_op jit(solution)/shard_map/ppermute | solution.py:19
  58.7 6.6 %collective-permute-start.15 = (bf16[96,384]{1,0:T(8,128)(2,1)S(1)}, bf16[96,384]{1,0:T(8,128)(2,1)S(1)}, u32[]{:S(2)}, u32[]{:S(2)}) collective-permute-start(bf16[96,384]{1,0:T(8,128)(2,1)S(1)} %get-tuple-element.59), channel_id=1, source_target_pairs={{0,3},{1,2},{2,1},{3,0},{4,7},{5,6},{6,5},{7,4},{8,11},{9,10},{10,... | collective-permute-start | bytes 221192 | tf_op jit(solution)/shard_map/ppermute | solution.py:19
  60.7 11.9 %collective-permute-start.22 = (bf16[96,384]{1,0:T(8,128)(2,1)S(1)}, bf16[96,384]{1,0:T(8,128)(2,1)S(1)}, u32[]{:S(2)}, u32[]{:S(2)}) collective-permute-start(bf16[96,384]{1,0:T(8,128)(2,1)S(1)} %get-tuple-element.57), channel_id=1, source_target_pairs={{0,3},{1,2},{2,1},{3,0},{4,7},{5,6},{6,5},{7,4},{8,11},{9,10},{10,... | collective-permute-start | bytes 221192 | tf_op jit(solution)/shard_map/ppermute | solution.py:19
  61.8 10.8 %collective-permute-start.23 = (bf16[96,384]{1,0:T(8,128)(2,1)S(1)}, bf16[96,384]{1,0:T(8,128)(2,1)S(1)}, u32[]{:S(2)}, u32[]{:S(2)}) collective-permute-start(bf16[96,384]{1,0:T(8,128)(2,1)S(1)} %get-tuple-element.57), channel_id=1, source_target_pairs={{0,1},{1,0},{2,3},{3,2},{4,5},{5,4},{6,7},{7,6},{8,9},{9,8},{10,11... | collective-permute-start | bytes 221192 | tf_op jit(solution)/shard_map/ppermute | solution.py:19
  62.7 9.9 %collective-permute-start.24 = (bf16[96,384]{1,0:T(8,128)(2,1)S(1)}, bf16[96,384]{1,0:T(8,128)(2,1)S(1)}, u32[]{:S(2)}, u32[]{:S(2)}) collective-permute-start(bf16[96,384]{1,0:T(8,128)(2,1)S(1)} %get-tuple-element.57), channel_id=1, source_target_pairs={{0,2},{1,3},{2,0},{3,1},{4,6},{5,7},{6,4},{7,5},{8,10},{9,11},{10,... | collective-permute-start | bytes 221192 | tf_op jit(solution)/shard_map/ppermute | solution.py:19
  65.3 4.4 %collective-permute-start.17 = (bf16[96,384]{1,0:T(8,128)(2,1)S(1)}, bf16[96,384]{1,0:T(8,128)(2,1)S(1)}, u32[]{:S(2)}, u32[]{:S(2)}) collective-permute-start(bf16[96,384]{1,0:T(8,128)(2,1)S(1)} %get-tuple-element.59), channel_id=1, source_target_pairs={{0,2},{1,3},{2,0},{3,1},{4,6},{5,7},{6,4},{7,5},{8,10},{9,11},{10,... | collective-permute-start | bytes 221192 | tf_op jit(solution)/shard_map/ppermute | solution.py:19
  71.2 6.8 %collective-permute-start.25 = (bf16[384,384]{1,0:T(8,128)(2,1)S(1)}, bf16[384,384]{1,0:T(8,128)(2,1)S(1)}, u32[]{:S(2)}, u32[]{:S(2)}) collective-permute-start(bf16[384,384]{1,0:T(8,128)(2,1)S(1)} %get-tuple-element.49), channel_id=1, source_target_pairs={{0,16},{8,24},{16,0},{24,8},{1,17},{9,25},{17,1},{25,9},{2,18},{10... | collective-permute-start | bytes 884744 | tf_op jit(solution)/shard_map/ppermute | solution.py:19
  78.1 5.7 %collective-permute-start.30 = (bf16[96,384]{1,0:T(8,128)(2,1)S(1)}, bf16[96,384]{1,0:T(8,128)(2,1)S(1)}, u32[]{:S(2)}, u32[]{:S(2)}) collective-permute-start(bf16[96,384]{1,0:T(8,128)(2,1)S(1)} %get-tuple-element.62), channel_id=1, source_target_pairs={{0,3},{1,2},{2,1},{3,0},{4,7},{5,6},{6,5},{7,4},{8,11},{9,10},{10,... | collective-permute-start | bytes 221192 | tf_op jit(solution)/shard_map/ppermute | solution.py:19
  79.2 6.0 %collective-permute-start.31 = (bf16[96,384]{1,0:T(8,128)(2,1)S(1)}, bf16[96,384]{1,0:T(8,128)(2,1)S(1)}, u32[]{:S(2)}, u32[]{:S(2)}) collective-permute-start(bf16[96,384]{1,0:T(8,128)(2,1)S(1)} %get-tuple-element.64), channel_id=1, source_target_pairs={{0,1},{1,0},{2,3},{3,2},{4,5},{5,4},{6,7},{7,6},{8,9},{9,8},{10,11... | collective-permute-start | bytes 221192 | tf_op jit(solution)/shard_map/ppermute | solution.py:19
  80.3 5.0 %collective-permute-start.32 = (bf16[96,384]{1,0:T(8,128)(2,1)S(1)}, bf16[96,384]{1,0:T(8,128)(2,1)S(1)}, u32[]{:S(2)}, u32[]{:S(2)}) collective-permute-start(bf16[96,384]{1,0:T(8,128)(2,1)S(1)} %get-tuple-element.63), channel_id=1, source_target_pairs={{0,2},{1,3},{2,0},{3,1},{4,6},{5,7},{6,4},{7,5},{8,10},{9,11},{10,... | collective-permute-start | bytes 221192 | tf_op jit(solution)/shard_map/ppermute | solution.py:19
  81.7 6.3 %collective-permute-start.26 = (bf16[96,384]{1,0:T(8,128)(2,1)S(1)}, bf16[96,384]{1,0:T(8,128)(2,1)S(1)}, u32[]{:S(2)}, u32[]{:S(2)}) collective-permute-start(bf16[96,384]{1,0:T(8,128)(2,1)S(1)} %get-tuple-element.65), channel_id=1, source_target_pairs={{0,3},{1,2},{2,1},{3,0},{4,7},{5,6},{6,5},{7,4},{8,11},{9,10},{10,... | collective-permute-start | bytes 221192 | tf_op jit(solution)/shard_map/ppermute | solution.py:19
  82.8 5.2 %collective-permute-start.27 = (bf16[96,384]{1,0:T(8,128)(2,1)S(1)}, bf16[96,384]{1,0:T(8,128)(2,1)S(1)}, u32[]{:S(2)}, u32[]{:S(2)}) collective-permute-start(bf16[96,384]{1,0:T(8,128)(2,1)S(1)} %get-tuple-element.67), channel_id=1, source_target_pairs={{0,1},{1,0},{2,3},{3,2},{4,5},{5,4},{6,7},{7,6},{8,9},{9,8},{10,11... | collective-permute-start | bytes 221192 | tf_op jit(solution)/shard_map/ppermute | solution.py:19
  85.4 6.0 %collective-permute-start.33 = (bf16[48,384]{1,0:T(8,128)(2,1)S(1)}, bf16[48,384]{1,0:T(8,128)(2,1)S(1)}, u32[]{:S(2)}, u32[]{:S(2)}) collective-permute-start(bf16[48,384]{1,0:T(8,128)(2,1)S(1)} %constant_dynamic-slice_fusion), channel_id=1, source_target_pairs={{0,4},{1,5},{2,6},{3,7},{4,0},{5,1},{6,2},{7,3},{8,12},{9,13},{10,... | collective-permute-start | bytes 110600 | tf_op jit(solution)/shard_map/ppermute | solution.py:19
  88.3 5.0 %collective-permute-start.29 = (bf16[48,384]{1,0:T(8,128)(2,1)S(1)}, bf16[48,384]{1,0:T(8,128)(2,1)S(1)}, u32[]{:S(2)}, u32[]{:S(2)}) collective-permute-start(bf16[48,384]{1,0:T(8,128)(2,1)S(1)} %constant_dynamic-slice_fusion.4), channel_id=1, source_target_pairs={{0,4},{1,5},{2,6},{3,7},{4,0},{5,1},{6,2},{7,3},{8,12},{9,13},{10,... | collective-permute-start | bytes 110600 | tf_op jit(solution)/shard_map/ppermute | solution.py:19
  (5 other events, 12.5 us)

commit v3 on v2

--- a/solution.py
+++ b/solution.py
@@ -9,7 +9,7 @@
 
 ITERS = 2
 LIMIT = 32 * 1024 * 1024
-COST = 2000000000
+COST = 5 * 10**9
 VMEM = pl.BlockSpec(memory_space=pltpu.VMEM)
 SMEM = pl.BlockSpec(memory_space=pltpu.SMEM)
 
@@ -31,11 +31,17 @@
     return 1 - side("sec", 2) if lax.axis_size("sec") == 4 else 0 * lax.axis_index("sec")
 
 
-def arrange_kernel(slot, own_steps, other_steps, left_own, left_other, right_own, right_other, piece, *outs):
-    lefts, rights, counts, passed = outs
+def arrange_kernel(slot, own_steps, other_steps, left_own, left_other, right_own, right_other, *rest):
+    *pieces, lefts, rights, counts, passed = rest
     pairs, size, _ = left_own.shape
-    own = (side("sec", 1) == outer_slot()) == (slot == 0)
-    passed[...] = piece[...]
+    own_first = side("sec", 1) == outer_slot()
+    own = own_first == (slot == 0)
+    if len(pieces) == 1:
+        passed[...] = pieces[0][...]
+    else:
+        width = pieces[0].shape[1]
+        passed[:, :width] = jnp.where(own_first, pieces[0][...], pieces[1][...])
+        passed[:, width:] = jnp.where(own_first, pieces[1][...], pieces[0][...])
     for term in range(2):
         moving = [jnp.where(own, own_steps[p, term], other_steps[p, term]) for p in range(pairs)]
         total = functools.reduce(lambda a, b: a + b, moving)
@@ -51,19 +57,20 @@
             lefts[term, :, columns] = left if term == 0 else left.T
 
 
-def arrange(slot, steps, lefts, rights, piece):
+def arrange(slot, steps, lefts, rights, *pieces):
     pairs, size, _ = lefts[0].shape
+    rows, width = pieces[0].shape
     shape = jax.ShapeDtypeStruct((2, size, pairs * size), lefts[0].dtype)
     counts = jax.ShapeDtypeStruct((2, 8, 128), jnp.int32)
     return pl.pallas_call(
         functools.partial(arrange_kernel, slot),
-        out_shape=(shape, shape, counts, jax.ShapeDtypeStruct(piece.shape, piece.dtype)),
-        in_specs=[SMEM] * 2 + [VMEM] * 5,
+        out_shape=(shape, shape, counts, jax.ShapeDtypeStruct((rows, width * len(pieces)), pieces[0].dtype)),
+        in_specs=[SMEM] * 2 + [VMEM] * (4 + len(pieces)),
         out_specs=(VMEM,) * 4,
         compiler_params=pltpu.CompilerParams(vmem_limit_bytes=LIMIT),
         cost_estimate=pl.CostEstimate(flops=COST, bytes_accessed=1, transcendentals=0),
         name="arrange",
-    )(*steps, *lefts, *rights, piece)
+    )(*steps, *lefts, *rights, *pieces)
 
 
 def chunks(size, parts):
@@ -261,22 +268,20 @@
 
     own_roots = wavefunction[0]
     other_roots = swap(own_roots, "sec", 1)
-    lefts = (left_ops, swap(left_ops, "sec", 1))
-    rights = (right_ops, swap(right_ops, "sec", 1))
-    moves = (offsets, swap(offsets, "sec", 1))
     own_root = jnp.where(core == 0, own_roots[0], own_roots[1])
     other_root = jnp.where(core == 0, other_roots[0], other_roots[1])
     start = jnp.concatenate(both_slots(own_root, other_root), axis=1)
+    start, left_given, right_given = lax.optimization_barrier((start, left_ops, right_ops))
+    lefts = (left_ops, swap(left_given, "sec", 1))
+    rights = (right_ops, swap(right_given, "sec", 1))
+    moves = (offsets, swap(offsets, "sec", 1))
     *outer_weights, passed = arrange(0, moves, lefts, rights, start)
     together = beside(start, passed)
-    *inner_weights, passed = arrange(1, moves, lefts, rights, together)
-    together = gather(together, groups[-1], passed)
-    for group in groups[-2::-1]:
-        together = gather(together, group)
-    together = respread(together)
-    vectors = [together[:, :width], together[:, width:]]
-    own_diagonals = both_slots(diagonal[0], swap(diagonal[0], "sec", 1))
-    both_diagonals = beside(jnp.concatenate(own_diagonals, axis=1))
+    vectors = [gather_all(together[:, :width]), gather_all(together[:, width:])]
+    own_diagonal = diagonal[0]
+    *inner_weights, slots = arrange(1, moves, lefts, rights, own_diagonal, swap(own_diagonal, "sec", 1))
+    both_diagonals = beside(slots)
+    own_diagonals = [slots[:, :width], slots[:, width:]]
     diagonals = [both_diagonals[:, :width], both_diagonals[:, width:]]
 
     for turn in range(ITERS):
@@ -304,7 +309,7 @@
             inner[1],
         )
         blocks = list(merge(respread(own), arrived[0], respread(other), *arrived[1:]))
-        for k in range(2):
+        for k in (0, 1):
             block = blocks[k]
             for group in groups:
                 block = scatter(block, group).astype(bf16)

time: 95.6 us -> 86.6 us (0.906)
  waiting for transfers between devices: 29.2 us -> 15.1 us
  starting transfers between devices: 43.3 us -> 49.9 us
    ppermute x35 -> x38, waiting for transfers between devices: 29.2 us -> 15.1 us  [swap(): return lax.ppermute(block, axis, route)]
    ppermute x35 -> x38, starting transfers between devices: 43.3 us -> 49.9 us  [swap(): return lax.ppermute(block, axis, route)]
    unnamed x5 -> x7, local copies, waits for them, and re-layouts: 3.3 us -> 3.3 us
  transfers between devices with their start and end apart: 35 -> 38, of which waited for: 14 -> 15; matrix products, arithmetic and copies ran while one was open for 3% -> 2% of each run, Pallas kernels for 15% -> 15%
where the time goes in v3:
time: 86.6 us; the launch traced here: 86.2 us
  starting transfers between devices  49.9 us (58%)
  Pallas kernels  15.2 us (18%)
  waiting for transfers between devices  15.1 us (17%)
  local copies, waits for them, and re-layouts  3.77 us (4%)
  other arithmetic  1.91 us (2%)
    ppermute x38, starting transfers between devices, swap(): return lax.ppermute(block, axis, route)  49.9 us
    ppermute x38, waiting for transfers between devices, swap(): return lax.ppermute(block, axis, route)  15.1 us
    pallas_call x6, Pallas kernels, call(): pl.pallas_call(kernel, out_shape=shapes, in_specs=[VMEM] * (4 + len(more)...  11.6 us
    pallas_call x2, Pallas kernels, arrange(): pl.pallas_call(functools.partial(arrange_kernel, slot), out_shape=(shape,...  3.49 us
    unnamed x7, local copies, waits for them, and re-layouts  3.3 us
  transfers between devices with their start and end apart: 38, of which 15 were waited for; matrix products, arithmetic and copies ran while one was open for 2% of the time, Pallas kernels for 15%

profile of v3, /device:TPU:0, one launch (start us, length us, event | category | flops | bytes accessed | tf_op | source)
XLA Modules:
  0.0 86.2 jit_solution(120401168383511771)
XLA Ops:
  4.3 3.9 %collective-permute-start.4 = (bf16[48,768]{1,0:T(8,128)(2,1)S(1)}, bf16[48,768]{1,0:T(8,128)(2,1)S(1)}, u32[]{:S(2)}, u32[]{:S(2)}) collective-permute-start(bf16[48,768]{1,0:T(8,128)(2,1)S(1)} %pad_maximum_fusion.2.rest_0_), channel_id=1, source_target_pairs={{0,4},{1,5},{2,6},{3,7},{4,0},{5,1},{6,2},{7,3},{8,12},{9,13},{10,... | collective-permute-start | bytes 221192 | tf_op jit(solution)/shard_map/ppermute | solution.py:19
  8.2 1.3 %copy-done = bf16[4,384,384]{2,1,0:T(8,128)(2,1)S(1)} copy-done((bf16[4,384,384]{2,1,0:T(8,128)(2,1)S(1)}, bf16[4,384,384]{2,1,0:T(8,128)(2,1)}, u32[]{:S(2)}) %copy-start) | copy-done | bytes 1179672
  9.5 1.3 %copy-done.1 = bf16[4,384,384]{2,1,0:T(8,128)(2,1)S(1)} copy-done((bf16[4,384,384]{2,1,0:T(8,128)(2,1)S(1)}, bf16[4,384,384]{2,1,0:T(8,128)(2,1)}, u32[]{:S(2)}) %copy-start.1) | copy-done | bytes 1179672
  10.7 1.7 %arrange.2 = (bf16[2,384,1536]{2,1,0:T(8,128)(2,1)S(1)}, bf16[2,384,1536]{2,1,0:T(8,128)(2,1)S(1)}, s32[2,8,128]{2,1,0:T(8,128)S(1)}, bf16[48,768]{1,0:T(8,128)(2,1)S(1)}) custom-call(s32[4,2]{1,0:T(4,128)S(1)} %copy.7.own_steps, s32[4,2]{1,0:T(4,128)S(1)} %collective-permute-done.other_steps, bf16[4,384,384]{2,1,0:T(8,128)(2,1)S(1)} %copy-done, ...), custom_call_target="tpu_custom_call" | custom-call | flops 5000000000 | bytes 1 | tf_op jit(solution)/shard_map/arrange/pallas_call | solution.py:65
  12.6 2.9 %collective-permute-start.9 = (bf16[96,384]{1,0:T(8,128)(2,1)S(1)}, bf16[96,384]{1,0:T(8,128)(2,1)S(1)}, u32[]{:S(2)}, u32[]{:S(2)}) collective-permute-start(bf16[96,384]{1,0:T(8,128)(2,1)S(1)} %get-tuple-element.67), channel_id=1, source_target_pairs={{0,3},{1,2},{2,1},{3,0},{4,7},{5,6},{6,5},{7,4},{8,11},{9,10},{10,... | collective-permute-start | bytes 221192 | tf_op jit(solution)/shard_map/ppermute | solution.py:19
  16.2 2.9 %collective-permute-start.5 = (bf16[96,384]{1,0:T(8,128)(2,1)S(1)}, bf16[96,384]{1,0:T(8,128)(2,1)S(1)}, u32[]{:S(2)}, u32[]{:S(2)}) collective-permute-start(bf16[96,384]{1,0:T(8,128)(2,1)S(1)} %get-tuple-element.69), channel_id=1, source_target_pairs={{0,3},{1,2},{2,1},{3,0},{4,7},{5,6},{6,5},{7,4},{8,11},{9,10},{10,... | collective-permute-start | bytes 221192 | tf_op jit(solution)/shard_map/ppermute | solution.py:19
  19.7 1.7 %arrange.3 = (bf16[2,384,1536]{2,1,0:T(8,128)(2,1)S(1)}, bf16[2,384,1536]{2,1,0:T(8,128)(2,1)S(1)}, s32[2,8,128]{2,1,0:T(8,128)S(1)}, f32[48,768]{1,0:T(8,128)S(1)}) custom-call(s32[4,2]{1,0:T(4,128)S(1)} %copy.7.own_steps, s32[4,2]{1,0:T(4,128)S(1)} %collective-permute-done.other_steps, bf16[4,384,384]{2,1,0:T(8,128)(2,1)S(1)} %copy-done, ...), custom_call_target="tpu_custom_call" | custom-call | flops 5000000000 | bytes 1 | tf_op jit(solution)/shard_map/arrange/pallas_call | solution.py:65
  23.6 2.7 %collective-permute-start.17 = (f32[48,768]{1,0:T(8,128)S(1)}, f32[48,768]{1,0:T(8,128)S(1)}, u32[]{:S(2)}, u32[]{:S(2)}) collective-permute-start(f32[48,768]{1,0:T(8,128)S(1)} %get-tuple-element.49), channel_id=1, source_target_pairs={{0,4},{1,5},{2,6},{3,7},{4,0},{5,1},{6,2},{7,3},{8,12},{9,13},{10,... | collective-permute-start | bytes 442376 | tf_op jit(solution)/shard_map/ppermute | solution.py:19
  26.2 1.7 %collective-permute-done.7 = bf16[96,384]{1,0:T(8,128)(2,1)S(1)} collective-permute-done((bf16[96,384]{1,0:T(8,128)(2,1)S(1)}, bf16[96,384]{1,0:T(8,128)(2,1)S(1)}, u32[]{:S(2)}, u32[]{:S(2)}) %collective-permute-start.7) | collective-permute-done | bytes 73760 | tf_op jit(solution)/shard_map/ppermute | solution.py:19
  27.9 1.6 %first.2 = (bf16[384,384]{1,0:T(8,128)(2,1)S(1)}, f32[384,384]{1,0:T(8,128)S(1)}) custom-call(s32[2,8,128]{2,1,0:T(8,128)S(1)} %get-tuple-element.35.counts, bf16[384,384]{1,0:T(8,128)(2,1)S(1)} %constant_dynamic-update-slice_fusion.12.vector, bf16[2,384,1536]{2,1,0:T(8,128)(2,1)S(1)} %get-tuple-element.37.lefts, ...), custom_call_target="tpu_custom_call" | custom-call | flops 5000000000 | bytes 1 | tf_op jit(solution)/shard_map/first/pallas_call | solution.py:196
  29.6 1.6 %collective-permute-start.12 = (bf16[384,384]{1,0:T(8,128)(2,1)S(1)}, bf16[384,384]{1,0:T(8,128)(2,1)S(1)}, u32[]{:S(2)}, u32[]{:S(2)}) collective-permute-start(bf16[384,384]{1,0:T(8,128)(2,1)S(1)} %get-tuple-element.46), channel_id=1, source_target_pairs={{0,16},{8,24},{16,0},{24,8},{1,17},{9,25},{17,1},{25,9},{2,18},{10... | collective-permute-start | bytes 884744 | tf_op jit(solution)/shard_map/ppermute | solution.py:19
  31.3 2.4 %inner.2 = (f32[384,384]{1,0:T(8,128)S(1)}, f32[384,384]{1,0:T(8,128)S(1)}) custom-call(s32[2,8,128]{2,1,0:T(8,128)S(1)} %get-tuple-element.40.counts, bf16[384,384]{1,0:T(8,128)(2,1)S(1)} %constant_dynamic-update-slice_fusion.8.vector, bf16[2,384,1536]{2,1,0:T(8,128)(2,1)S(1)} %get-tuple-element.41.lefts, bf16[2,384,1536]{2,1,0:T(8,128)(2,1)S(1)} %get-tuple-element.42.rights), custom_call_target="tpu_custom_call" | custom-call | flops 5000000000 | bytes 1 | tf_op jit(solution)/shard_map/inner/pallas_call | solution.py:196
  33.6 1.8 %second.2 = (f32[384,384]{1,0:T(8,128)S(1)}, f32[384,384]{1,0:T(8,128)S(1)}) custom-call(s32[2,8,128]{2,1,0:T(8,128)S(1)} %get-tuple-element.35.counts, bf16[384,384]{1,0:T(8,128)(2,1)S(1)} %constant_dynamic-update-slice_fusion.12.vector, bf16[2,384,1536]{2,1,0:T(8,128)(2,1)S(1)} %get-tuple-element.37.lefts, ...), custom_call_target="tpu_custom_call" | custom-call | flops 5000000000 | bytes 1 | tf_op jit(solution)/shard_map/second/pallas_call | solution.py:196
  36.5 1.2 %collective-permute-start.21 = (bf16[96,384]{1,0:T(8,128)(2,1)S(1)}, bf16[96,384]{1,0:T(8,128)(2,1)S(1)}, u32[]{:S(2)}, u32[]{:S(2)}) collective-permute-start(bf16[96,384]{1,0:T(8,128)(2,1)S(1)} %get-tuple-element.76), channel_id=1, source_target_pairs={{0,3},{1,2},{2,1},{3,0},{4,7},{5,6},{6,5},{7,4},{8,11},{9,10},{10,... | collective-permute-start | bytes 221192 | tf_op jit(solution)/shard_map/ppermute | solution.py:19
  38.7 1.4 %collective-permute-start.23 = (bf16[96,384]{1,0:T(8,128)(2,1)S(1)}, bf16[96,384]{1,0:T(8,128)(2,1)S(1)}, u32[]{:S(2)}, u32[]{:S(2)}) collective-permute-start(bf16[96,384]{1,0:T(8,128)(2,1)S(1)} %get-tuple-element.77), channel_id=1, source_target_pairs={{0,2},{1,3},{2,0},{3,1},{4,6},{5,7},{6,4},{7,5},{8,10},{9,11},{10,... | collective-permute-start | bytes 221192 | tf_op jit(solution)/shard_map/ppermute | solution.py:19
  40.1 1.2 %collective-permute-start.13 = (bf16[96,384]{1,0:T(8,128)(2,1)S(1)}, bf16[96,384]{1,0:T(8,128)(2,1)S(1)}, u32[]{:S(2)}, u32[]{:S(2)}) collective-permute-start(bf16[96,384]{1,0:T(8,128)(2,1)S(1)} %get-tuple-element.79), channel_id=1, source_target_pairs={{0,3},{1,2},{2,1},{3,0},{4,7},{5,6},{6,5},{7,4},{8,11},{9,10},{10,... | collective-permute-start | bytes 221192 | tf_op jit(solution)/shard_map/ppermute | solution.py:19
  43.7 2.1 %collective-permute-start.24 = (bf16[96,384]{1,0:T(8,128)(2,1)S(1)}, bf16[96,384]{1,0:T(8,128)(2,1)S(1)}, u32[]{:S(2)}, u32[]{:S(2)}) collective-permute-start(bf16[96,384]{1,0:T(8,128)(2,1)S(1)} %add_convert_fusion.2), channel_id=1, source_target_pairs={{0,4},{1,5},{2,6},{3,7},{4,0},{5,1},{6,2},{7,3},{8,12},{9,13},{10,... | collective-permute-start | bytes 221192 | tf_op jit(solution)/shard_map/ppermute | solution.py:19
  47.1 2.2 %collective-permute-start.16 = (bf16[96,384]{1,0:T(8,128)(2,1)S(1)}, bf16[96,384]{1,0:T(8,128)(2,1)S(1)}, u32[]{:S(2)}, u32[]{:S(2)}) collective-permute-start(bf16[96,384]{1,0:T(8,128)(2,1)S(1)} %add_convert_fusion.3), channel_id=1, source_target_pairs={{0,4},{1,5},{2,6},{3,7},{4,0},{5,1},{6,2},{7,3},{8,12},{9,13},{10,... | collective-permute-start | bytes 221192 | tf_op jit(solution)/shard_map/ppermute | solution.py:19
  49.5 1.8 %collective-permute-start.25 = (bf16[96,384]{1,0:T(8,128)(2,1)S(1)}, bf16[96,384]{1,0:T(8,128)(2,1)S(1)}, u32[]{:S(2)}, u32[]{:S(2)}) collective-permute-start(bf16[96,384]{1,0:T(8,128)(2,1)S(1)} %get-tuple-element.63), channel_id=1, source_target_pairs={{0,3},{1,2},{2,1},{3,0},{4,7},{5,6},{6,5},{7,4},{8,11},{9,10},{10,... | collective-permute-start | bytes 221192 | tf_op jit(solution)/shard_map/ppermute | solution.py:19
  53.1 1.8 %collective-permute-start.18 = (bf16[96,384]{1,0:T(8,128)(2,1)S(1)}, bf16[96,384]{1,0:T(8,128)(2,1)S(1)}, u32[]{:S(2)}, u32[]{:S(2)}) collective-permute-start(bf16[96,384]{1,0:T(8,128)(2,1)S(1)} %get-tuple-element.65), channel_id=1, source_target_pairs={{0,3},{1,2},{2,1},{3,0},{4,7},{5,6},{6,5},{7,4},{8,11},{9,10},{10,... | collective-permute-start | bytes 221192 | tf_op jit(solution)/shard_map/ppermute | solution.py:19
  56.8 2.4 %inner.3 = (f32[384,384]{1,0:T(8,128)S(1)}, f32[384,384]{1,0:T(8,128)S(1)}) custom-call(s32[2,8,128]{2,1,0:T(8,128)S(1)} %get-tuple-element.40.counts, bf16[384,384]{1,0:T(8,128)(2,1)S(1)} %constant_dynamic-update-slice_fusion.vector, bf16[2,384,1536]{2,1,0:T(8,128)(2,1)S(1)} %get-tuple-element.41.lefts, bf16[2,384,1536]{2,1,0:T(8,128)(2,1)S(1)} %get-tuple-element.42.rights), custom_call_target="tpu_custom_call" | custom-call | flops 5000000000 | bytes 1 | tf_op jit(solution)/shard_map/inner/pallas_call | solution.py:196
  60.5 1.9 %first.3 = (bf16[384,384]{1,0:T(8,128)(2,1)S(1)}, f32[384,384]{1,0:T(8,128)S(1)}) custom-call(s32[2,8,128]{2,1,0:T(8,128)S(1)} %get-tuple-element.35.counts, bf16[384,384]{1,0:T(8,128)(2,1)S(1)} %constant_dynamic-update-slice_fusion.4.vector, bf16[2,384,1536]{2,1,0:T(8,128)(2,1)S(1)} %get-tuple-element.37.lefts, ...), custom_call_target="tpu_custom_call" | custom-call | flops 5000000000 | bytes 1 | tf_op jit(solution)/shard_map/first/pallas_call | solution.py:196
  62.4 1.9 %collective-permute-start.28 = (bf16[384,384]{1,0:T(8,128)(2,1)S(1)}, bf16[384,384]{1,0:T(8,128)(2,1)S(1)}, u32[]{:S(2)}, u32[]{:S(2)}) collective-permute-start(bf16[384,384]{1,0:T(8,128)(2,1)S(1)} %get-tuple-element.55), channel_id=1, source_target_pairs={{0,16},{8,24},{16,0},{24,8},{1,17},{9,25},{17,1},{25,9},{2,18},{10... | collective-permute-start | bytes 884744 | tf_op jit(solution)/shard_map/ppermute | solution.py:19
  64.2 1.6 %second.3 = (f32[384,384]{1,0:T(8,128)S(1)}, f32[384,384]{1,0:T(8,128)S(1)}) custom-call(s32[2,8,128]{2,1,0:T(8,128)S(1)} %get-tuple-element.35.counts, bf16[384,384]{1,0:T(8,128)(2,1)S(1)} %constant_dynamic-update-slice_fusion.4.vector, bf16[2,384,1536]{2,1,0:T(8,128)(2,1)S(1)} %get-tuple-element.37.lefts, ...), custom_call_target="tpu_custom_call" | custom-call | flops 5000000000 | bytes 1 | tf_op jit(solution)/shard_map/second/pallas_call | solution.py:196
  65.8 3.4 %collective-permute-done.28.arrived = bf16[384,384]{1,0:T(8,128)(2,1)S(1)} collective-permute-done((bf16[384,384]{1,0:T(8,128)(2,1)S(1)}, bf16[384,384]{1,0:T(8,128)(2,1)S(1)}, u32[]{:S(2)}, u32[]{:S(2)}) %collective-permute-start.28) | collective-permute-done | bytes 294944 | tf_op jit(solution)/shard_map/ppermute | solution.py:19
  69.3 1.4 %collective-permute-start.33 = (bf16[96,384]{1,0:T(8,128)(2,1)S(1)}, bf16[96,384]{1,0:T(8,128)(2,1)S(1)}, u32[]{:S(2)}, u32[]{:S(2)}) collective-permute-start(bf16[96,384]{1,0:T(8,128)(2,1)S(1)} %get-tuple-element.70), channel_id=1, source_target_pairs={{0,3},{1,2},{2,1},{3,0},{4,7},{5,6},{6,5},{7,4},{8,11},{9,10},{10,... | collective-permute-start | bytes 221192 | tf_op jit(solution)/shard_map/ppermute | solution.py:19
  71.3 1.5 %collective-permute-start.35 = (bf16[96,384]{1,0:T(8,128)(2,1)S(1)}, bf16[96,384]{1,0:T(8,128)(2,1)S(1)}, u32[]{:S(2)}, u32[]{:S(2)}) collective-permute-start(bf16[96,384]{1,0:T(8,128)(2,1)S(1)} %get-tuple-element.71), channel_id=1, source_target_pairs={{0,2},{1,3},{2,0},{3,1},{4,6},{5,7},{6,4},{7,5},{8,10},{9,11},{10,... | collective-permute-start | bytes 221192 | tf_op jit(solution)/shard_map/ppermute | solution.py:19
  72.9 1.4 %collective-permute-start.29 = (bf16[96,384]{1,0:T(8,128)(2,1)S(1)}, bf16[96,384]{1,0:T(8,128)(2,1)S(1)}, u32[]{:S(2)}, u32[]{:S(2)}) collective-permute-start(bf16[96,384]{1,0:T(8,128)(2,1)S(1)} %get-tuple-element.73), channel_id=1, source_target_pairs={{0,3},{1,2},{2,1},{3,0},{4,7},{5,6},{6,5},{7,4},{8,11},{9,10},{10,... | collective-permute-start | bytes 221192 | tf_op jit(solution)/shard_map/ppermute | solution.py:19
  74.9 1.5 %collective-permute-start.31 = (bf16[96,384]{1,0:T(8,128)(2,1)S(1)}, bf16[96,384]{1,0:T(8,128)(2,1)S(1)}, u32[]{:S(2)}, u32[]{:S(2)}) collective-permute-start(bf16[96,384]{1,0:T(8,128)(2,1)S(1)} %get-tuple-element.74), channel_id=1, source_target_pairs={{0,2},{1,3},{2,0},{3,1},{4,6},{5,7},{6,4},{7,5},{8,10},{9,11},{10,... | collective-permute-start | bytes 221192 | tf_op jit(solution)/shard_map/ppermute | solution.py:19
  76.5 2.2 %collective-permute-start.36 = (bf16[48,384]{1,0:T(8,128)(2,1)S(1)}, bf16[48,384]{1,0:T(8,128)(2,1)S(1)}, u32[]{:S(2)}, u32[]{:S(2)}) collective-permute-start(bf16[48,384]{1,0:T(8,128)(2,1)S(1)} %constant_dynamic-slice_fusion), channel_id=1, source_target_pairs={{0,4},{1,5},{2,6},{3,7},{4,0},{5,1},{6,2},{7,3},{8,12},{9,13},{10,... | collective-permute-start | bytes 110600 | tf_op jit(solution)/shard_map/ppermute | solution.py:19
  79.3 2.5 %collective-permute-start.32 = (bf16[48,384]{1,0:T(8,128)(2,1)S(1)}, bf16[48,384]{1,0:T(8,128)(2,1)S(1)}, u32[]{:S(2)}, u32[]{:S(2)}) collective-permute-start(bf16[48,384]{1,0:T(8,128)(2,1)S(1)} %constant_dynamic-slice_fusion.4), channel_id=1, source_target_pairs={{0,4},{1,5},{2,6},{3,7},{4,0},{5,1},{6,2},{7,3},{8,12},{9,13},{10,... | collective-permute-start | bytes 110600 | tf_op jit(solution)/shard_map/ppermute | solution.py:19
  81.8 2.4 %collective-permute-done.32 = bf16[48,384]{1,0:T(8,128)(2,1)S(1)} collective-permute-done((bf16[48,384]{1,0:T(8,128)(2,1)S(1)}, bf16[48,384]{1,0:T(8,128)(2,1)S(1)}, u32[]{:S(2)}, u32[]{:S(2)}) %collective-permute-start.32) | collective-permute-done | bytes 36896 | tf_op jit(solution)/shard_map/ppermute | solution.py:19
  (98 shorter events, 22.6 us)
Async XLA Ops:
  2.4 5.8 %collective-permute-start.2 = (bf16[4,384,384]{2,1,0:T(8,128)(2,1)}, bf16[4,384,384]{2,1,0:T(8,128)(2,1)S(1)}, u32[]{:S(2)}, u32[]{:S(2)}) collective-permute-start(bf16[4,384,384]{2,1,0:T(8,128)(2,1)} %left_own.3), channel_id=1, source_target_pairs={{0,8},{8,0},{16,24},{24,16},{1,9},{9,1},{17,25},{25,17},{2,10},{10... | collective-permute-start | bytes 3538952 | tf_op jit(solution)/shard_map/ppermute | solution.py:19
  2.8 5.4 %collective-permute-start.3 = (bf16[4,384,384]{2,1,0:T(8,128)(2,1)}, bf16[4,384,384]{2,1,0:T(8,128)(2,1)S(1)}, u32[]{:S(2)}, u32[]{:S(2)}) collective-permute-start(bf16[4,384,384]{2,1,0:T(8,128)(2,1)} %right_own.3), channel_id=1, source_target_pairs={{0,8},{8,0},{16,24},{24,16},{1,9},{9,1},{17,25},{25,17},{2,10},{10... | collective-permute-start | bytes 3538952 | tf_op jit(solution)/shard_map/ppermute | solution.py:19
  3.7 4.5 %collective-permute-start = (s32[4,2]{1,0:T(4,128)S(1)}, s32[4,2]{1,0:T(4,128)S(1)}, u32[]{:S(2)}, u32[]{:S(2)}) collective-permute-start(s32[4,2]{1,0:T(4,128)S(1)} %copy.7.own_steps), channel_id=1, source_target_pairs={{0,8},{8,0},{16,24},{24,16},{1,9},{9,1},{17,25},{25,17},{2,10},{10... | collective-permute-start | bytes 104 | tf_op jit(solution)/shard_map/ppermute | solution.py:19
  4.1 15.1 %collective-permute-start.8 = (f32[48,384]{1,0:T(8,128)}, f32[48,384]{1,0:T(8,128)S(1)}, u32[]{:S(2)}, u32[]{:S(2)}) collective-permute-start(f32[48,384]{1,0:T(8,128)} %bitcast.14), channel_id=1, source_target_pairs={{0,8},{8,0},{16,24},{24,16},{1,9},{9,1},{17,25},{25,17},{2,10},{10... | collective-permute-start | bytes 221192 | tf_op jit(solution)/shard_map/ppermute | solution.py:19
  4.3 8.3 %collective-permute-start.4 = (bf16[48,768]{1,0:T(8,128)(2,1)S(1)}, bf16[48,768]{1,0:T(8,128)(2,1)S(1)}, u32[]{:S(2)}, u32[]{:S(2)}) collective-permute-start(bf16[48,768]{1,0:T(8,128)(2,1)S(1)} %pad_maximum_fusion.2.rest_0_), channel_id=1, source_target_pairs={{0,4},{1,5},{2,6},{3,7},{4,0},{5,1},{6,2},{7,3},{8,12},{9,13},{10,... | collective-permute-start | bytes 221192 | tf_op jit(solution)/shard_map/ppermute | solution.py:19
  12.6 18.6 %collective-permute-start.9 = (bf16[96,384]{1,0:T(8,128)(2,1)S(1)}, bf16[96,384]{1,0:T(8,128)(2,1)S(1)}, u32[]{:S(2)}, u32[]{:S(2)}) collective-permute-start(bf16[96,384]{1,0:T(8,128)(2,1)S(1)} %get-tuple-element.67), channel_id=1, source_target_pairs={{0,3},{1,2},{2,1},{3,0},{4,7},{5,6},{6,5},{7,4},{8,11},{9,10},{10,... | collective-permute-start | bytes 221192 | tf_op jit(solution)/shard_map/ppermute | solution.py:19
  15.5 15.7 %collective-permute-start.10 = (bf16[96,384]{1,0:T(8,128)(2,1)S(1)}, bf16[96,384]{1,0:T(8,128)(2,1)S(1)}, u32[]{:S(2)}, u32[]{:S(2)}) collective-permute-start(bf16[96,384]{1,0:T(8,128)(2,1)S(1)} %get-tuple-element.67), channel_id=1, source_target_pairs={{0,1},{1,0},{2,3},{3,2},{4,5},{5,4},{6,7},{7,6},{8,9},{9,8},{10,11... | collective-permute-start | bytes 221192 | tf_op jit(solution)/shard_map/ppermute | solution.py:19
  16.1 15.2 %collective-permute-start.11 = (bf16[96,384]{1,0:T(8,128)(2,1)S(1)}, bf16[96,384]{1,0:T(8,128)(2,1)S(1)}, u32[]{:S(2)}, u32[]{:S(2)}) collective-permute-start(bf16[96,384]{1,0:T(8,128)(2,1)S(1)} %get-tuple-element.67), channel_id=1, source_target_pairs={{0,2},{1,3},{2,0},{3,1},{4,6},{5,7},{6,4},{7,5},{8,10},{9,11},{10,... | collective-permute-start | bytes 221192 | tf_op jit(solution)/shard_map/ppermute | solution.py:19
  16.2 6.2 %collective-permute-start.5 = (bf16[96,384]{1,0:T(8,128)(2,1)S(1)}, bf16[96,384]{1,0:T(8,128)(2,1)S(1)}, u32[]{:S(2)}, u32[]{:S(2)}) collective-permute-start(bf16[96,384]{1,0:T(8,128)(2,1)S(1)} %get-tuple-element.69), channel_id=1, source_target_pairs={{0,3},{1,2},{2,1},{3,0},{4,7},{5,6},{6,5},{7,4},{8,11},{9,10},{10,... | collective-permute-start | bytes 221192 | tf_op jit(solution)/shard_map/ppermute | solution.py:19
  19.2 4.4 %collective-permute-start.6 = (bf16[96,384]{1,0:T(8,128)(2,1)S(1)}, bf16[96,384]{1,0:T(8,128)(2,1)S(1)}, u32[]{:S(2)}, u32[]{:S(2)}) collective-permute-start(bf16[96,384]{1,0:T(8,128)(2,1)S(1)} %get-tuple-element.69), channel_id=1, source_target_pairs={{0,1},{1,0},{2,3},{3,2},{4,5},{5,4},{6,7},{7,6},{8,9},{9,8},{10,11... | collective-permute-start | bytes 221192 | tf_op jit(solution)/shard_map/ppermute | solution.py:19
  22.4 5.5 %collective-permute-start.7 = (bf16[96,384]{1,0:T(8,128)(2,1)S(1)}, bf16[96,384]{1,0:T(8,128)(2,1)S(1)}, u32[]{:S(2)}, u32[]{:S(2)}) collective-permute-start(bf16[96,384]{1,0:T(8,128)(2,1)S(1)} %get-tuple-element.69), channel_id=1, source_target_pairs={{0,2},{1,3},{2,0},{3,1},{4,6},{5,7},{6,4},{7,5},{8,10},{9,11},{10,... | collective-permute-start | bytes 221192 | tf_op jit(solution)/shard_map/ppermute | solution.py:19
  23.6 11.9 %collective-permute-start.17 = (f32[48,768]{1,0:T(8,128)S(1)}, f32[48,768]{1,0:T(8,128)S(1)}, u32[]{:S(2)}, u32[]{:S(2)}) collective-permute-start(f32[48,768]{1,0:T(8,128)S(1)} %get-tuple-element.49), channel_id=1, source_target_pairs={{0,4},{1,5},{2,6},{3,7},{4,0},{5,1},{6,2},{7,3},{8,12},{9,13},{10,... | collective-permute-start | bytes 442376 | tf_op jit(solution)/shard_map/ppermute | solution.py:19
  29.6 6.8 %collective-permute-start.12 = (bf16[384,384]{1,0:T(8,128)(2,1)S(1)}, bf16[384,384]{1,0:T(8,128)(2,1)S(1)}, u32[]{:S(2)}, u32[]{:S(2)}) collective-permute-start(bf16[384,384]{1,0:T(8,128)(2,1)S(1)} %get-tuple-element.46), channel_id=1, source_target_pairs={{0,16},{8,24},{16,0},{24,8},{1,17},{9,25},{17,1},{25,9},{2,18},{10... | collective-permute-start | bytes 884744 | tf_op jit(solution)/shard_map/ppermute | solution.py:19
  36.5 6.0 %collective-permute-start.21 = (bf16[96,384]{1,0:T(8,128)(2,1)S(1)}, bf16[96,384]{1,0:T(8,128)(2,1)S(1)}, u32[]{:S(2)}, u32[]{:S(2)}) collective-permute-start(bf16[96,384]{1,0:T(8,128)(2,1)S(1)} %get-tuple-element.76), channel_id=1, source_target_pairs={{0,3},{1,2},{2,1},{3,0},{4,7},{5,6},{6,5},{7,4},{8,11},{9,10},{10,... | collective-permute-start | bytes 221192 | tf_op jit(solution)/shard_map/ppermute | solution.py:19
  37.7 5.9 %collective-permute-start.22 = (bf16[96,384]{1,0:T(8,128)(2,1)S(1)}, bf16[96,384]{1,0:T(8,128)(2,1)S(1)}, u32[]{:S(2)}, u32[]{:S(2)}) collective-permute-start(bf16[96,384]{1,0:T(8,128)(2,1)S(1)} %get-tuple-element.78), channel_id=1, source_target_pairs={{0,1},{1,0},{2,3},{3,2},{4,5},{5,4},{6,7},{7,6},{8,9},{9,8},{10,11... | collective-permute-start | bytes 221192 | tf_op jit(solution)/shard_map/ppermute | solution.py:19
  38.7 5.0 %collective-permute-start.23 = (bf16[96,384]{1,0:T(8,128)(2,1)S(1)}, bf16[96,384]{1,0:T(8,128)(2,1)S(1)}, u32[]{:S(2)}, u32[]{:S(2)}) collective-permute-start(bf16[96,384]{1,0:T(8,128)(2,1)S(1)} %get-tuple-element.77), channel_id=1, source_target_pairs={{0,2},{1,3},{2,0},{3,1},{4,6},{5,7},{6,4},{7,5},{8,10},{9,11},{10,... | collective-permute-start | bytes 221192 | tf_op jit(solution)/shard_map/ppermute | solution.py:19
  40.1 5.8 %collective-permute-start.13 = (bf16[96,384]{1,0:T(8,128)(2,1)S(1)}, bf16[96,384]{1,0:T(8,128)(2,1)S(1)}, u32[]{:S(2)}, u32[]{:S(2)}) collective-permute-start(bf16[96,384]{1,0:T(8,128)(2,1)S(1)} %get-tuple-element.79), channel_id=1, source_target_pairs={{0,3},{1,2},{2,1},{3,0},{4,7},{5,6},{6,5},{7,4},{8,11},{9,10},{10,... | collective-permute-start | bytes 221192 | tf_op jit(solution)/shard_map/ppermute | solution.py:19
  41.3 4.9 %collective-permute-start.14 = (bf16[96,384]{1,0:T(8,128)(2,1)S(1)}, bf16[96,384]{1,0:T(8,128)(2,1)S(1)}, u32[]{:S(2)}, u32[]{:S(2)}) collective-permute-start(bf16[96,384]{1,0:T(8,128)(2,1)S(1)} %get-tuple-element.81), channel_id=1, source_target_pairs={{0,1},{1,0},{2,3},{3,2},{4,5},{5,4},{6,7},{7,6},{8,9},{9,8},{10,11... | collective-permute-start | bytes 221192 | tf_op jit(solution)/shard_map/ppermute | solution.py:19
  42.5 4.6 %collective-permute-start.15 = (bf16[96,384]{1,0:T(8,128)(2,1)S(1)}, bf16[96,384]{1,0:T(8,128)(2,1)S(1)}, u32[]{:S(2)}, u32[]{:S(2)}) collective-permute-start(bf16[96,384]{1,0:T(8,128)(2,1)S(1)} %get-tuple-element.80), channel_id=1, source_target_pairs={{0,2},{1,3},{2,0},{3,1},{4,6},{5,7},{6,4},{7,5},{8,10},{9,11},{10,... | collective-permute-start | bytes 221192 | tf_op jit(solution)/shard_map/ppermute | solution.py:19
  43.7 5.7 %collective-permute-start.24 = (bf16[96,384]{1,0:T(8,128)(2,1)S(1)}, bf16[96,384]{1,0:T(8,128)(2,1)S(1)}, u32[]{:S(2)}, u32[]{:S(2)}) collective-permute-start(bf16[96,384]{1,0:T(8,128)(2,1)S(1)} %add_convert_fusion.2), channel_id=1, source_target_pairs={{0,4},{1,5},{2,6},{3,7},{4,0},{5,1},{6,2},{7,3},{8,12},{9,13},{10,... | collective-permute-start | bytes 221192 | tf_op jit(solution)/shard_map/ppermute | solution.py:19
  47.1 5.9 %collective-permute-start.16 = (bf16[96,384]{1,0:T(8,128)(2,1)S(1)}, bf16[96,384]{1,0:T(8,128)(2,1)S(1)}, u32[]{:S(2)}, u32[]{:S(2)}) collective-permute-start(bf16[96,384]{1,0:T(8,128)(2,1)S(1)} %add_convert_fusion.3), channel_id=1, source_target_pairs={{0,4},{1,5},{2,6},{3,7},{4,0},{5,1},{6,2},{7,3},{8,12},{9,13},{10,... | collective-permute-start | bytes 221192 | tf_op jit(solution)/shard_map/ppermute | solution.py:19
  49.5 6.6 %collective-permute-start.25 = (bf16[96,384]{1,0:T(8,128)(2,1)S(1)}, bf16[96,384]{1,0:T(8,128)(2,1)S(1)}, u32[]{:S(2)}, u32[]{:S(2)}) collective-permute-start(bf16[96,384]{1,0:T(8,128)(2,1)S(1)} %get-tuple-element.63), channel_id=1, source_target_pairs={{0,3},{1,2},{2,1},{3,0},{4,7},{5,6},{6,5},{7,4},{8,11},{9,10},{10,... | collective-permute-start | bytes 221192 | tf_op jit(solution)/shard_map/ppermute | solution.py:19
  51.3 5.4 %collective-permute-start.26 = (bf16[96,384]{1,0:T(8,128)(2,1)S(1)}, bf16[96,384]{1,0:T(8,128)(2,1)S(1)}, u32[]{:S(2)}, u32[]{:S(2)}) collective-permute-start(bf16[96,384]{1,0:T(8,128)(2,1)S(1)} %get-tuple-element.63), channel_id=1, source_target_pairs={{0,1},{1,0},{2,3},{3,2},{4,5},{5,4},{6,7},{7,6},{8,9},{9,8},{10,11... | collective-permute-start | bytes 221192 | tf_op jit(solution)/shard_map/ppermute | solution.py:19
  53.1 6.0 %collective-permute-start.18 = (bf16[96,384]{1,0:T(8,128)(2,1)S(1)}, bf16[96,384]{1,0:T(8,128)(2,1)S(1)}, u32[]{:S(2)}, u32[]{:S(2)}) collective-permute-start(bf16[96,384]{1,0:T(8,128)(2,1)S(1)} %get-tuple-element.65), channel_id=1, source_target_pairs={{0,3},{1,2},{2,1},{3,0},{4,7},{5,6},{6,5},{7,4},{8,11},{9,10},{10,... | collective-permute-start | bytes 221192 | tf_op jit(solution)/shard_map/ppermute | solution.py:19
  62.4 6.8 %collective-permute-start.28 = (bf16[384,384]{1,0:T(8,128)(2,1)S(1)}, bf16[384,384]{1,0:T(8,128)(2,1)S(1)}, u32[]{:S(2)}, u32[]{:S(2)}) collective-permute-start(bf16[384,384]{1,0:T(8,128)(2,1)S(1)} %get-tuple-element.55), channel_id=1, source_target_pairs={{0,16},{8,24},{16,0},{24,8},{1,17},{9,25},{17,1},{25,9},{2,18},{10... | collective-permute-start | bytes 884744 | tf_op jit(solution)/shard_map/ppermute | solution.py:19
  69.3 5.6 %collective-permute-start.33 = (bf16[96,384]{1,0:T(8,128)(2,1)S(1)}, bf16[96,384]{1,0:T(8,128)(2,1)S(1)}, u32[]{:S(2)}, u32[]{:S(2)}) collective-permute-start(bf16[96,384]{1,0:T(8,128)(2,1)S(1)} %get-tuple-element.70), channel_id=1, source_target_pairs={{0,3},{1,2},{2,1},{3,0},{4,7},{5,6},{6,5},{7,4},{8,11},{9,10},{10,... | collective-permute-start | bytes 221192 | tf_op jit(solution)/shard_map/ppermute | solution.py:19
  70.7 5.7 %collective-permute-start.34 = (bf16[96,384]{1,0:T(8,128)(2,1)S(1)}, bf16[96,384]{1,0:T(8,128)(2,1)S(1)}, u32[]{:S(2)}, u32[]{:S(2)}) collective-permute-start(bf16[96,384]{1,0:T(8,128)(2,1)S(1)} %get-tuple-element.72), channel_id=1, source_target_pairs={{0,1},{1,0},{2,3},{3,2},{4,5},{5,4},{6,7},{7,6},{8,9},{9,8},{10,11... | collective-permute-start | bytes 221192 | tf_op jit(solution)/shard_map/ppermute | solution.py:19
  71.3 5.1 %collective-permute-start.35 = (bf16[96,384]{1,0:T(8,128)(2,1)S(1)}, bf16[96,384]{1,0:T(8,128)(2,1)S(1)}, u32[]{:S(2)}, u32[]{:S(2)}) collective-permute-start(bf16[96,384]{1,0:T(8,128)(2,1)S(1)} %get-tuple-element.71), channel_id=1, source_target_pairs={{0,2},{1,3},{2,0},{3,1},{4,6},{5,7},{6,4},{7,5},{8,10},{9,11},{10,... | collective-permute-start | bytes 221192 | tf_op jit(solution)/shard_map/ppermute | solution.py:19
  72.9 5.8 %collective-permute-start.29 = (bf16[96,384]{1,0:T(8,128)(2,1)S(1)}, bf16[96,384]{1,0:T(8,128)(2,1)S(1)}, u32[]{:S(2)}, u32[]{:S(2)}) collective-permute-start(bf16[96,384]{1,0:T(8,128)(2,1)S(1)} %get-tuple-element.73), channel_id=1, source_target_pairs={{0,3},{1,2},{2,1},{3,0},{4,7},{5,6},{6,5},{7,4},{8,11},{9,10},{10,... | collective-permute-start | bytes 221192 | tf_op jit(solution)/shard_map/ppermute | solution.py:19
  74.3 4.7 %collective-permute-start.30 = (bf16[96,384]{1,0:T(8,128)(2,1)S(1)}, bf16[96,384]{1,0:T(8,128)(2,1)S(1)}, u32[]{:S(2)}, u32[]{:S(2)}) collective-permute-start(bf16[96,384]{1,0:T(8,128)(2,1)S(1)} %get-tuple-element.75), channel_id=1, source_target_pairs={{0,1},{1,0},{2,3},{3,2},{4,5},{5,4},{6,7},{7,6},{8,9},{9,8},{10,11... | collective-permute-start | bytes 221192 | tf_op jit(solution)/shard_map/ppermute | solution.py:19
  76.5 5.3 %collective-permute-start.36 = (bf16[48,384]{1,0:T(8,128)(2,1)S(1)}, bf16[48,384]{1,0:T(8,128)(2,1)S(1)}, u32[]{:S(2)}, u32[]{:S(2)}) collective-permute-start(bf16[48,384]{1,0:T(8,128)(2,1)S(1)} %constant_dynamic-slice_fusion), channel_id=1, source_target_pairs={{0,4},{1,5},{2,6},{3,7},{4,0},{5,1},{6,2},{7,3},{8,12},{9,13},{10,... | collective-permute-start | bytes 110600 | tf_op jit(solution)/shard_map/ppermute | solution.py:19
  79.3 4.9 %collective-permute-start.32 = (bf16[48,384]{1,0:T(8,128)(2,1)S(1)}, bf16[48,384]{1,0:T(8,128)(2,1)S(1)}, u32[]{:S(2)}, u32[]{:S(2)}) collective-permute-start(bf16[48,384]{1,0:T(8,128)(2,1)S(1)} %constant_dynamic-slice_fusion.4), channel_id=1, source_target_pairs={{0,4},{1,5},{2,6},{3,7},{4,0},{5,1},{6,2},{7,3},{8,12},{9,13},{10,... | collective-permute-start | bytes 110600 | tf_op jit(solution)/shard_map/ppermute | solution.py:19
  (9 other events, 31.8 us)

commit v4 on v3

--- a/solution.py
+++ b/solution.py
@@ -8,7 +8,7 @@
 from jax.sharding import PartitionSpec as P
 
 ITERS = 2
-LIMIT = 32 * 1024 * 1024
+LIMIT = 8 * 1024 * 1024
 COST = 5 * 10**9
 VMEM = pl.BlockSpec(memory_space=pltpu.VMEM)
 SMEM = pl.BlockSpec(memory_space=pltpu.SMEM)
@@ -242,11 +242,14 @@
     def gather(block, group, own=None):
         rows = block.shape[0]
         place = position(group)
+        first_arrived = None
         whole = jnp.zeros((rows << len(group), block.shape[1]), block.dtype)
         whole = lax.dynamic_update_slice_in_dim(whole, block if own is None else own, place * rows, 0)
         for j, distance in partners(group):
-            whole = lax.dynamic_update_slice_in_dim(whole, swap(block, "op", distance), (place ^ j) * rows, 0)
-        return whole
+            piece = swap(block, "op", distance)
+            first_arrived = piece if first_arrived is None else first_arrived
+            whole = lax.dynamic_update_slice_in_dim(whole, piece, (place ^ j) * rows, 0)
+        return whole, first_arrived
 
     def respread(block):
         if shard % 16 == 0:
@@ -256,8 +259,8 @@
 
     def gather_all(block):
         for group in groups[::-1]:
-            block = gather(block, group)
-        return respread(block)
+            block, first_arrived = gather(block, group)
+        return respread(block), first_arrived
 
     def beside(block, own=None):
         own = block if own is None else own
@@ -277,7 +280,7 @@
     moves = (offsets, swap(offsets, "sec", 1))
     *outer_weights, passed = arrange(0, moves, lefts, rights, start)
     together = beside(start, passed)
-    vectors = [gather_all(together[:, :width]), gather_all(together[:, width:])]
+    vectors = [gather_all(together[:, :width])[0], gather_all(together[:, width:])[0]]
     own_diagonal = diagonal[0]
     *inner_weights, slots = arrange(1, moves, lefts, rights, own_diagonal, swap(own_diagonal, "sec", 1))
     both_diagonals = beside(slots)
@@ -301,7 +304,7 @@
             functools.partial(second_kernel, members),
             "second",
             (f32, f32),
-            COST,
+            COST//10,
             vectors[0],
             outer_weights,
             stayed,
@@ -315,7 +318,10 @@
                 block = scatter(block, group).astype(bf16)
             if turn < ITERS - 1:
                 total = block.astype(f32) + swap(block, "op", last).astype(f32)
-                vectors[k] = gather_all((total / diagonals[k]).astype(bf16))
+                ready = (total / diagonals[k]).astype(bf16)
+                if k == 1:
+                    ready, _ = lax.optimization_barrier((ready, first_arrived))
+                vectors[k], first_arrived = gather_all(ready)
             else:
                 blocks[k] = (scatter(block, [last]) / own_diagonals[k]).astype(bf16)
     kept = jnp.where(mine, blocks[0], blocks[1])

time: 86.6 us -> 85.5 us (0.987)
    unnamed x7 -> x11, local copies, waits for them, and re-layouts: 3.3 us -> 3.31 us
  transfers between devices with their start and end apart: 38 -> 38, of which waited for: 15 -> 17; matrix products, arithmetic and copies ran while one was open for 2% -> 2% of each run, Pallas kernels for 15% -> 17%
where the time goes in v4:
time: 85.5 us; the launch traced here: 85.6 us
  starting transfers between devices  49.7 us (58%)
  Pallas kernels  15.1 us (18%)
  waiting for transfers between devices  14.7 us (17%)
  local copies, waits for them, and re-layouts  3.81 us (4%)
  other arithmetic  1.88 us (2%)
    ppermute x38, starting transfers between devices, swap(): return lax.ppermute(block, axis, route)  49.7 us
    ppermute x38, waiting for transfers between devices, swap(): return lax.ppermute(block, axis, route)  14.7 us
    pallas_call x6, Pallas kernels, call(): pl.pallas_call(kernel, out_shape=shapes, in_specs=[VMEM] * (4 + len(more)...  11.5 us
    pallas_call x2, Pallas kernels, arrange(): pl.pallas_call(functools.partial(arrange_kernel, slot), out_shape=(shape,...  3.49 us
    unnamed x11, local copies, waits for them, and re-layouts  3.31 us
  transfers between devices with their start and end apart: 38, of which 17 were waited for; matrix products, arithmetic and copies ran while one was open for 2% of the time, Pallas kernels for 17%

profile of v4, /device:TPU:0, one launch (start us, length us, event | category | flops | bytes accessed | tf_op | source)
XLA Modules:
  0.0 85.6 jit_solution(3619010404217215541)
XLA Ops:
  4.3 3.9 %collective-permute-start.4 = (bf16[48,768]{1,0:T(8,128)(2,1)S(1)}, bf16[48,768]{1,0:T(8,128)(2,1)S(1)}, u32[]{:S(2)}, u32[]{:S(2)}) collective-permute-start(bf16[48,768]{1,0:T(8,128)(2,1)S(1)} %pad_maximum_fusion.2.rest_0_), channel_id=1, source_target_pairs={{0,4},{1,5},{2,6},{3,7},{4,0},{5,1},{6,2},{7,3},{8,12},{9,13},{10,... | collective-permute-start | bytes 221192 | tf_op jit(solution)/shard_map/ppermute | solution.py:19
  8.2 1.3 %copy-done = bf16[4,384,384]{2,1,0:T(8,128)(2,1)S(1)} copy-done((bf16[4,384,384]{2,1,0:T(8,128)(2,1)S(1)}, bf16[4,384,384]{2,1,0:T(8,128)(2,1)}, u32[]{:S(2)}) %copy-start) | copy-done | bytes 1179672
  9.5 1.3 %copy-done.2 = bf16[4,384,384]{2,1,0:T(8,128)(2,1)S(1)} copy-done((bf16[4,384,384]{2,1,0:T(8,128)(2,1)S(1)}, bf16[4,384,384]{2,1,0:T(8,128)(2,1)}, u32[]{:S(2)}) %copy-start.2) | copy-done | bytes 1179672
  10.8 1.7 %arrange.2 = (bf16[2,384,1536]{2,1,0:T(8,128)(2,1)S(1)}, bf16[2,384,1536]{2,1,0:T(8,128)(2,1)S(1)}, s32[2,8,128]{2,1,0:T(8,128)S(1)}, bf16[48,768]{1,0:T(8,128)(2,1)S(1)}) custom-call(s32[4,2]{1,0:T(4,128)S(1)} %copy.7.own_steps, s32[4,2]{1,0:T(4,128)S(1)} %collective-permute-done.other_steps, bf16[4,384,384]{2,1,0:T(8,128)(2,1)S(1)} %copy-done, ...), custom_call_target="tpu_custom_call" | custom-call | flops 5000000000 | bytes 1 | tf_op jit(solution)/shard_map/arrange/pallas_call | solution.py:65
  12.6 2.9 %collective-permute-start.9 = (bf16[96,384]{1,0:T(8,128)(2,1)S(1)}, bf16[96,384]{1,0:T(8,128)(2,1)S(1)}, u32[]{:S(2)}, u32[]{:S(2)}) collective-permute-start(bf16[96,384]{1,0:T(8,128)(2,1)S(1)} %get-tuple-element.67), channel_id=1, source_target_pairs={{0,3},{1,2},{2,1},{3,0},{4,7},{5,6},{6,5},{7,4},{8,11},{9,10},{10,... | collective-permute-start | bytes 221192 | tf_op jit(solution)/shard_map/ppermute | solution.py:19
  16.2 2.9 %collective-permute-start.5 = (bf16[96,384]{1,0:T(8,128)(2,1)S(1)}, bf16[96,384]{1,0:T(8,128)(2,1)S(1)}, u32[]{:S(2)}, u32[]{:S(2)}) collective-permute-start(bf16[96,384]{1,0:T(8,128)(2,1)S(1)} %get-tuple-element.69), channel_id=1, source_target_pairs={{0,3},{1,2},{2,1},{3,0},{4,7},{5,6},{6,5},{7,4},{8,11},{9,10},{10,... | collective-permute-start | bytes 221192 | tf_op jit(solution)/shard_map/ppermute | solution.py:19
  19.7 1.7 %arrange.3 = (bf16[2,384,1536]{2,1,0:T(8,128)(2,1)S(1)}, bf16[2,384,1536]{2,1,0:T(8,128)(2,1)S(1)}, s32[2,8,128]{2,1,0:T(8,128)S(1)}, f32[48,768]{1,0:T(8,128)S(1)}) custom-call(s32[4,2]{1,0:T(4,128)S(1)} %copy.7.own_steps, s32[4,2]{1,0:T(4,128)S(1)} %collective-permute-done.other_steps, bf16[4,384,384]{2,1,0:T(8,128)(2,1)S(1)} %copy-done.1, ...), custom_call_target="tpu_custom_call" | custom-call | flops 5000000000 | bytes 1 | tf_op jit(solution)/shard_map/arrange/pallas_call | solution.py:65
  23.6 2.7 %collective-permute-start.17 = (f32[48,768]{1,0:T(8,128)S(1)}, f32[48,768]{1,0:T(8,128)S(1)}, u32[]{:S(2)}, u32[]{:S(2)}) collective-permute-start(f32[48,768]{1,0:T(8,128)S(1)} %get-tuple-element.50), channel_id=1, source_target_pairs={{0,4},{1,5},{2,6},{3,7},{4,0},{5,1},{6,2},{7,3},{8,12},{9,13},{10,... | collective-permute-start | bytes 442376 | tf_op jit(solution)/shard_map/ppermute | solution.py:19
  26.2 1.7 %collective-permute-done.7 = bf16[96,384]{1,0:T(8,128)(2,1)S(1)} collective-permute-done((bf16[96,384]{1,0:T(8,128)(2,1)S(1)}, bf16[96,384]{1,0:T(8,128)(2,1)S(1)}, u32[]{:S(2)}, u32[]{:S(2)}) %collective-permute-start.7) | collective-permute-done | bytes 73760 | tf_op jit(solution)/shard_map/ppermute | solution.py:19
  27.9 1.6 %first.2 = (bf16[384,384]{1,0:T(8,128)(2,1)S(1)}, f32[384,384]{1,0:T(8,128)S(1)}) custom-call(s32[2,8,128]{2,1,0:T(8,128)S(1)} %get-tuple-element.36.counts, bf16[384,384]{1,0:T(8,128)(2,1)S(1)} %constant_dynamic-update-slice_fusion.12.vector, bf16[2,384,1536]{2,1,0:T(8,128)(2,1)S(1)} %get-tuple-element.38.lefts, ...), custom_call_target="tpu_custom_call" | custom-call | flops 5000000000 | bytes 1 | tf_op jit(solution)/shard_map/first/pallas_call | solution.py:196
  29.5 1.6 %collective-permute-start.12 = (bf16[384,384]{1,0:T(8,128)(2,1)S(1)}, bf16[384,384]{1,0:T(8,128)(2,1)S(1)}, u32[]{:S(2)}, u32[]{:S(2)}) collective-permute-start(bf16[384,384]{1,0:T(8,128)(2,1)S(1)} %get-tuple-element.47), channel_id=1, source_target_pairs={{0,16},{8,24},{16,0},{24,8},{1,17},{9,25},{17,1},{25,9},{2,18},{10... | collective-permute-start | bytes 884744 | tf_op jit(solution)/shard_map/ppermute | solution.py:19
  31.3 2.4 %inner.2 = (f32[384,384]{1,0:T(8,128)S(1)}, f32[384,384]{1,0:T(8,128)S(1)}) custom-call(s32[2,8,128]{2,1,0:T(8,128)S(1)} %get-tuple-element.41.counts, bf16[384,384]{1,0:T(8,128)(2,1)S(1)} %constant_dynamic-update-slice_fusion.8.vector, bf16[2,384,1536]{2,1,0:T(8,128)(2,1)S(1)} %get-tuple-element.42.lefts, bf16[2,384,1536]{2,1,0:T(8,128)(2,1)S(1)} %get-tuple-element.43.rights), custom_call_target="tpu_custom_call" | custom-call | flops 5000000000 | bytes 1 | tf_op jit(solution)/shard_map/inner/pallas_call | solution.py:196
  33.6 1.8 %second.2 = (f32[384,384]{1,0:T(8,128)S(1)}, f32[384,384]{1,0:T(8,128)S(1)}) custom-call(s32[2,8,128]{2,1,0:T(8,128)S(1)} %get-tuple-element.36.counts, bf16[384,384]{1,0:T(8,128)(2,1)S(1)} %constant_dynamic-update-slice_fusion.12.vector, bf16[2,384,1536]{2,1,0:T(8,128)(2,1)S(1)} %get-tuple-element.38.lefts, ...), custom_call_target="tpu_custom_call" | custom-call | flops 500000000 | bytes 1 | tf_op jit(solution)/shard_map/second/pallas_call | solution.py:196
  36.4 1.4 %collective-permute-start.13 = (bf16[96,384]{1,0:T(8,128)(2,1)S(1)}, bf16[96,384]{1,0:T(8,128)(2,1)S(1)}, u32[]{:S(2)}, u32[]{:S(2)}) collective-permute-start(bf16[96,384]{1,0:T(8,128)(2,1)S(1)} %get-tuple-element.79), channel_id=1, source_target_pairs={{0,3},{1,2},{2,1},{3,0},{4,7},{5,6},{6,5},{7,4},{8,11},{9,10},{10,... | collective-permute-start | bytes 221192 | tf_op jit(solution)/shard_map/ppermute | solution.py:19
  38.7 1.3 %collective-permute-start.15 = (bf16[96,384]{1,0:T(8,128)(2,1)S(1)}, bf16[96,384]{1,0:T(8,128)(2,1)S(1)}, u32[]{:S(2)}, u32[]{:S(2)}) collective-permute-start(bf16[96,384]{1,0:T(8,128)(2,1)S(1)} %get-tuple-element.80), channel_id=1, source_target_pairs={{0,2},{1,3},{2,0},{3,1},{4,6},{5,7},{6,4},{7,5},{8,10},{9,11},{10,... | collective-permute-start | bytes 221192 | tf_op jit(solution)/shard_map/ppermute | solution.py:19
  40.0 1.4 %collective-permute-start.21 = (bf16[96,384]{1,0:T(8,128)(2,1)S(1)}, bf16[96,384]{1,0:T(8,128)(2,1)S(1)}, u32[]{:S(2)}, u32[]{:S(2)}) collective-permute-start(bf16[96,384]{1,0:T(8,128)(2,1)S(1)} %get-tuple-element.76), channel_id=1, source_target_pairs={{0,3},{1,2},{2,1},{3,0},{4,7},{5,6},{6,5},{7,4},{8,11},{9,10},{10,... | collective-permute-start | bytes 221192 | tf_op jit(solution)/shard_map/ppermute | solution.py:19
  43.8 2.1 %collective-permute-start.16 = (bf16[96,384]{1,0:T(8,128)(2,1)S(1)}, bf16[96,384]{1,0:T(8,128)(2,1)S(1)}, u32[]{:S(2)}, u32[]{:S(2)}) collective-permute-start(bf16[96,384]{1,0:T(8,128)(2,1)S(1)} %add_convert_fusion.3), channel_id=1, source_target_pairs={{0,4},{1,5},{2,6},{3,7},{4,0},{5,1},{6,2},{7,3},{8,12},{9,13},{10,... | collective-permute-start | bytes 221192 | tf_op jit(solution)/shard_map/ppermute | solution.py:19
  47.2 2.0 %collective-permute-start.24 = (bf16[96,384]{1,0:T(8,128)(2,1)S(1)}, bf16[96,384]{1,0:T(8,128)(2,1)S(1)}, u32[]{:S(2)}, u32[]{:S(2)}) collective-permute-start(bf16[96,384]{1,0:T(8,128)(2,1)S(1)} %add_convert_fusion.2), channel_id=1, source_target_pairs={{0,4},{1,5},{2,6},{3,7},{4,0},{5,1},{6,2},{7,3},{8,12},{9,13},{10,... | collective-permute-start | bytes 221192 | tf_op jit(solution)/shard_map/ppermute | solution.py:19
  49.6 1.6 %collective-permute-start.18 = (bf16[96,384]{1,0:T(8,128)(2,1)S(1)}, bf16[96,384]{1,0:T(8,128)(2,1)S(1)}, u32[]{:S(2)}, u32[]{:S(2)}) collective-permute-start(bf16[96,384]{1,0:T(8,128)(2,1)S(1)} %get-tuple-element.65), channel_id=1, source_target_pairs={{0,3},{1,2},{2,1},{3,0},{4,7},{5,6},{6,5},{7,4},{8,11},{9,10},{10,... | collective-permute-start | bytes 221192 | tf_op jit(solution)/shard_map/ppermute | solution.py:19
  51.2 1.2 %collective-permute-start.19 = (bf16[96,384]{1,0:T(8,128)(2,1)S(1)}, bf16[96,384]{1,0:T(8,128)(2,1)S(1)}, u32[]{:S(2)}, u32[]{:S(2)}) collective-permute-start(bf16[96,384]{1,0:T(8,128)(2,1)S(1)} %get-tuple-element.65), channel_id=1, source_target_pairs={{0,1},{1,0},{2,3},{3,2},{4,5},{5,4},{6,7},{7,6},{8,9},{9,8},{10,11... | collective-permute-start | bytes 221192 | tf_op jit(solution)/shard_map/ppermute | solution.py:19
  53.3 1.7 %collective-permute-done.18 = bf16[96,384]{1,0:T(8,128)(2,1)S(1)} collective-permute-done((bf16[96,384]{1,0:T(8,128)(2,1)S(1)}, bf16[96,384]{1,0:T(8,128)(2,1)S(1)}, u32[]{:S(2)}, u32[]{:S(2)}) %collective-permute-start.18) | collective-permute-done | bytes 73760 | tf_op jit(solution)/shard_map/ppermute | solution.py:19
  55.0 2.0 %collective-permute-start.25 = (bf16[96,384]{1,0:T(8,128)(2,1)S(1)}, bf16[96,384]{1,0:T(8,128)(2,1)S(1)}, u32[]{:S(2)}, u32[]{:S(2)}) collective-permute-start(bf16[96,384]{1,0:T(8,128)(2,1)S(1)} %fusion.3), channel_id=1, source_target_pairs={{0,3},{1,2},{2,1},{3,0},{4,7},{5,6},{6,5},{7,4},{8,11},{9,10},{10,... | collective-permute-start | bytes 221192 | tf_op jit(solution)/shard_map/ppermute | solution.py:19
  58.6 1.6 %first.3 = (bf16[384,384]{1,0:T(8,128)(2,1)S(1)}, f32[384,384]{1,0:T(8,128)S(1)}) custom-call(s32[2,8,128]{2,1,0:T(8,128)S(1)} %get-tuple-element.36.counts, bf16[384,384]{1,0:T(8,128)(2,1)S(1)} %constant_dynamic-update-slice_fusion.4.vector, bf16[2,384,1536]{2,1,0:T(8,128)(2,1)S(1)} %get-tuple-element.38.lefts, ...), custom_call_target="tpu_custom_call" | custom-call | flops 5000000000 | bytes 1 | tf_op jit(solution)/shard_map/first/pallas_call | solution.py:196
  60.2 2.3 %collective-permute-start.28 = (bf16[384,384]{1,0:T(8,128)(2,1)S(1)}, bf16[384,384]{1,0:T(8,128)(2,1)S(1)}, u32[]{:S(2)}, u32[]{:S(2)}) collective-permute-start(bf16[384,384]{1,0:T(8,128)(2,1)S(1)} %get-tuple-element.57), channel_id=1, source_target_pairs={{0,16},{8,24},{16,0},{24,8},{1,17},{9,25},{17,1},{25,9},{2,18},{10... | collective-permute-start | bytes 884744 | tf_op jit(solution)/shard_map/ppermute | solution.py:19
  62.6 2.6 %inner.3 = (f32[384,384]{1,0:T(8,128)S(1)}, f32[384,384]{1,0:T(8,128)S(1)}) custom-call(s32[2,8,128]{2,1,0:T(8,128)S(1)} %get-tuple-element.41.counts, bf16[384,384]{1,0:T(8,128)(2,1)S(1)} %constant_dynamic-update-slice_fusion.vector, bf16[2,384,1536]{2,1,0:T(8,128)(2,1)S(1)} %get-tuple-element.42.lefts, bf16[2,384,1536]{2,1,0:T(8,128)(2,1)S(1)} %get-tuple-element.43.rights), custom_call_target="tpu_custom_call" | custom-call | flops 5000000000 | bytes 1 | tf_op jit(solution)/shard_map/inner/pallas_call | solution.py:196
  65.2 1.6 %second.3 = (f32[384,384]{1,0:T(8,128)S(1)}, f32[384,384]{1,0:T(8,128)S(1)}) custom-call(s32[2,8,128]{2,1,0:T(8,128)S(1)} %get-tuple-element.36.counts, bf16[384,384]{1,0:T(8,128)(2,1)S(1)} %constant_dynamic-update-slice_fusion.4.vector, bf16[2,384,1536]{2,1,0:T(8,128)(2,1)S(1)} %get-tuple-element.38.lefts, ...), custom_call_target="tpu_custom_call" | custom-call | flops 500000000 | bytes 1 | tf_op jit(solution)/shard_map/second/pallas_call | solution.py:196
  67.3 2.0 %collective-permute-start.33 = (bf16[96,384]{1,0:T(8,128)(2,1)S(1)}, bf16[96,384]{1,0:T(8,128)(2,1)S(1)}, u32[]{:S(2)}, u32[]{:S(2)}) collective-permute-start(bf16[96,384]{1,0:T(8,128)(2,1)S(1)} %get-tuple-element.70), channel_id=1, source_target_pairs={{0,3},{1,2},{2,1},{3,0},{4,7},{5,6},{6,5},{7,4},{8,11},{9,10},{10,... | collective-permute-start | bytes 221192 | tf_op jit(solution)/shard_map/ppermute | solution.py:19
  70.9 2.0 %collective-permute-start.29 = (bf16[96,384]{1,0:T(8,128)(2,1)S(1)}, bf16[96,384]{1,0:T(8,128)(2,1)S(1)}, u32[]{:S(2)}, u32[]{:S(2)}) collective-permute-start(bf16[96,384]{1,0:T(8,128)(2,1)S(1)} %get-tuple-element.73), channel_id=1, source_target_pairs={{0,3},{1,2},{2,1},{3,0},{4,7},{5,6},{6,5},{7,4},{8,11},{9,10},{10,... | collective-permute-start | bytes 221192 | tf_op jit(solution)/shard_map/ppermute | solution.py:19
  74.7 2.3 %collective-permute-start.36 = (bf16[48,384]{1,0:T(8,128)(2,1)S(1)}, bf16[48,384]{1,0:T(8,128)(2,1)S(1)}, u32[]{:S(2)}, u32[]{:S(2)}) collective-permute-start(bf16[48,384]{1,0:T(8,128)(2,1)S(1)} %constant_dynamic-slice_fusion), channel_id=1, source_target_pairs={{0,4},{1,5},{2,6},{3,7},{4,0},{5,1},{6,2},{7,3},{8,12},{9,13},{10,... | collective-permute-start | bytes 110600 | tf_op jit(solution)/shard_map/ppermute | solution.py:19
  78.2 2.2 %collective-permute-start.32 = (bf16[48,384]{1,0:T(8,128)(2,1)S(1)}, bf16[48,384]{1,0:T(8,128)(2,1)S(1)}, u32[]{:S(2)}, u32[]{:S(2)}) collective-permute-start(bf16[48,384]{1,0:T(8,128)(2,1)S(1)} %constant_dynamic-slice_fusion.4), channel_id=1, source_target_pairs={{0,4},{1,5},{2,6},{3,7},{4,0},{5,1},{6,2},{7,3},{8,12},{9,13},{10,... | collective-permute-start | bytes 110600 | tf_op jit(solution)/shard_map/ppermute | solution.py:19
  80.4 3.2 %collective-permute-done.32 = bf16[48,384]{1,0:T(8,128)(2,1)S(1)} collective-permute-done((bf16[48,384]{1,0:T(8,128)(2,1)S(1)}, bf16[48,384]{1,0:T(8,128)(2,1)S(1)}, u32[]{:S(2)}, u32[]{:S(2)}) %collective-permute-start.32) | collective-permute-done | bytes 36896 | tf_op jit(solution)/shard_map/ppermute | solution.py:19
  83.7 1.2 %collective-permute-done.37 = bf16[48,384]{1,0:T(8,128)(2,1)S(1)} collective-permute-done((bf16[48,384]{1,0:T(8,128)(2,1)S(1)}, bf16[48,384]{1,0:T(8,128)(2,1)S(1)}, u32[]{:S(2)}, u32[]{:S(2)}) %collective-permute-start.37) | collective-permute-done | bytes 36896 | tf_op jit(solution)/shard_map/ppermute | solution.py:19
  (103 shorter events, 22.4 us)
Async XLA Ops:
  2.4 5.8 %collective-permute-start.2 = (bf16[4,384,384]{2,1,0:T(8,128)(2,1)}, bf16[4,384,384]{2,1,0:T(8,128)(2,1)S(1)}, u32[]{:S(2)}, u32[]{:S(2)}) collective-permute-start(bf16[4,384,384]{2,1,0:T(8,128)(2,1)} %left_own.3), channel_id=1, source_target_pairs={{0,8},{8,0},{16,24},{24,16},{1,9},{9,1},{17,25},{25,17},{2,10},{10... | collective-permute-start | bytes 3538952 | tf_op jit(solution)/shard_map/ppermute | solution.py:19
  2.8 5.4 %collective-permute-start.3 = (bf16[4,384,384]{2,1,0:T(8,128)(2,1)}, bf16[4,384,384]{2,1,0:T(8,128)(2,1)S(1)}, u32[]{:S(2)}, u32[]{:S(2)}) collective-permute-start(bf16[4,384,384]{2,1,0:T(8,128)(2,1)} %right_own.3), channel_id=1, source_target_pairs={{0,8},{8,0},{16,24},{24,16},{1,9},{9,1},{17,25},{25,17},{2,10},{10... | collective-permute-start | bytes 3538952 | tf_op jit(solution)/shard_map/ppermute | solution.py:19
  3.7 4.5 %collective-permute-start = (s32[4,2]{1,0:T(4,128)S(1)}, s32[4,2]{1,0:T(4,128)S(1)}, u32[]{:S(2)}, u32[]{:S(2)}) collective-permute-start(s32[4,2]{1,0:T(4,128)S(1)} %copy.7.own_steps), channel_id=1, source_target_pairs={{0,8},{8,0},{16,24},{24,16},{1,9},{9,1},{17,25},{25,17},{2,10},{10... | collective-permute-start | bytes 104 | tf_op jit(solution)/shard_map/ppermute | solution.py:19
  4.1 15.1 %collective-permute-start.8 = (f32[48,384]{1,0:T(8,128)}, f32[48,384]{1,0:T(8,128)S(1)}, u32[]{:S(2)}, u32[]{:S(2)}) collective-permute-start(f32[48,384]{1,0:T(8,128)} %bitcast.14), channel_id=1, source_target_pairs={{0,8},{8,0},{16,24},{24,16},{1,9},{9,1},{17,25},{25,17},{2,10},{10... | collective-permute-start | bytes 221192 | tf_op jit(solution)/shard_map/ppermute | solution.py:19
  4.3 8.3 %collective-permute-start.4 = (bf16[48,768]{1,0:T(8,128)(2,1)S(1)}, bf16[48,768]{1,0:T(8,128)(2,1)S(1)}, u32[]{:S(2)}, u32[]{:S(2)}) collective-permute-start(bf16[48,768]{1,0:T(8,128)(2,1)S(1)} %pad_maximum_fusion.2.rest_0_), channel_id=1, source_target_pairs={{0,4},{1,5},{2,6},{3,7},{4,0},{5,1},{6,2},{7,3},{8,12},{9,13},{10,... | collective-permute-start | bytes 221192 | tf_op jit(solution)/shard_map/ppermute | solution.py:19
  12.6 18.6 %collective-permute-start.9 = (bf16[96,384]{1,0:T(8,128)(2,1)S(1)}, bf16[96,384]{1,0:T(8,128)(2,1)S(1)}, u32[]{:S(2)}, u32[]{:S(2)}) collective-permute-start(bf16[96,384]{1,0:T(8,128)(2,1)S(1)} %get-tuple-element.67), channel_id=1, source_target_pairs={{0,3},{1,2},{2,1},{3,0},{4,7},{5,6},{6,5},{7,4},{8,11},{9,10},{10,... | collective-permute-start | bytes 221192 | tf_op jit(solution)/shard_map/ppermute | solution.py:19
  15.5 15.6 %collective-permute-start.10 = (bf16[96,384]{1,0:T(8,128)(2,1)S(1)}, bf16[96,384]{1,0:T(8,128)(2,1)S(1)}, u32[]{:S(2)}, u32[]{:S(2)}) collective-permute-start(bf16[96,384]{1,0:T(8,128)(2,1)S(1)} %get-tuple-element.67), channel_id=1, source_target_pairs={{0,1},{1,0},{2,3},{3,2},{4,5},{5,4},{6,7},{7,6},{8,9},{9,8},{10,11... | collective-permute-start | bytes 221192 | tf_op jit(solution)/shard_map/ppermute | solution.py:19
  16.1 15.1 %collective-permute-start.11 = (bf16[96,384]{1,0:T(8,128)(2,1)S(1)}, bf16[96,384]{1,0:T(8,128)(2,1)S(1)}, u32[]{:S(2)}, u32[]{:S(2)}) collective-permute-start(bf16[96,384]{1,0:T(8,128)(2,1)S(1)} %get-tuple-element.67), channel_id=1, source_target_pairs={{0,2},{1,3},{2,0},{3,1},{4,6},{5,7},{6,4},{7,5},{8,10},{9,11},{10,... | collective-permute-start | bytes 221192 | tf_op jit(solution)/shard_map/ppermute | solution.py:19
  16.2 6.2 %collective-permute-start.5 = (bf16[96,384]{1,0:T(8,128)(2,1)S(1)}, bf16[96,384]{1,0:T(8,128)(2,1)S(1)}, u32[]{:S(2)}, u32[]{:S(2)}) collective-permute-start(bf16[96,384]{1,0:T(8,128)(2,1)S(1)} %get-tuple-element.69), channel_id=1, source_target_pairs={{0,3},{1,2},{2,1},{3,0},{4,7},{5,6},{6,5},{7,4},{8,11},{9,10},{10,... | collective-permute-start | bytes 221192 | tf_op jit(solution)/shard_map/ppermute | solution.py:19
  22.4 5.5 %collective-permute-start.7 = (bf16[96,384]{1,0:T(8,128)(2,1)S(1)}, bf16[96,384]{1,0:T(8,128)(2,1)S(1)}, u32[]{:S(2)}, u32[]{:S(2)}) collective-permute-start(bf16[96,384]{1,0:T(8,128)(2,1)S(1)} %get-tuple-element.69), channel_id=1, source_target_pairs={{0,2},{1,3},{2,0},{3,1},{4,6},{5,7},{6,4},{7,5},{8,10},{9,11},{10,... | collective-permute-start | bytes 221192 | tf_op jit(solution)/shard_map/ppermute | solution.py:19
  23.6 11.8 %collective-permute-start.17 = (f32[48,768]{1,0:T(8,128)S(1)}, f32[48,768]{1,0:T(8,128)S(1)}, u32[]{:S(2)}, u32[]{:S(2)}) collective-permute-start(f32[48,768]{1,0:T(8,128)S(1)} %get-tuple-element.50), channel_id=1, source_target_pairs={{0,4},{1,5},{2,6},{3,7},{4,0},{5,1},{6,2},{7,3},{8,12},{9,13},{10,... | collective-permute-start | bytes 442376 | tf_op jit(solution)/shard_map/ppermute | solution.py:19
  29.5 6.8 %collective-permute-start.12 = (bf16[384,384]{1,0:T(8,128)(2,1)S(1)}, bf16[384,384]{1,0:T(8,128)(2,1)S(1)}, u32[]{:S(2)}, u32[]{:S(2)}) collective-permute-start(bf16[384,384]{1,0:T(8,128)(2,1)S(1)} %get-tuple-element.47), channel_id=1, source_target_pairs={{0,16},{8,24},{16,0},{24,8},{1,17},{9,25},{17,1},{25,9},{2,18},{10... | collective-permute-start | bytes 884744 | tf_op jit(solution)/shard_map/ppermute | solution.py:19
  36.4 6.2 %collective-permute-start.13 = (bf16[96,384]{1,0:T(8,128)(2,1)S(1)}, bf16[96,384]{1,0:T(8,128)(2,1)S(1)}, u32[]{:S(2)}, u32[]{:S(2)}) collective-permute-start(bf16[96,384]{1,0:T(8,128)(2,1)S(1)} %get-tuple-element.79), channel_id=1, source_target_pairs={{0,3},{1,2},{2,1},{3,0},{4,7},{5,6},{6,5},{7,4},{8,11},{9,10},{10,... | collective-permute-start | bytes 221192 | tf_op jit(solution)/shard_map/ppermute | solution.py:19
  37.8 5.8 %collective-permute-start.14 = (bf16[96,384]{1,0:T(8,128)(2,1)S(1)}, bf16[96,384]{1,0:T(8,128)(2,1)S(1)}, u32[]{:S(2)}, u32[]{:S(2)}) collective-permute-start(bf16[96,384]{1,0:T(8,128)(2,1)S(1)} %get-tuple-element.81), channel_id=1, source_target_pairs={{0,1},{1,0},{2,3},{3,2},{4,5},{5,4},{6,7},{7,6},{8,9},{9,8},{10,11... | collective-permute-start | bytes 221192 | tf_op jit(solution)/shard_map/ppermute | solution.py:19
  38.7 5.0 %collective-permute-start.15 = (bf16[96,384]{1,0:T(8,128)(2,1)S(1)}, bf16[96,384]{1,0:T(8,128)(2,1)S(1)}, u32[]{:S(2)}, u32[]{:S(2)}) collective-permute-start(bf16[96,384]{1,0:T(8,128)(2,1)S(1)} %get-tuple-element.80), channel_id=1, source_target_pairs={{0,2},{1,3},{2,0},{3,1},{4,6},{5,7},{6,4},{7,5},{8,10},{9,11},{10,... | collective-permute-start | bytes 221192 | tf_op jit(solution)/shard_map/ppermute | solution.py:19
  40.0 5.8 %collective-permute-start.21 = (bf16[96,384]{1,0:T(8,128)(2,1)S(1)}, bf16[96,384]{1,0:T(8,128)(2,1)S(1)}, u32[]{:S(2)}, u32[]{:S(2)}) collective-permute-start(bf16[96,384]{1,0:T(8,128)(2,1)S(1)} %get-tuple-element.76), channel_id=1, source_target_pairs={{0,3},{1,2},{2,1},{3,0},{4,7},{5,6},{6,5},{7,4},{8,11},{9,10},{10,... | collective-permute-start | bytes 221192 | tf_op jit(solution)/shard_map/ppermute | solution.py:19
  41.4 4.7 %collective-permute-start.22 = (bf16[96,384]{1,0:T(8,128)(2,1)S(1)}, bf16[96,384]{1,0:T(8,128)(2,1)S(1)}, u32[]{:S(2)}, u32[]{:S(2)}) collective-permute-start(bf16[96,384]{1,0:T(8,128)(2,1)S(1)} %get-tuple-element.78), channel_id=1, source_target_pairs={{0,1},{1,0},{2,3},{3,2},{4,5},{5,4},{6,7},{7,6},{8,9},{9,8},{10,11... | collective-permute-start | bytes 221192 | tf_op jit(solution)/shard_map/ppermute | solution.py:19
  42.6 4.5 %collective-permute-start.23 = (bf16[96,384]{1,0:T(8,128)(2,1)S(1)}, bf16[96,384]{1,0:T(8,128)(2,1)S(1)}, u32[]{:S(2)}, u32[]{:S(2)}) collective-permute-start(bf16[96,384]{1,0:T(8,128)(2,1)S(1)} %get-tuple-element.77), channel_id=1, source_target_pairs={{0,2},{1,3},{2,0},{3,1},{4,6},{5,7},{6,4},{7,5},{8,10},{9,11},{10,... | collective-permute-start | bytes 221192 | tf_op jit(solution)/shard_map/ppermute | solution.py:19
  43.8 5.8 %collective-permute-start.16 = (bf16[96,384]{1,0:T(8,128)(2,1)S(1)}, bf16[96,384]{1,0:T(8,128)(2,1)S(1)}, u32[]{:S(2)}, u32[]{:S(2)}) collective-permute-start(bf16[96,384]{1,0:T(8,128)(2,1)S(1)} %add_convert_fusion.3), channel_id=1, source_target_pairs={{0,4},{1,5},{2,6},{3,7},{4,0},{5,1},{6,2},{7,3},{8,12},{9,13},{10,... | collective-permute-start | bytes 221192 | tf_op jit(solution)/shard_map/ppermute | solution.py:19
  47.2 6.1 %collective-permute-start.24 = (bf16[96,384]{1,0:T(8,128)(2,1)S(1)}, bf16[96,384]{1,0:T(8,128)(2,1)S(1)}, u32[]{:S(2)}, u32[]{:S(2)}) collective-permute-start(bf16[96,384]{1,0:T(8,128)(2,1)S(1)} %add_convert_fusion.2), channel_id=1, source_target_pairs={{0,4},{1,5},{2,6},{3,7},{4,0},{5,1},{6,2},{7,3},{8,12},{9,13},{10,... | collective-permute-start | bytes 221192 | tf_op jit(solution)/shard_map/ppermute | solution.py:19
  49.6 5.4 %collective-permute-start.18 = (bf16[96,384]{1,0:T(8,128)(2,1)S(1)}, bf16[96,384]{1,0:T(8,128)(2,1)S(1)}, u32[]{:S(2)}, u32[]{:S(2)}) collective-permute-start(bf16[96,384]{1,0:T(8,128)(2,1)S(1)} %get-tuple-element.65), channel_id=1, source_target_pairs={{0,3},{1,2},{2,1},{3,0},{4,7},{5,6},{6,5},{7,4},{8,11},{9,10},{10,... | collective-permute-start | bytes 221192 | tf_op jit(solution)/shard_map/ppermute | solution.py:19
  51.2 7.4 %collective-permute-start.19 = (bf16[96,384]{1,0:T(8,128)(2,1)S(1)}, bf16[96,384]{1,0:T(8,128)(2,1)S(1)}, u32[]{:S(2)}, u32[]{:S(2)}) collective-permute-start(bf16[96,384]{1,0:T(8,128)(2,1)S(1)} %get-tuple-element.65), channel_id=1, source_target_pairs={{0,1},{1,0},{2,3},{3,2},{4,5},{5,4},{6,7},{7,6},{8,9},{9,8},{10,11... | collective-permute-start | bytes 221192 | tf_op jit(solution)/shard_map/ppermute | solution.py:19
  52.4 6.2 %collective-permute-start.20 = (bf16[96,384]{1,0:T(8,128)(2,1)S(1)}, bf16[96,384]{1,0:T(8,128)(2,1)S(1)}, u32[]{:S(2)}, u32[]{:S(2)}) collective-permute-start(bf16[96,384]{1,0:T(8,128)(2,1)S(1)} %get-tuple-element.65), channel_id=1, source_target_pairs={{0,2},{1,3},{2,0},{3,1},{4,6},{5,7},{6,4},{7,5},{8,10},{9,11},{10,... | collective-permute-start | bytes 221192 | tf_op jit(solution)/shard_map/ppermute | solution.py:19
  55.0 7.5 %collective-permute-start.25 = (bf16[96,384]{1,0:T(8,128)(2,1)S(1)}, bf16[96,384]{1,0:T(8,128)(2,1)S(1)}, u32[]{:S(2)}, u32[]{:S(2)}) collective-permute-start(bf16[96,384]{1,0:T(8,128)(2,1)S(1)} %fusion.3), channel_id=1, source_target_pairs={{0,3},{1,2},{2,1},{3,0},{4,7},{5,6},{6,5},{7,4},{8,11},{9,10},{10,... | collective-permute-start | bytes 221192 | tf_op jit(solution)/shard_map/ppermute | solution.py:19
  57.1 5.5 %collective-permute-start.26 = (bf16[96,384]{1,0:T(8,128)(2,1)S(1)}, bf16[96,384]{1,0:T(8,128)(2,1)S(1)}, u32[]{:S(2)}, u32[]{:S(2)}) collective-permute-start(bf16[96,384]{1,0:T(8,128)(2,1)S(1)} %fusion.3), channel_id=1, source_target_pairs={{0,1},{1,0},{2,3},{3,2},{4,5},{5,4},{6,7},{7,6},{8,9},{9,8},{10,11... | collective-permute-start | bytes 221192 | tf_op jit(solution)/shard_map/ppermute | solution.py:19
  58.0 4.6 %collective-permute-start.27 = (bf16[96,384]{1,0:T(8,128)(2,1)S(1)}, bf16[96,384]{1,0:T(8,128)(2,1)S(1)}, u32[]{:S(2)}, u32[]{:S(2)}) collective-permute-start(bf16[96,384]{1,0:T(8,128)(2,1)S(1)} %fusion.3), channel_id=1, source_target_pairs={{0,2},{1,3},{2,0},{3,1},{4,6},{5,7},{6,4},{7,5},{8,10},{9,11},{10,... | collective-permute-start | bytes 221192 | tf_op jit(solution)/shard_map/ppermute | solution.py:19
  60.2 7.0 %collective-permute-start.28 = (bf16[384,384]{1,0:T(8,128)(2,1)S(1)}, bf16[384,384]{1,0:T(8,128)(2,1)S(1)}, u32[]{:S(2)}, u32[]{:S(2)}) collective-permute-start(bf16[384,384]{1,0:T(8,128)(2,1)S(1)} %get-tuple-element.57), channel_id=1, source_target_pairs={{0,16},{8,24},{16,0},{24,8},{1,17},{9,25},{17,1},{25,9},{2,18},{10... | collective-permute-start | bytes 884744 | tf_op jit(solution)/shard_map/ppermute | solution.py:19
  67.3 6.5 %collective-permute-start.33 = (bf16[96,384]{1,0:T(8,128)(2,1)S(1)}, bf16[96,384]{1,0:T(8,128)(2,1)S(1)}, u32[]{:S(2)}, u32[]{:S(2)}) collective-permute-start(bf16[96,384]{1,0:T(8,128)(2,1)S(1)} %get-tuple-element.70), channel_id=1, source_target_pairs={{0,3},{1,2},{2,1},{3,0},{4,7},{5,6},{6,5},{7,4},{8,11},{9,10},{10,... | collective-permute-start | bytes 221192 | tf_op jit(solution)/shard_map/ppermute | solution.py:19
  69.3 5.2 %collective-permute-start.34 = (bf16[96,384]{1,0:T(8,128)(2,1)S(1)}, bf16[96,384]{1,0:T(8,128)(2,1)S(1)}, u32[]{:S(2)}, u32[]{:S(2)}) collective-permute-start(bf16[96,384]{1,0:T(8,128)(2,1)S(1)} %get-tuple-element.72), channel_id=1, source_target_pairs={{0,1},{1,0},{2,3},{3,2},{4,5},{5,4},{6,7},{7,6},{8,9},{9,8},{10,11... | collective-permute-start | bytes 221192 | tf_op jit(solution)/shard_map/ppermute | solution.py:19
  70.9 6.1 %collective-permute-start.29 = (bf16[96,384]{1,0:T(8,128)(2,1)S(1)}, bf16[96,384]{1,0:T(8,128)(2,1)S(1)}, u32[]{:S(2)}, u32[]{:S(2)}) collective-permute-start(bf16[96,384]{1,0:T(8,128)(2,1)S(1)} %get-tuple-element.73), channel_id=1, source_target_pairs={{0,3},{1,2},{2,1},{3,0},{4,7},{5,6},{6,5},{7,4},{8,11},{9,10},{10,... | collective-permute-start | bytes 221192 | tf_op jit(solution)/shard_map/ppermute | solution.py:19
  74.7 5.7 %collective-permute-start.36 = (bf16[48,384]{1,0:T(8,128)(2,1)S(1)}, bf16[48,384]{1,0:T(8,128)(2,1)S(1)}, u32[]{:S(2)}, u32[]{:S(2)}) collective-permute-start(bf16[48,384]{1,0:T(8,128)(2,1)S(1)} %constant_dynamic-slice_fusion), channel_id=1, source_target_pairs={{0,4},{1,5},{2,6},{3,7},{4,0},{5,1},{6,2},{7,3},{8,12},{9,13},{10,... | collective-permute-start | bytes 110600 | tf_op jit(solution)/shard_map/ppermute | solution.py:19
  78.2 5.3 %collective-permute-start.32 = (bf16[48,384]{1,0:T(8,128)(2,1)S(1)}, bf16[48,384]{1,0:T(8,128)(2,1)S(1)}, u32[]{:S(2)}, u32[]{:S(2)}) collective-permute-start(bf16[48,384]{1,0:T(8,128)(2,1)S(1)} %constant_dynamic-slice_fusion.4), channel_id=1, source_target_pairs={{0,4},{1,5},{2,6},{3,7},{4,0},{5,1},{6,2},{7,3},{8,12},{9,13},{10,... | collective-permute-start | bytes 110600 | tf_op jit(solution)/shard_map/ppermute | solution.py:19
  (11 other events, 49.7 us)

commit v5 on v4

--- a/solution.py
+++ b/solution.py
@@ -280,8 +280,9 @@
     moves = (offsets, swap(offsets, "sec", 1))
     *outer_weights, passed = arrange(0, moves, lefts, rights, start)
     together = beside(start, passed)
-    vectors = [gather_all(together[:, :width])[0], gather_all(together[:, width:])[0]]
-    own_diagonal = diagonal[0]
+    together, own_diagonal = lax.optimization_barrier((together, diagonal[0]))
+    together, _ = gather_all(together)
+    vectors = [together[:, :width], together[:, width:]]
     *inner_weights, slots = arrange(1, moves, lefts, rights, own_diagonal, swap(own_diagonal, "sec", 1))
     both_diagonals = beside(slots)
     own_diagonals = [slots[:, :width], slots[:, width:]]

time: 85.5 us -> 84.4 us (0.987)
  waiting for transfers between devices: 14.7 us -> 13 us
    ppermute x38 -> x35, waiting for transfers between devices: 14.7 us -> 13 us  [swap(): return lax.ppermute(block, axis, route)]
    ppermute x38 -> x35, starting transfers between devices: 49.7 us -> 49.3 us  [swap(): return lax.ppermute(block, axis, route)]
  transfers between devices with their start and end apart: 38 -> 35, of which waited for: 17 -> 13; matrix products, arithmetic and copies ran while one was open for 2% -> 2% of each run, Pallas kernels for 17% -> 19%
where the time goes in v5:
time: 84.4 us; the launch traced here: 84.2 us
  starting transfers between devices  49.3 us (58%)
  Pallas kernels  15.9 us (19%)
  waiting for transfers between devices  13 us (15%)
  local copies, waits for them, and re-layouts  3.82 us (5%)
  other arithmetic  1.83 us (2%)
    ppermute x35, starting transfers between devices, swap(): return lax.ppermute(block, axis, route)  49.3 us
    ppermute x35, waiting for transfers between devices, swap(): return lax.ppermute(block, axis, route)  13 us
    pallas_call x6, Pallas kernels, call(): pl.pallas_call(kernel, out_shape=shapes, in_specs=[VMEM] * (4 + len(more)...  12.2 us
    pallas_call x2, Pallas kernels, arrange(): pl.pallas_call(functools.partial(arrange_kernel, slot), out_shape=(shape,...  3.49 us
    unnamed x11, local copies, waits for them, and re-layouts  3.31 us
  transfers between devices with their start and end apart: 35, of which 13 were waited for; matrix products, arithmetic and copies ran while one was open for 2% of the time, Pallas kernels for 19%

profile of v5, /device:TPU:0, one launch (start us, length us, event | category | flops | bytes accessed | tf_op | source)
XLA Modules:
  0.0 84.2 jit_solution(17224640501465337434)
XLA Ops:
  4.1 3.7 %collective-permute-start.4 = (bf16[48,768]{1,0:T(8,128)(2,1)S(1)}, bf16[48,768]{1,0:T(8,128)(2,1)S(1)}, u32[]{:S(2)}, u32[]{:S(2)}) collective-permute-start(bf16[48,768]{1,0:T(8,128)(2,1)S(1)} %pad_maximum_fusion.2.rest_0_), channel_id=1, source_target_pairs={{0,4},{1,5},{2,6},{3,7},{4,0},{5,1},{6,2},{7,3},{8,12},{9,13},{10,... | collective-permute-start | bytes 221192 | tf_op jit(solution)/shard_map/ppermute | solution.py:19
  7.9 1.3 %copy-done = bf16[4,384,384]{2,1,0:T(8,128)(2,1)S(1)} copy-done((bf16[4,384,384]{2,1,0:T(8,128)(2,1)S(1)}, bf16[4,384,384]{2,1,0:T(8,128)(2,1)}, u32[]{:S(2)}) %copy-start) | copy-done | bytes 1179672
  9.1 1.3 %copy-done.2 = bf16[4,384,384]{2,1,0:T(8,128)(2,1)S(1)} copy-done((bf16[4,384,384]{2,1,0:T(8,128)(2,1)S(1)}, bf16[4,384,384]{2,1,0:T(8,128)(2,1)}, u32[]{:S(2)}) %copy-start.2) | copy-done | bytes 1179672
  10.4 1.7 %arrange.2 = (bf16[2,384,1536]{2,1,0:T(8,128)(2,1)S(1)}, bf16[2,384,1536]{2,1,0:T(8,128)(2,1)S(1)}, s32[2,8,128]{2,1,0:T(8,128)S(1)}, bf16[48,768]{1,0:T(8,128)(2,1)S(1)}) custom-call(s32[4,2]{1,0:T(4,128)S(1)} %copy.7.own_steps, s32[4,2]{1,0:T(4,128)S(1)} %collective-permute-done.other_steps, bf16[4,384,384]{2,1,0:T(8,128)(2,1)S(1)} %copy-done, ...), custom_call_target="tpu_custom_call" | custom-call | flops 5000000000 | bytes 1 | tf_op jit(solution)/shard_map/arrange/pallas_call | solution.py:65
  12.2 3.3 %collective-permute-start.5 = (bf16[96,768]{1,0:T(8,128)(2,1)S(1)}, bf16[96,768]{1,0:T(8,128)(2,1)S(1)}, u32[]{:S(2)}, u32[]{:S(2)}) collective-permute-start(bf16[96,768]{1,0:T(8,128)(2,1)S(1)} %pad_maximum_fusion.1), channel_id=1, source_target_pairs={{0,3},{1,2},{2,1},{3,0},{4,7},{5,6},{6,5},{7,4},{8,11},{9,10},{10,... | collective-permute-start | bytes 442376 | tf_op jit(solution)/shard_map/ppermute | solution.py:19
  17.4 1.7 %arrange.3 = (bf16[2,384,1536]{2,1,0:T(8,128)(2,1)S(1)}, bf16[2,384,1536]{2,1,0:T(8,128)(2,1)S(1)}, s32[2,8,128]{2,1,0:T(8,128)S(1)}, f32[48,768]{1,0:T(8,128)S(1)}) custom-call(s32[4,2]{1,0:T(4,128)S(1)} %copy.7.own_steps, s32[4,2]{1,0:T(4,128)S(1)} %collective-permute-done.other_steps, bf16[4,384,384]{2,1,0:T(8,128)(2,1)S(1)} %copy-done.1, ...), custom_call_target="tpu_custom_call" | custom-call | flops 5000000000 | bytes 1 | tf_op jit(solution)/shard_map/arrange/pallas_call | solution.py:65
  19.2 3.0 %collective-permute-start.14 = (f32[48,768]{1,0:T(8,128)S(1)}, f32[48,768]{1,0:T(8,128)S(1)}, u32[]{:S(2)}, u32[]{:S(2)}) collective-permute-start(f32[48,768]{1,0:T(8,128)S(1)} %get-tuple-element.54), channel_id=1, source_target_pairs={{0,4},{1,5},{2,6},{3,7},{4,0},{5,1},{6,2},{7,3},{8,12},{9,13},{10,... | collective-permute-start | bytes 442376 | tf_op jit(solution)/shard_map/ppermute | solution.py:19
  23.1 1.6 %first.2 = (bf16[384,384]{1,0:T(8,128)(2,1)S(1)}, f32[384,384]{1,0:T(8,128)S(1)}) custom-call(s32[2,8,128]{2,1,0:T(8,128)S(1)} %get-tuple-element.38.counts, bf16[384,384]{1,0:T(8,128)(2,1)S(1)} %get-tuple-element.71.vector, bf16[2,384,1536]{2,1,0:T(8,128)(2,1)S(1)} %get-tuple-element.41.lefts, bf16[2,384,1536]{2,1,0:T(8,128)(2,1)S(1)} %get-tuple-element.42.rights), custom_call_target="tpu_custom_call" | custom-call | flops 5000000000 | bytes 1 | tf_op jit(solution)/shard_map/first/pallas_call | solution.py:196
  24.7 1.6 %collective-permute-start.9 = (bf16[384,384]{1,0:T(8,128)(2,1)S(1)}, bf16[384,384]{1,0:T(8,128)(2,1)S(1)}, u32[]{:S(2)}, u32[]{:S(2)}) collective-permute-start(bf16[384,384]{1,0:T(8,128)(2,1)S(1)} %get-tuple-element.51), channel_id=1, source_target_pairs={{0,16},{8,24},{16,0},{24,8},{1,17},{9,25},{17,1},{25,9},{2,18},{10... | collective-permute-start | bytes 884744 | tf_op jit(solution)/shard_map/ppermute | solution.py:19
  26.3 2.7 %inner.2 = (f32[384,384]{1,0:T(8,128)S(1)}, f32[384,384]{1,0:T(8,128)S(1)}) custom-call(s32[2,8,128]{2,1,0:T(8,128)S(1)} %get-tuple-element.45.counts, bf16[384,384]{1,0:T(8,128)(2,1)S(1)} %get-tuple-element.70.vector, bf16[2,384,1536]{2,1,0:T(8,128)(2,1)S(1)} %get-tuple-element.46.lefts, bf16[2,384,1536]{2,1,0:T(8,128)(2,1)S(1)} %get-tuple-element.47.rights), custom_call_target="tpu_custom_call" | custom-call | flops 5000000000 | bytes 1 | tf_op jit(solution)/shard_map/inner/pallas_call | solution.py:196
  29.0 1.8 %second.2 = (f32[384,384]{1,0:T(8,128)S(1)}, f32[384,384]{1,0:T(8,128)S(1)}) custom-call(s32[2,8,128]{2,1,0:T(8,128)S(1)} %get-tuple-element.38.counts, bf16[384,384]{1,0:T(8,128)(2,1)S(1)} %get-tuple-element.71.vector, bf16[2,384,1536]{2,1,0:T(8,128)(2,1)S(1)} %get-tuple-element.41.lefts, bf16[2,384,1536]{2,1,0:T(8,128)(2,1)S(1)} %get-tuple-element.42.rights, ...), custom_call_target="tpu_custom_call" | custom-call | flops 500000000 | bytes 1 | tf_op jit(solution)/shard_map/second/pallas_call | solution.py:196
  30.9 2.7 %collective-permute-done.9.arrived = bf16[384,384]{1,0:T(8,128)(2,1)S(1)} collective-permute-done((bf16[384,384]{1,0:T(8,128)(2,1)S(1)}, bf16[384,384]{1,0:T(8,128)(2,1)S(1)}, u32[]{:S(2)}, u32[]{:S(2)}) %collective-permute-start.9) | collective-permute-done | bytes 294944 | tf_op jit(solution)/shard_map/ppermute | solution.py:19
  33.7 1.9 %collective-permute-start.10 = (bf16[96,384]{1,0:T(8,128)(2,1)S(1)}, bf16[96,384]{1,0:T(8,128)(2,1)S(1)}, u32[]{:S(2)}, u32[]{:S(2)}) collective-permute-start(bf16[96,384]{1,0:T(8,128)(2,1)S(1)} %get-tuple-element.81), channel_id=1, source_target_pairs={{0,3},{1,2},{2,1},{3,0},{4,7},{5,6},{6,5},{7,4},{8,11},{9,10},{10,... | collective-permute-start | bytes 221192 | tf_op jit(solution)/shard_map/ppermute | solution.py:19
  35.5 1.4 %collective-permute-start.11 = (bf16[96,384]{1,0:T(8,128)(2,1)S(1)}, bf16[96,384]{1,0:T(8,128)(2,1)S(1)}, u32[]{:S(2)}, u32[]{:S(2)}) collective-permute-start(bf16[96,384]{1,0:T(8,128)(2,1)S(1)} %get-tuple-element.83), channel_id=1, source_target_pairs={{0,1},{1,0},{2,3},{3,2},{4,5},{5,4},{6,7},{7,6},{8,9},{9,8},{10,11... | collective-permute-start | bytes 221192 | tf_op jit(solution)/shard_map/ppermute | solution.py:19
  37.2 1.9 %collective-permute-start.18 = (bf16[96,384]{1,0:T(8,128)(2,1)S(1)}, bf16[96,384]{1,0:T(8,128)(2,1)S(1)}, u32[]{:S(2)}, u32[]{:S(2)}) collective-permute-start(bf16[96,384]{1,0:T(8,128)(2,1)S(1)} %get-tuple-element.78), channel_id=1, source_target_pairs={{0,3},{1,2},{2,1},{3,0},{4,7},{5,6},{6,5},{7,4},{8,11},{9,10},{10,... | collective-permute-start | bytes 221192 | tf_op jit(solution)/shard_map/ppermute | solution.py:19
  39.1 1.4 %collective-permute-start.19 = (bf16[96,384]{1,0:T(8,128)(2,1)S(1)}, bf16[96,384]{1,0:T(8,128)(2,1)S(1)}, u32[]{:S(2)}, u32[]{:S(2)}) collective-permute-start(bf16[96,384]{1,0:T(8,128)(2,1)S(1)} %get-tuple-element.80), channel_id=1, source_target_pairs={{0,1},{1,0},{2,3},{3,2},{4,5},{5,4},{6,7},{7,6},{8,9},{9,8},{10,11... | collective-permute-start | bytes 221192 | tf_op jit(solution)/shard_map/ppermute | solution.py:19
  41.8 2.6 %collective-permute-start.13 = (bf16[96,384]{1,0:T(8,128)(2,1)S(1)}, bf16[96,384]{1,0:T(8,128)(2,1)S(1)}, u32[]{:S(2)}, u32[]{:S(2)}) collective-permute-start(bf16[96,384]{1,0:T(8,128)(2,1)S(1)} %add_convert_fusion.3), channel_id=1, source_target_pairs={{0,4},{1,5},{2,6},{3,7},{4,0},{5,1},{6,2},{7,3},{8,12},{9,13},{10,... | collective-permute-start | bytes 221192 | tf_op jit(solution)/shard_map/ppermute | solution.py:19
  44.9 3.3 %collective-permute-start.21 = (bf16[96,384]{1,0:T(8,128)(2,1)S(1)}, bf16[96,384]{1,0:T(8,128)(2,1)S(1)}, u32[]{:S(2)}, u32[]{:S(2)}) collective-permute-start(bf16[96,384]{1,0:T(8,128)(2,1)S(1)} %add_convert_fusion.2), channel_id=1, source_target_pairs={{0,4},{1,5},{2,6},{3,7},{4,0},{5,1},{6,2},{7,3},{8,12},{9,13},{10,... | collective-permute-start | bytes 221192 | tf_op jit(solution)/shard_map/ppermute | solution.py:19
  50.7 1.9 %collective-permute-start.17 = (bf16[96,384]{1,0:T(8,128)(2,1)S(1)}, bf16[96,384]{1,0:T(8,128)(2,1)S(1)}, u32[]{:S(2)}, u32[]{:S(2)}) collective-permute-start(bf16[96,384]{1,0:T(8,128)(2,1)S(1)} %get-tuple-element.69), channel_id=1, source_target_pairs={{0,2},{1,3},{2,0},{3,1},{4,6},{5,7},{6,4},{7,5},{8,10},{9,11},{10,... | collective-permute-start | bytes 221192 | tf_op jit(solution)/shard_map/ppermute | solution.py:19
  52.7 2.0 %collective-permute-done.15 = bf16[96,384]{1,0:T(8,128)(2,1)S(1)} collective-permute-done((bf16[96,384]{1,0:T(8,128)(2,1)S(1)}, bf16[96,384]{1,0:T(8,128)(2,1)S(1)}, u32[]{:S(2)}, u32[]{:S(2)}) %collective-permute-start.15) | collective-permute-done | bytes 73760 | tf_op jit(solution)/shard_map/ppermute | solution.py:19
  56.8 1.4 %collective-permute-start.24 = (bf16[96,384]{1,0:T(8,128)(2,1)S(1)}, bf16[96,384]{1,0:T(8,128)(2,1)S(1)}, u32[]{:S(2)}, u32[]{:S(2)}) collective-permute-start(bf16[96,384]{1,0:T(8,128)(2,1)S(1)} %fusion.3), channel_id=1, source_target_pairs={{0,2},{1,3},{2,0},{3,1},{4,6},{5,7},{6,4},{7,5},{8,10},{9,11},{10,... | collective-permute-start | bytes 221192 | tf_op jit(solution)/shard_map/ppermute | solution.py:19
  58.2 1.6 %first.3 = (bf16[384,384]{1,0:T(8,128)(2,1)S(1)}, f32[384,384]{1,0:T(8,128)S(1)}) custom-call(s32[2,8,128]{2,1,0:T(8,128)S(1)} %get-tuple-element.38.counts, bf16[384,384]{1,0:T(8,128)(2,1)S(1)} %constant_dynamic-update-slice_fusion.4.vector, bf16[2,384,1536]{2,1,0:T(8,128)(2,1)S(1)} %get-tuple-element.41.lefts, ...), custom_call_target="tpu_custom_call" | custom-call | flops 5000000000 | bytes 1 | tf_op jit(solution)/shard_map/first/pallas_call | solution.py:196
  59.8 1.6 %collective-permute-start.25 = (bf16[384,384]{1,0:T(8,128)(2,1)S(1)}, bf16[384,384]{1,0:T(8,128)(2,1)S(1)}, u32[]{:S(2)}, u32[]{:S(2)}) collective-permute-start(bf16[384,384]{1,0:T(8,128)(2,1)S(1)} %get-tuple-element.61), channel_id=1, source_target_pairs={{0,16},{8,24},{16,0},{24,8},{1,17},{9,25},{17,1},{25,9},{2,18},{10... | collective-permute-start | bytes 884744 | tf_op jit(solution)/shard_map/ppermute | solution.py:19
  61.6 3.0 %inner.3 = (f32[384,384]{1,0:T(8,128)S(1)}, f32[384,384]{1,0:T(8,128)S(1)}) custom-call(s32[2,8,128]{2,1,0:T(8,128)S(1)} %get-tuple-element.45.counts, bf16[384,384]{1,0:T(8,128)(2,1)S(1)} %constant_dynamic-update-slice_fusion.vector, bf16[2,384,1536]{2,1,0:T(8,128)(2,1)S(1)} %get-tuple-element.46.lefts, bf16[2,384,1536]{2,1,0:T(8,128)(2,1)S(1)} %get-tuple-element.47.rights), custom_call_target="tpu_custom_call" | custom-call | flops 5000000000 | bytes 1 | tf_op jit(solution)/shard_map/inner/pallas_call | solution.py:196
  64.5 1.6 %second.3 = (f32[384,384]{1,0:T(8,128)S(1)}, f32[384,384]{1,0:T(8,128)S(1)}) custom-call(s32[2,8,128]{2,1,0:T(8,128)S(1)} %get-tuple-element.38.counts, bf16[384,384]{1,0:T(8,128)(2,1)S(1)} %constant_dynamic-update-slice_fusion.4.vector, bf16[2,384,1536]{2,1,0:T(8,128)(2,1)S(1)} %get-tuple-element.41.lefts, ...), custom_call_target="tpu_custom_call" | custom-call | flops 500000000 | bytes 1 | tf_op jit(solution)/shard_map/second/pallas_call | solution.py:196
  66.7 1.4 %collective-permute-start.30 = (bf16[96,384]{1,0:T(8,128)(2,1)S(1)}, bf16[96,384]{1,0:T(8,128)(2,1)S(1)}, u32[]{:S(2)}, u32[]{:S(2)}) collective-permute-start(bf16[96,384]{1,0:T(8,128)(2,1)S(1)} %get-tuple-element.72), channel_id=1, source_target_pairs={{0,3},{1,2},{2,1},{3,0},{4,7},{5,6},{6,5},{7,4},{8,11},{9,10},{10,... | collective-permute-start | bytes 221192 | tf_op jit(solution)/shard_map/ppermute | solution.py:19
  69.0 1.3 %collective-permute-start.32 = (bf16[96,384]{1,0:T(8,128)(2,1)S(1)}, bf16[96,384]{1,0:T(8,128)(2,1)S(1)}, u32[]{:S(2)}, u32[]{:S(2)}) collective-permute-start(bf16[96,384]{1,0:T(8,128)(2,1)S(1)} %get-tuple-element.73), channel_id=1, source_target_pairs={{0,2},{1,3},{2,0},{3,1},{4,6},{5,7},{6,4},{7,5},{8,10},{9,11},{10,... | collective-permute-start | bytes 221192 | tf_op jit(solution)/shard_map/ppermute | solution.py:19
  70.3 1.4 %collective-permute-start.26 = (bf16[96,384]{1,0:T(8,128)(2,1)S(1)}, bf16[96,384]{1,0:T(8,128)(2,1)S(1)}, u32[]{:S(2)}, u32[]{:S(2)}) collective-permute-start(bf16[96,384]{1,0:T(8,128)(2,1)S(1)} %get-tuple-element.75), channel_id=1, source_target_pairs={{0,3},{1,2},{2,1},{3,0},{4,7},{5,6},{6,5},{7,4},{8,11},{9,10},{10,... | collective-permute-start | bytes 221192 | tf_op jit(solution)/shard_map/ppermute | solution.py:19
  72.6 1.3 %collective-permute-start.28 = (bf16[96,384]{1,0:T(8,128)(2,1)S(1)}, bf16[96,384]{1,0:T(8,128)(2,1)S(1)}, u32[]{:S(2)}, u32[]{:S(2)}) collective-permute-start(bf16[96,384]{1,0:T(8,128)(2,1)S(1)} %get-tuple-element.76), channel_id=1, source_target_pairs={{0,2},{1,3},{2,0},{3,1},{4,6},{5,7},{6,4},{7,5},{8,10},{9,11},{10,... | collective-permute-start | bytes 221192 | tf_op jit(solution)/shard_map/ppermute | solution.py:19
  74.0 2.9 %collective-permute-start.33 = (bf16[48,384]{1,0:T(8,128)(2,1)S(1)}, bf16[48,384]{1,0:T(8,128)(2,1)S(1)}, u32[]{:S(2)}, u32[]{:S(2)}) collective-permute-start(bf16[48,384]{1,0:T(8,128)(2,1)S(1)} %constant_dynamic-slice_fusion), channel_id=1, source_target_pairs={{0,4},{1,5},{2,6},{3,7},{4,0},{5,1},{6,2},{7,3},{8,12},{9,13},{10,... | collective-permute-start | bytes 110600 | tf_op jit(solution)/shard_map/ppermute | solution.py:19
  77.0 3.2 %collective-permute-start.29 = (bf16[48,384]{1,0:T(8,128)(2,1)S(1)}, bf16[48,384]{1,0:T(8,128)(2,1)S(1)}, u32[]{:S(2)}, u32[]{:S(2)}) collective-permute-start(bf16[48,384]{1,0:T(8,128)(2,1)S(1)} %constant_dynamic-slice_fusion.4), channel_id=1, source_target_pairs={{0,4},{1,5},{2,6},{3,7},{4,0},{5,1},{6,2},{7,3},{8,12},{9,13},{10,... | collective-permute-start | bytes 110600 | tf_op jit(solution)/shard_map/ppermute | solution.py:19
  80.2 1.9 %collective-permute-done.29 = bf16[48,384]{1,0:T(8,128)(2,1)S(1)} collective-permute-done((bf16[48,384]{1,0:T(8,128)(2,1)S(1)}, bf16[48,384]{1,0:T(8,128)(2,1)S(1)}, u32[]{:S(2)}, u32[]{:S(2)}) %collective-permute-start.29) | collective-permute-done | bytes 36896 | tf_op jit(solution)/shard_map/ppermute | solution.py:19
  (94 shorter events, 18.7 us)
Async XLA Ops:
  2.4 5.4 %collective-permute-start.2 = (bf16[4,384,384]{2,1,0:T(8,128)(2,1)}, bf16[4,384,384]{2,1,0:T(8,128)(2,1)S(1)}, u32[]{:S(2)}, u32[]{:S(2)}) collective-permute-start(bf16[4,384,384]{2,1,0:T(8,128)(2,1)} %left_own.3), channel_id=1, source_target_pairs={{0,8},{8,0},{16,24},{24,16},{1,9},{9,1},{17,25},{25,17},{2,10},{10... | collective-permute-start | bytes 3538952 | tf_op jit(solution)/shard_map/ppermute | solution.py:19
  2.8 5.0 %collective-permute-start.3 = (bf16[4,384,384]{2,1,0:T(8,128)(2,1)}, bf16[4,384,384]{2,1,0:T(8,128)(2,1)S(1)}, u32[]{:S(2)}, u32[]{:S(2)}) collective-permute-start(bf16[4,384,384]{2,1,0:T(8,128)(2,1)} %right_own.3), channel_id=1, source_target_pairs={{0,8},{8,0},{16,24},{24,16},{1,9},{9,1},{17,25},{25,17},{2,10},{10... | collective-permute-start | bytes 3538952 | tf_op jit(solution)/shard_map/ppermute | solution.py:19
  3.7 4.1 %collective-permute-start = (s32[4,2]{1,0:T(4,128)S(1)}, s32[4,2]{1,0:T(4,128)S(1)}, u32[]{:S(2)}, u32[]{:S(2)}) collective-permute-start(s32[4,2]{1,0:T(4,128)S(1)} %copy.7.own_steps), channel_id=1, source_target_pairs={{0,8},{8,0},{16,24},{24,16},{1,9},{9,1},{17,25},{25,17},{2,10},{10... | collective-permute-start | bytes 104 | tf_op jit(solution)/shard_map/ppermute | solution.py:19
  4.1 8.1 %collective-permute-start.4 = (bf16[48,768]{1,0:T(8,128)(2,1)S(1)}, bf16[48,768]{1,0:T(8,128)(2,1)S(1)}, u32[]{:S(2)}, u32[]{:S(2)}) collective-permute-start(bf16[48,768]{1,0:T(8,128)(2,1)S(1)} %pad_maximum_fusion.2.rest_0_), channel_id=1, source_target_pairs={{0,4},{1,5},{2,6},{3,7},{4,0},{5,1},{6,2},{7,3},{8,12},{9,13},{10,... | collective-permute-start | bytes 221192 | tf_op jit(solution)/shard_map/ppermute | solution.py:19
  12.2 9.9 %collective-permute-start.5 = (bf16[96,768]{1,0:T(8,128)(2,1)S(1)}, bf16[96,768]{1,0:T(8,128)(2,1)S(1)}, u32[]{:S(2)}, u32[]{:S(2)}) collective-permute-start(bf16[96,768]{1,0:T(8,128)(2,1)S(1)} %pad_maximum_fusion.1), channel_id=1, source_target_pairs={{0,3},{1,2},{2,1},{3,0},{4,7},{5,6},{6,5},{7,4},{8,11},{9,10},{10,... | collective-permute-start | bytes 442376 | tf_op jit(solution)/shard_map/ppermute | solution.py:19
  15.5 7.3 %collective-permute-start.6 = (bf16[96,768]{1,0:T(8,128)(2,1)S(1)}, bf16[96,768]{1,0:T(8,128)(2,1)S(1)}, u32[]{:S(2)}, u32[]{:S(2)}) collective-permute-start(bf16[96,768]{1,0:T(8,128)(2,1)S(1)} %pad_maximum_fusion.1), channel_id=1, source_target_pairs={{0,1},{1,0},{2,3},{3,2},{4,5},{5,4},{6,7},{7,6},{8,9},{9,8},{10,11... | collective-permute-start | bytes 442376 | tf_op jit(solution)/shard_map/ppermute | solution.py:19
  16.0 7.0 %collective-permute-start.7 = (bf16[96,768]{1,0:T(8,128)(2,1)S(1)}, bf16[96,768]{1,0:T(8,128)(2,1)S(1)}, u32[]{:S(2)}, u32[]{:S(2)}) collective-permute-start(bf16[96,768]{1,0:T(8,128)(2,1)S(1)} %pad_maximum_fusion.1), channel_id=1, source_target_pairs={{0,2},{1,3},{2,0},{3,1},{4,6},{5,7},{6,4},{7,5},{8,10},{9,11},{10,... | collective-permute-start | bytes 442376 | tf_op jit(solution)/shard_map/ppermute | solution.py:19
  19.2 11.7 %collective-permute-start.14 = (f32[48,768]{1,0:T(8,128)S(1)}, f32[48,768]{1,0:T(8,128)S(1)}, u32[]{:S(2)}, u32[]{:S(2)}) collective-permute-start(f32[48,768]{1,0:T(8,128)S(1)} %get-tuple-element.54), channel_id=1, source_target_pairs={{0,4},{1,5},{2,6},{3,7},{4,0},{5,1},{6,2},{7,3},{8,12},{9,13},{10,... | collective-permute-start | bytes 442376 | tf_op jit(solution)/shard_map/ppermute | solution.py:19
  24.7 8.8 %collective-permute-start.9 = (bf16[384,384]{1,0:T(8,128)(2,1)S(1)}, bf16[384,384]{1,0:T(8,128)(2,1)S(1)}, u32[]{:S(2)}, u32[]{:S(2)}) collective-permute-start(bf16[384,384]{1,0:T(8,128)(2,1)S(1)} %get-tuple-element.51), channel_id=1, source_target_pairs={{0,16},{8,24},{16,0},{24,8},{1,17},{9,25},{17,1},{25,9},{2,18},{10... | collective-permute-start | bytes 884744 | tf_op jit(solution)/shard_map/ppermute | solution.py:19
  33.7 6.8 %collective-permute-start.10 = (bf16[96,384]{1,0:T(8,128)(2,1)S(1)}, bf16[96,384]{1,0:T(8,128)(2,1)S(1)}, u32[]{:S(2)}, u32[]{:S(2)}) collective-permute-start(bf16[96,384]{1,0:T(8,128)(2,1)S(1)} %get-tuple-element.81), channel_id=1, source_target_pairs={{0,3},{1,2},{2,1},{3,0},{4,7},{5,6},{6,5},{7,4},{8,11},{9,10},{10,... | collective-permute-start | bytes 221192 | tf_op jit(solution)/shard_map/ppermute | solution.py:19
  35.5 6.0 %collective-permute-start.11 = (bf16[96,384]{1,0:T(8,128)(2,1)S(1)}, bf16[96,384]{1,0:T(8,128)(2,1)S(1)}, u32[]{:S(2)}, u32[]{:S(2)}) collective-permute-start(bf16[96,384]{1,0:T(8,128)(2,1)S(1)} %get-tuple-element.83), channel_id=1, source_target_pairs={{0,1},{1,0},{2,3},{3,2},{4,5},{5,4},{6,7},{7,6},{8,9},{9,8},{10,11... | collective-permute-start | bytes 221192 | tf_op jit(solution)/shard_map/ppermute | solution.py:19
  36.9 4.8 %collective-permute-start.12 = (bf16[96,384]{1,0:T(8,128)(2,1)S(1)}, bf16[96,384]{1,0:T(8,128)(2,1)S(1)}, u32[]{:S(2)}, u32[]{:S(2)}) collective-permute-start(bf16[96,384]{1,0:T(8,128)(2,1)S(1)} %get-tuple-element.82), channel_id=1, source_target_pairs={{0,2},{1,3},{2,0},{3,1},{4,6},{5,7},{6,4},{7,5},{8,10},{9,11},{10,... | collective-permute-start | bytes 221192 | tf_op jit(solution)/shard_map/ppermute | solution.py:19
  37.2 7.2 %collective-permute-start.18 = (bf16[96,384]{1,0:T(8,128)(2,1)S(1)}, bf16[96,384]{1,0:T(8,128)(2,1)S(1)}, u32[]{:S(2)}, u32[]{:S(2)}) collective-permute-start(bf16[96,384]{1,0:T(8,128)(2,1)S(1)} %get-tuple-element.78), channel_id=1, source_target_pairs={{0,3},{1,2},{2,1},{3,0},{4,7},{5,6},{6,5},{7,4},{8,11},{9,10},{10,... | collective-permute-start | bytes 221192 | tf_op jit(solution)/shard_map/ppermute | solution.py:19
  39.1 5.3 %collective-permute-start.19 = (bf16[96,384]{1,0:T(8,128)(2,1)S(1)}, bf16[96,384]{1,0:T(8,128)(2,1)S(1)}, u32[]{:S(2)}, u32[]{:S(2)}) collective-permute-start(bf16[96,384]{1,0:T(8,128)(2,1)S(1)} %get-tuple-element.80), channel_id=1, source_target_pairs={{0,1},{1,0},{2,3},{3,2},{4,5},{5,4},{6,7},{7,6},{8,9},{9,8},{10,11... | collective-permute-start | bytes 221192 | tf_op jit(solution)/shard_map/ppermute | solution.py:19
  40.5 4.4 %collective-permute-start.20 = (bf16[96,384]{1,0:T(8,128)(2,1)S(1)}, bf16[96,384]{1,0:T(8,128)(2,1)S(1)}, u32[]{:S(2)}, u32[]{:S(2)}) collective-permute-start(bf16[96,384]{1,0:T(8,128)(2,1)S(1)} %get-tuple-element.79), channel_id=1, source_target_pairs={{0,2},{1,3},{2,0},{3,1},{4,6},{5,7},{6,4},{7,5},{8,10},{9,11},{10,... | collective-permute-start | bytes 221192 | tf_op jit(solution)/shard_map/ppermute | solution.py:19
  41.8 7.2 %collective-permute-start.13 = (bf16[96,384]{1,0:T(8,128)(2,1)S(1)}, bf16[96,384]{1,0:T(8,128)(2,1)S(1)}, u32[]{:S(2)}, u32[]{:S(2)}) collective-permute-start(bf16[96,384]{1,0:T(8,128)(2,1)S(1)} %add_convert_fusion.3), channel_id=1, source_target_pairs={{0,4},{1,5},{2,6},{3,7},{4,0},{5,1},{6,2},{7,3},{8,12},{9,13},{10,... | collective-permute-start | bytes 221192 | tf_op jit(solution)/shard_map/ppermute | solution.py:19
  44.9 7.7 %collective-permute-start.21 = (bf16[96,384]{1,0:T(8,128)(2,1)S(1)}, bf16[96,384]{1,0:T(8,128)(2,1)S(1)}, u32[]{:S(2)}, u32[]{:S(2)}) collective-permute-start(bf16[96,384]{1,0:T(8,128)(2,1)S(1)} %add_convert_fusion.2), channel_id=1, source_target_pairs={{0,4},{1,5},{2,6},{3,7},{4,0},{5,1},{6,2},{7,3},{8,12},{9,13},{10,... | collective-permute-start | bytes 221192 | tf_op jit(solution)/shard_map/ppermute | solution.py:19
  49.1 5.6 %collective-permute-start.15 = (bf16[96,384]{1,0:T(8,128)(2,1)S(1)}, bf16[96,384]{1,0:T(8,128)(2,1)S(1)}, u32[]{:S(2)}, u32[]{:S(2)}) collective-permute-start(bf16[96,384]{1,0:T(8,128)(2,1)S(1)} %get-tuple-element.69), channel_id=1, source_target_pairs={{0,3},{1,2},{2,1},{3,0},{4,7},{5,6},{6,5},{7,4},{8,11},{9,10},{10,... | collective-permute-start | bytes 221192 | tf_op jit(solution)/shard_map/ppermute | solution.py:19
  49.8 8.3 %collective-permute-start.16 = (bf16[96,384]{1,0:T(8,128)(2,1)S(1)}, bf16[96,384]{1,0:T(8,128)(2,1)S(1)}, u32[]{:S(2)}, u32[]{:S(2)}) collective-permute-start(bf16[96,384]{1,0:T(8,128)(2,1)S(1)} %get-tuple-element.69), channel_id=1, source_target_pairs={{0,1},{1,0},{2,3},{3,2},{4,5},{5,4},{6,7},{7,6},{8,9},{9,8},{10,11... | collective-permute-start | bytes 221192 | tf_op jit(solution)/shard_map/ppermute | solution.py:19
  50.7 7.4 %collective-permute-start.17 = (bf16[96,384]{1,0:T(8,128)(2,1)S(1)}, bf16[96,384]{1,0:T(8,128)(2,1)S(1)}, u32[]{:S(2)}, u32[]{:S(2)}) collective-permute-start(bf16[96,384]{1,0:T(8,128)(2,1)S(1)} %get-tuple-element.69), channel_id=1, source_target_pairs={{0,2},{1,3},{2,0},{3,1},{4,6},{5,7},{6,4},{7,5},{8,10},{9,11},{10,... | collective-permute-start | bytes 221192 | tf_op jit(solution)/shard_map/ppermute | solution.py:19
  54.6 6.8 %collective-permute-start.22 = (bf16[96,384]{1,0:T(8,128)(2,1)S(1)}, bf16[96,384]{1,0:T(8,128)(2,1)S(1)}, u32[]{:S(2)}, u32[]{:S(2)}) collective-permute-start(bf16[96,384]{1,0:T(8,128)(2,1)S(1)} %fusion.3), channel_id=1, source_target_pairs={{0,3},{1,2},{2,1},{3,0},{4,7},{5,6},{6,5},{7,4},{8,11},{9,10},{10,... | collective-permute-start | bytes 221192 | tf_op jit(solution)/shard_map/ppermute | solution.py:19
  55.9 5.6 %collective-permute-start.23 = (bf16[96,384]{1,0:T(8,128)(2,1)S(1)}, bf16[96,384]{1,0:T(8,128)(2,1)S(1)}, u32[]{:S(2)}, u32[]{:S(2)}) collective-permute-start(bf16[96,384]{1,0:T(8,128)(2,1)S(1)} %fusion.3), channel_id=1, source_target_pairs={{0,1},{1,0},{2,3},{3,2},{4,5},{5,4},{6,7},{7,6},{8,9},{9,8},{10,11... | collective-permute-start | bytes 221192 | tf_op jit(solution)/shard_map/ppermute | solution.py:19
  56.8 4.8 %collective-permute-start.24 = (bf16[96,384]{1,0:T(8,128)(2,1)S(1)}, bf16[96,384]{1,0:T(8,128)(2,1)S(1)}, u32[]{:S(2)}, u32[]{:S(2)}) collective-permute-start(bf16[96,384]{1,0:T(8,128)(2,1)S(1)} %fusion.3), channel_id=1, source_target_pairs={{0,2},{1,3},{2,0},{3,1},{4,6},{5,7},{6,4},{7,5},{8,10},{9,11},{10,... | collective-permute-start | bytes 221192 | tf_op jit(solution)/shard_map/ppermute | solution.py:19
  59.8 6.8 %collective-permute-start.25 = (bf16[384,384]{1,0:T(8,128)(2,1)S(1)}, bf16[384,384]{1,0:T(8,128)(2,1)S(1)}, u32[]{:S(2)}, u32[]{:S(2)}) collective-permute-start(bf16[384,384]{1,0:T(8,128)(2,1)S(1)} %get-tuple-element.61), channel_id=1, source_target_pairs={{0,16},{8,24},{16,0},{24,8},{1,17},{9,25},{17,1},{25,9},{2,18},{10... | collective-permute-start | bytes 884744 | tf_op jit(solution)/shard_map/ppermute | solution.py:19
  66.7 5.9 %collective-permute-start.30 = (bf16[96,384]{1,0:T(8,128)(2,1)S(1)}, bf16[96,384]{1,0:T(8,128)(2,1)S(1)}, u32[]{:S(2)}, u32[]{:S(2)}) collective-permute-start(bf16[96,384]{1,0:T(8,128)(2,1)S(1)} %get-tuple-element.72), channel_id=1, source_target_pairs={{0,3},{1,2},{2,1},{3,0},{4,7},{5,6},{6,5},{7,4},{8,11},{9,10},{10,... | collective-permute-start | bytes 221192 | tf_op jit(solution)/shard_map/ppermute | solution.py:19
  68.1 5.8 %collective-permute-start.31 = (bf16[96,384]{1,0:T(8,128)(2,1)S(1)}, bf16[96,384]{1,0:T(8,128)(2,1)S(1)}, u32[]{:S(2)}, u32[]{:S(2)}) collective-permute-start(bf16[96,384]{1,0:T(8,128)(2,1)S(1)} %get-tuple-element.74), channel_id=1, source_target_pairs={{0,1},{1,0},{2,3},{3,2},{4,5},{5,4},{6,7},{7,6},{8,9},{9,8},{10,11... | collective-permute-start | bytes 221192 | tf_op jit(solution)/shard_map/ppermute | solution.py:19
  69.0 4.9 %collective-permute-start.32 = (bf16[96,384]{1,0:T(8,128)(2,1)S(1)}, bf16[96,384]{1,0:T(8,128)(2,1)S(1)}, u32[]{:S(2)}, u32[]{:S(2)}) collective-permute-start(bf16[96,384]{1,0:T(8,128)(2,1)S(1)} %get-tuple-element.73), channel_id=1, source_target_pairs={{0,2},{1,3},{2,0},{3,1},{4,6},{5,7},{6,4},{7,5},{8,10},{9,11},{10,... | collective-permute-start | bytes 221192 | tf_op jit(solution)/shard_map/ppermute | solution.py:19
  70.3 6.5 %collective-permute-start.26 = (bf16[96,384]{1,0:T(8,128)(2,1)S(1)}, bf16[96,384]{1,0:T(8,128)(2,1)S(1)}, u32[]{:S(2)}, u32[]{:S(2)}) collective-permute-start(bf16[96,384]{1,0:T(8,128)(2,1)S(1)} %get-tuple-element.75), channel_id=1, source_target_pairs={{0,3},{1,2},{2,1},{3,0},{4,7},{5,6},{6,5},{7,4},{8,11},{9,10},{10,... | collective-permute-start | bytes 221192 | tf_op jit(solution)/shard_map/ppermute | solution.py:19
  71.7 5.1 %collective-permute-start.27 = (bf16[96,384]{1,0:T(8,128)(2,1)S(1)}, bf16[96,384]{1,0:T(8,128)(2,1)S(1)}, u32[]{:S(2)}, u32[]{:S(2)}) collective-permute-start(bf16[96,384]{1,0:T(8,128)(2,1)S(1)} %get-tuple-element.77), channel_id=1, source_target_pairs={{0,1},{1,0},{2,3},{3,2},{4,5},{5,4},{6,7},{7,6},{8,9},{9,8},{10,11... | collective-permute-start | bytes 221192 | tf_op jit(solution)/shard_map/ppermute | solution.py:19
  72.6 4.4 %collective-permute-start.28 = (bf16[96,384]{1,0:T(8,128)(2,1)S(1)}, bf16[96,384]{1,0:T(8,128)(2,1)S(1)}, u32[]{:S(2)}, u32[]{:S(2)}) collective-permute-start(bf16[96,384]{1,0:T(8,128)(2,1)S(1)} %get-tuple-element.76), channel_id=1, source_target_pairs={{0,2},{1,3},{2,0},{3,1},{4,6},{5,7},{6,4},{7,5},{8,10},{9,11},{10,... | collective-permute-start | bytes 221192 | tf_op jit(solution)/shard_map/ppermute | solution.py:19
  74.0 6.3 %collective-permute-start.33 = (bf16[48,384]{1,0:T(8,128)(2,1)S(1)}, bf16[48,384]{1,0:T(8,128)(2,1)S(1)}, u32[]{:S(2)}, u32[]{:S(2)}) collective-permute-start(bf16[48,384]{1,0:T(8,128)(2,1)S(1)} %constant_dynamic-slice_fusion), channel_id=1, source_target_pairs={{0,4},{1,5},{2,6},{3,7},{4,0},{5,1},{6,2},{7,3},{8,12},{9,13},{10,... | collective-permute-start | bytes 110600 | tf_op jit(solution)/shard_map/ppermute | solution.py:19
  77.0 5.2 %collective-permute-start.29 = (bf16[48,384]{1,0:T(8,128)(2,1)S(1)}, bf16[48,384]{1,0:T(8,128)(2,1)S(1)}, u32[]{:S(2)}, u32[]{:S(2)}) collective-permute-start(bf16[48,384]{1,0:T(8,128)(2,1)S(1)} %constant_dynamic-slice_fusion.4), channel_id=1, source_target_pairs={{0,4},{1,5},{2,6},{3,7},{4,0},{5,1},{6,2},{7,3},{8,12},{9,13},{10,... | collective-permute-start | bytes 110600 | tf_op jit(solution)/shard_map/ppermute | solution.py:19
  (8 other events, 26.4 us)
